TPU v7x, 32 devices: a whole 2x2x4 slice. The times are simulated.
32 devices in a mesh: fsdp: 4 (over x, core), ctx: 2 (over y), tp: 4 (over z).
Axes of the slice: x: 2, y: 2, z: 4, core: 2. Of those that a mesh axis runs over, the one named last changes fastest.
Arguments:
- inputs: bfloat16 [8, 1536, 1536], P('fsdp', 'ctx'), may hold values from -6 to 6
- cotangent: bfloat16 [8, 1536, 1536], P('fsdp', 'ctx'), may hold values from -6 to 6
- positions: int32 [8, 1536], P('fsdp', 'ctx'), may hold values from 0 to 3070, as said below
- attn_gain: bfloat16 [1536], P('fsdp'), may hold values from 0.5 to 1.5
- query_weight: bfloat16 [1536, 1536], P('fsdp', 'tp'), may hold values from -0.15625 to 0.15625
- query_bias: bfloat16 [12, 128], P('tp', 'fsdp'), may hold values from -3 to 3
- key_weight: bfloat16 [1536, 256], P('fsdp'), may hold values from -0.15625 to 0.15625
- key_bias: bfloat16 [2, 128], P(None, 'fsdp'), may hold values from -3 to 3
- value_weight: bfloat16 [1536, 256], P('fsdp'), may hold values from -0.15625 to 0.15625
- value_bias: bfloat16 [2, 128], P(None, 'fsdp'), may hold values from -3 to 3
- output_weight: bfloat16 [1536, 1536], P('tp', 'fsdp'), may hold values from -0.3125 to 0.3125
- mlp_gain: bfloat16 [1536], P('fsdp'), may hold values from 0.5 to 1.5
- gate_weight: bfloat16 [1536, 8960], P('fsdp', 'tp'), may hold values from -0.15625 to 0.15625
- up_weight: bfloat16 [1536, 8960], P('fsdp', 'tp'), may hold values from -0.15625 to 0.15625
- down_weight: bfloat16 [8960, 1536], P('tp', 'fsdp'), may hold values from -0.0625 to 0.0625
Outputs:
- outputs: bfloat16 [8, 1536, 1536], P('fsdp', 'ctx')
- input_grad: float32 [8, 1536, 1536], P('fsdp', 'ctx')
- attn_gain_grad: float32 [1536], P('fsdp')
- query_weight_grad: float32 [1536, 1536], P('fsdp', 'tp')
- query_bias_grad: float32 [12, 128], P('tp', 'fsdp')
- key_weight_grad: float32 [1536, 256], P('fsdp')
- key_bias_grad: float32 [2, 128], P(None, 'fsdp')
- value_weight_grad: float32 [1536, 256], P('fsdp')
- value_bias_grad: float32 [2, 128], P(None, 'fsdp')
- output_weight_grad: float32 [1536, 1536], P('tp', 'fsdp')
- mlp_gain_grad: float32 [1536], P('fsdp')
- gate_weight_grad: float32 [1536, 8960], P('fsdp', 'tp')
- up_weight_grad: float32 [1536, 8960], P('fsdp', 'tp')
- down_weight_grad: float32 [8960, 1536], P('tp', 'fsdp')
Inputs may be any that keep to these rules, and one draw needn't show every extreme that they name: `positions`: each row starts at 0 and rises by 1 or 2 from one token to the next.
All inputs are finite; a program needn't handle non-finite values.
Results may differ from a plain program's by a relative error of at most 0.025.
Values may be sent and summed in bfloat16 or wider, within the bound.
No kernel may reach another device: no remote copies, remote signals or barrier semaphores. Data moves between devices by JAX's collectives and lax.ppermute only.
A program may use at most 320 MiB of HBM per device.

v0:
```python
import math

import jax
import jax.numpy as jnp
from jax import lax
from jax.sharding import PartitionSpec as P

EPS = 1e-06
THETA = 1000000.0


def rope_tables(position, width):
    half = width // 2
    freqs = jnp.exp(jnp.arange(half, dtype=jnp.float32) * (-2.0 * math.log(THETA) / width))
    angle = position.astype(jnp.float32)[..., None] * freqs
    angle = jnp.concatenate([angle, angle], axis=-1)
    return (jnp.cos(angle), jnp.sin(angle))


def rotate(values):
    half = values.shape[-1] // 2
    return jnp.concatenate([-values[..., half:], values[..., :half]], axis=-1)


def rope_apply(values, cosine, sine):
    return values * cosine + rotate(values) * sine


def rope_back(grads, cosine, sine):
    return grads * cosine - rotate(grads * sine)


def inner_rows(left, right):
    return lax.dot_general(
        left, right, (((0,), (0,)), ((), ())), preferred_element_type=jnp.float32
    )


def inner_cols(left, right):
    return lax.dot_general(
        left, right, (((1,), (1,)), ((), ())), preferred_element_type=jnp.float32
    )


def masked_scores(queries, keys, query_pos, key_pos):
    scale = 1.0 / math.sqrt(queries.shape[-1])
    logits = jnp.einsum("ihd,jd->hij", queries, keys, preferred_element_type=jnp.float32) * scale
    visible = key_pos[None, :] <= query_pos[:, None]
    return jnp.where(visible[None], logits, -1e30)


def attend(packed):
    queries, keys, values, query_pos, key_pos = packed
    logits = masked_scores(queries, keys, query_pos, key_pos)
    peak = jnp.max(logits, axis=-1, keepdims=True)
    log_total = peak + jnp.log(jnp.sum(jnp.exp(logits - peak), axis=-1, keepdims=True))
    weights = jnp.exp(logits - log_total).astype(jnp.bfloat16)
    mixed = jnp.einsum("hij,jd->ihd", weights, values, preferred_element_type=jnp.float32)
    return (mixed, log_total)


def attend_back(packed):
    queries, keys, values, query_pos, key_pos, log_total, out_grad = packed
    scale = 1.0 / math.sqrt(queries.shape[-1])
    logits = masked_scores(queries, keys, query_pos, key_pos)
    probs = jnp.exp(logits - log_total)
    prob_low = probs.astype(jnp.bfloat16)
    prob_grad = jnp.einsum("ihd,jd->hij", out_grad, values, preferred_element_type=jnp.float32)
    value_grad = jnp.einsum("hij,ihd->jd", prob_low, out_grad, preferred_element_type=jnp.float32)
    center = jnp.sum(probs * prob_grad, axis=-1, keepdims=True)
    logit_grad = (probs * (prob_grad - center)).astype(jnp.bfloat16)
    query_grad = (
        jnp.einsum("hij,jd->ihd", logit_grad, keys, preferred_element_type=jnp.float32) * scale
    )
    key_grad = (
        jnp.einsum("hij,ihd->jd", logit_grad, queries, preferred_element_type=jnp.float32) * scale
    )
    return (query_grad, key_grad, value_grad)


def local(
    inputs,
    cotangent,
    positions,
    attn_gain,
    query_weight,
    query_bias,
    key_weight,
    key_bias,
    value_weight,
    value_bias,
    output_weight,
    mlp_gain,
    gate_weight,
    up_weight,
    down_weight,
):
    seq_count, block_len, width = inputs.shape
    tp_index = lax.axis_index("tp")
    ctx_index = lax.axis_index("ctx")
    tp_count = lax.axis_size("tp")
    (
        attn_scale,
        query_full,
        qbias_full,
        key_full,
        kbias_full,
        value_full,
        vbias_full,
        output_full,
        mlp_scale,
        gate_full,
        up_full,
        down_full,
    ) = (
        lax.all_gather(attn_gain, "fsdp", axis=0, tiled=True),
        lax.all_gather(query_weight, "fsdp", axis=0, tiled=True),
        lax.all_gather(query_bias, "fsdp", axis=1, tiled=True),
        lax.all_gather(key_weight, "fsdp", axis=0, tiled=True),
        lax.all_gather(key_bias, "fsdp", axis=1, tiled=True),
        lax.all_gather(value_weight, "fsdp", axis=0, tiled=True),
        lax.all_gather(value_bias, "fsdp", axis=1, tiled=True),
        lax.all_gather(output_weight, "fsdp", axis=1, tiled=True),
        lax.all_gather(mlp_gain, "fsdp", axis=0, tiled=True),
        lax.all_gather(gate_weight, "fsdp", axis=0, tiled=True),
        lax.all_gather(up_weight, "fsdp", axis=0, tiled=True),
        lax.all_gather(down_weight, "fsdp", axis=1, tiled=True),
    )
    local_heads, head_dim = qbias_full.shape
    kv_heads = kbias_full.shape[0]
    kv_index = tp_index // (tp_count // kv_heads)
    tokens = seq_count * block_len
    flat_in = inputs.reshape(tokens, width).astype(jnp.float32)
    attn_gamma = attn_scale.astype(jnp.float32)
    first_root = lax.rsqrt(jnp.mean(flat_in * flat_in, axis=-1, keepdims=True) + EPS)
    normed_one = (flat_in * first_root * attn_gamma).astype(jnp.bfloat16)
    query_lin = jnp.dot(normed_one, query_full, preferred_element_type=jnp.float32)
    query_lin = query_lin + qbias_full.reshape(-1).astype(jnp.float32)
    key_cols = lax.dynamic_slice_in_dim(key_full, kv_index * head_dim, head_dim, 1)
    value_cols = lax.dynamic_slice_in_dim(value_full, kv_index * head_dim, head_dim, 1)
    key_shift = (
        lax.dynamic_slice_in_dim(kbias_full, kv_index, 1, 0).reshape(head_dim).astype(jnp.float32)
    )
    value_shift = (
        lax.dynamic_slice_in_dim(vbias_full, kv_index, 1, 0).reshape(head_dim).astype(jnp.float32)
    )
    key_lin = jnp.dot(normed_one, key_cols, preferred_element_type=jnp.float32) + key_shift
    value_rows = jnp.dot(normed_one, value_cols, preferred_element_type=jnp.float32) + value_shift
    value_rows = value_rows.astype(jnp.bfloat16).reshape(seq_count, block_len, head_dim)
    cosine, sine = rope_tables(positions, head_dim)
    query_rot = rope_apply(
        query_lin.reshape(seq_count, block_len, local_heads, head_dim),
        cosine[:, :, None],
        sine[:, :, None],
    ).astype(jnp.bfloat16)
    key_rot = rope_apply(key_lin.reshape(seq_count, block_len, head_dim), cosine, sine).astype(
        jnp.bfloat16
    )
    key_all, value_all = (
        lax.all_gather(key_rot, "ctx", axis=1, tiled=True),
        lax.all_gather(value_rows, "ctx", axis=1, tiled=True),
    )
    seq_len = key_all.shape[1]
    query_order = jnp.broadcast_to(
        ctx_index * block_len + jnp.arange(block_len, dtype=jnp.int32)[None, :],
        (seq_count, block_len),
    )
    key_order = jnp.broadcast_to(
        jnp.arange(seq_len, dtype=jnp.int32)[None, :], (seq_count, seq_len)
    )
    attended, log_total = lax.map(attend, (query_rot, key_all, value_all, query_order, key_order))
    attended_low = attended.astype(jnp.bfloat16).reshape(tokens, local_heads * head_dim)
    branch = lax.psum(jnp.dot(attended_low, output_full, preferred_element_type=jnp.float32), "tp")
    hidden_state = flat_in + branch
    mlp_gamma = mlp_scale.astype(jnp.float32)
    second_root = lax.rsqrt(jnp.mean(hidden_state * hidden_state, axis=-1, keepdims=True) + EPS)
    normed_two = (hidden_state * second_root * mlp_gamma).astype(jnp.bfloat16)
    gate = jnp.dot(normed_two, gate_full, preferred_element_type=jnp.float32)
    up_part = jnp.dot(normed_two, up_full, preferred_element_type=jnp.float32)
    act = (jax.nn.silu(gate) * up_part).astype(jnp.bfloat16)
    mixed = lax.psum(
        jnp.dot(act, down_full, preferred_element_type=jnp.float32).astype(jnp.bfloat16), "tp"
    ).astype(jnp.float32)
    outputs = (hidden_state + mixed).astype(jnp.bfloat16)
    cot_low = cotangent.reshape(tokens, width)
    cot_full = cot_low.astype(jnp.float32)
    down_term = inner_rows(act, cot_low)
    act_grad = inner_cols(cot_low, down_full)
    sigma = jax.nn.sigmoid(gate)
    gate_grad = (act_grad * up_part * (sigma * (1.0 + gate * (1.0 - sigma)))).astype(jnp.bfloat16)
    up_grad = (act_grad * (gate * sigma)).astype(jnp.bfloat16)
    gate_term = inner_rows(normed_two, gate_grad)
    up_term = inner_rows(normed_two, up_grad)
    two_part = inner_cols(gate_grad, gate_full) + inner_cols(up_grad, up_full)
    two_grad = lax.psum(two_part, "tp")
    mlp_gain_term = jnp.sum(two_grad * hidden_state * second_root, axis=0)
    scaled_two = mlp_gamma * two_grad
    hidden_grad = (
        cot_full
        + second_root * scaled_two
        - hidden_state
        * second_root**3
        * jnp.mean(scaled_two * hidden_state, axis=-1, keepdims=True)
    )
    branch_grad = hidden_grad.astype(jnp.bfloat16)
    output_term = inner_rows(attended_low, branch_grad)
    attended_grad = inner_cols(branch_grad, output_full).astype(jnp.bfloat16)
    attended_grad = attended_grad.reshape(seq_count, block_len, local_heads, head_dim)
    query_rot_grad, key_rot_grad, value_rot_grad = lax.map(
        attend_back,
        (query_rot, key_all, value_all, query_order, key_order, log_total, attended_grad),
    )
    query_lin_grad = rope_back(query_rot_grad, cosine[:, :, None], sine[:, :, None]).astype(
        jnp.bfloat16
    )
    query_lin_grad = query_lin_grad.reshape(tokens, local_heads * head_dim)
    qbias_term = jnp.sum(query_lin_grad.astype(jnp.float32), axis=0).reshape(local_heads, head_dim)
    query_term = inner_rows(normed_one, query_lin_grad)
    one_part = inner_cols(query_lin_grad, query_full)
    key_spread = jnp.concatenate(
        [key_rot_grad * (kv_index == slot).astype(jnp.float32) for slot in range(kv_heads)], axis=-1
    )
    value_spread = jnp.concatenate(
        [value_rot_grad * (kv_index == slot).astype(jnp.float32) for slot in range(kv_heads)],
        axis=-1,
    )
    key_piece, value_piece = (
        lax.psum_scatter(key_spread, ("ctx", "tp"), scatter_dimension=1, tiled=True),
        lax.psum_scatter(value_spread, ("ctx", "tp"), scatter_dimension=1, tiled=True),
    )
    piece_len = key_piece.shape[1]
    piece_pos = lax.dynamic_slice_in_dim(positions, tp_index * piece_len, piece_len, 1)
    piece_cos, piece_sin = rope_tables(piece_pos, head_dim)
    key_piece = rope_back(
        key_piece.reshape(seq_count, piece_len, kv_heads, head_dim),
        piece_cos[:, :, None],
        piece_sin[:, :, None],
    )
    key_piece = key_piece.astype(jnp.bfloat16).reshape(seq_count, piece_len, kv_heads * head_dim)
    value_piece = value_piece.astype(jnp.bfloat16)
    key_lin_grad, value_lin_grad = (
        lax.all_gather(key_piece, "tp", axis=1, tiled=True),
        lax.all_gather(value_piece, "tp", axis=1, tiled=True),
    )
    key_lin_grad = key_lin_grad.reshape(tokens, kv_heads * head_dim)
    value_lin_grad = value_lin_grad.reshape(tokens, kv_heads * head_dim)
    key_term = inner_rows(normed_one, key_lin_grad)
    value_term = inner_rows(normed_one, value_lin_grad)
    kbias_term = jnp.sum(key_lin_grad.astype(jnp.float32), axis=0).reshape(kv_heads, head_dim)
    vbias_term = jnp.sum(value_lin_grad.astype(jnp.float32), axis=0).reshape(kv_heads, head_dim)
    one_grad = lax.psum(one_part.astype(jnp.bfloat16), "tp").astype(jnp.float32)
    one_grad = (
        one_grad + inner_cols(key_lin_grad, key_full) + inner_cols(value_lin_grad, value_full)
    )
    attn_gain_term = jnp.sum(one_grad * flat_in * first_root, axis=0)
    scaled_one = attn_gamma * one_grad
    input_grad = (
        hidden_grad
        + first_root * scaled_one
        - flat_in * first_root**3 * jnp.mean(scaled_one * flat_in, axis=-1, keepdims=True)
    )
    all_parts = (
        lax.psum_scatter(
            attn_gain_term.astype(jnp.bfloat16), ("fsdp", "ctx"), scatter_dimension=0, tiled=True
        ).astype(jnp.float32),
        lax.psum_scatter(
            query_term.astype(jnp.bfloat16), ("fsdp", "ctx"), scatter_dimension=0, tiled=True
        ).astype(jnp.float32),
        lax.psum_scatter(
            qbias_term.astype(jnp.bfloat16), ("fsdp", "ctx"), scatter_dimension=1, tiled=True
        ).astype(jnp.float32),
        lax.psum_scatter(
            key_term.astype(jnp.bfloat16), ("fsdp", "ctx"), scatter_dimension=0, tiled=True
        ).astype(jnp.float32),
        lax.psum_scatter(
            kbias_term.astype(jnp.bfloat16), ("fsdp", "ctx"), scatter_dimension=1, tiled=True
        ).astype(jnp.float32),
        lax.psum_scatter(
            value_term.astype(jnp.bfloat16), ("fsdp", "ctx"), scatter_dimension=0, tiled=True
        ).astype(jnp.float32),
        lax.psum_scatter(
            vbias_term.astype(jnp.bfloat16), ("fsdp", "ctx"), scatter_dimension=1, tiled=True
        ).astype(jnp.float32),
        lax.psum_scatter(
            output_term.astype(jnp.bfloat16), ("fsdp", "ctx"), scatter_dimension=1, tiled=True
        ).astype(jnp.float32),
        lax.psum_scatter(
            mlp_gain_term.astype(jnp.bfloat16), ("fsdp", "ctx"), scatter_dimension=0, tiled=True
        ).astype(jnp.float32),
        lax.psum_scatter(
            gate_term.astype(jnp.bfloat16), ("fsdp", "ctx"), scatter_dimension=0, tiled=True
        ).astype(jnp.float32),
        lax.psum_scatter(
            up_term.astype(jnp.bfloat16), ("fsdp", "ctx"), scatter_dimension=0, tiled=True
        ).astype(jnp.float32),
        lax.psum_scatter(
            down_term.astype(jnp.bfloat16), ("fsdp", "ctx"), scatter_dimension=1, tiled=True
        ).astype(jnp.float32),
    )
    (
        attn_gain_grad,
        query_weight_grad,
        query_bias_grad,
        key_weight_grad,
        key_bias_grad,
        value_weight_grad,
        value_bias_grad,
        output_weight_grad,
        mlp_gain_grad,
        gate_weight_grad,
        up_weight_grad,
        down_weight_grad,
    ) = (
        lax.all_gather(all_parts[0].astype(jnp.bfloat16), "ctx", axis=0, tiled=True).astype(
            jnp.float32
        ),
        lax.all_gather(all_parts[1].astype(jnp.bfloat16), "ctx", axis=0, tiled=True).astype(
            jnp.float32
        ),
        lax.all_gather(all_parts[2].astype(jnp.bfloat16), "ctx", axis=1, tiled=True).astype(
            jnp.float32
        ),
        lax.all_gather(all_parts[3].astype(jnp.bfloat16), "ctx", axis=0, tiled=True).astype(
            jnp.float32
        ),
        lax.all_gather(all_parts[4].astype(jnp.bfloat16), "ctx", axis=1, tiled=True).astype(
            jnp.float32
        ),
        lax.all_gather(all_parts[5].astype(jnp.bfloat16), "ctx", axis=0, tiled=True).astype(
            jnp.float32
        ),
        lax.all_gather(all_parts[6].astype(jnp.bfloat16), "ctx", axis=1, tiled=True).astype(
            jnp.float32
        ),
        lax.all_gather(all_parts[7].astype(jnp.bfloat16), "ctx", axis=1, tiled=True).astype(
            jnp.float32
        ),
        lax.all_gather(all_parts[8].astype(jnp.bfloat16), "ctx", axis=0, tiled=True).astype(
            jnp.float32
        ),
        lax.all_gather(all_parts[9].astype(jnp.bfloat16), "ctx", axis=0, tiled=True).astype(
            jnp.float32
        ),
        lax.all_gather(all_parts[10].astype(jnp.bfloat16), "ctx", axis=0, tiled=True).astype(
            jnp.float32
        ),
        lax.all_gather(all_parts[11].astype(jnp.bfloat16), "ctx", axis=1, tiled=True).astype(
            jnp.float32
        ),
    )
    return (
        outputs.reshape(seq_count, block_len, width),
        input_grad.reshape(seq_count, block_len, width),
        attn_gain_grad,
        query_weight_grad,
        query_bias_grad,
        key_weight_grad,
        key_bias_grad,
        value_weight_grad,
        value_bias_grad,
        output_weight_grad,
        mlp_gain_grad,
        gate_weight_grad,
        up_weight_grad,
        down_weight_grad,
    )


def solution(mesh):
    in_specs = (
        P("fsdp", "ctx", None),
        P("fsdp", "ctx", None),
        P("fsdp", "ctx"),
        P("fsdp"),
        P("fsdp", "tp"),
        P("tp", "fsdp"),
        P("fsdp", None),
        P(None, "fsdp"),
        P("fsdp", None),
        P(None, "fsdp"),
        P("tp", "fsdp"),
        P("fsdp"),
        P("fsdp", "tp"),
        P("fsdp", "tp"),
        P("tp", "fsdp"),
    )
    out_specs = (
        P("fsdp", "ctx", None),
        P("fsdp", "ctx", None),
        P("fsdp"),
        P("fsdp", "tp"),
        P("tp", "fsdp"),
        P("fsdp", None),
        P(None, "fsdp"),
        P("fsdp", None),
        P(None, "fsdp"),
        P("tp", "fsdp"),
        P("fsdp"),
        P("fsdp", "tp"),
        P("fsdp", "tp"),
        P("tp", "fsdp"),
    )
    return jax.shard_map(local, mesh=mesh, in_specs=in_specs, out_specs=out_specs, check_vma=False)
```

profile of v0, /device:TPU:0, one launch (start us, length us, event | category | flops | bytes accessed | tf_op | source)
XLA Modules:
  0.0 2144.2 jit_solution(4010389649741347711)
XLA Ops:
  114.6 48.3 %while.26 = (s32[]{:T(128)}, bf16[2,768,3,128]{1,3,2,0:T(8,128)(2,1)}, f32[2,3,768,1]{2,1,3,0:T(4,128)S(1)}, bf16[2,1536,128]{2,1,0:T(8,128)(2,1)}, s32[2,1536]{...) while((s32[]{:T(128)}, ...), condition=%wide.region_4.5_spmd, body=%wide.region_1.4_spmd.sunk | while | flops 1852045056 | bytes 62443716 | solution.py:171
  180.3 319.0 %all-reduce.11.cloned.1.call-done = f32[1536,1536]{1,0:T(8,128)} async-done(((f32[1536,1536]{1,0:T(8,128)}), f32[1536,1536]{1,0:T(8,128)}) %all-reduce.11.cloned.1.call-update) | async-done | bytes 9437200 | tf_op jit(solution)/shard_map/psum | solution.py:173
  518.3 31.1 %all-gather.21.cloned.1.call-done = bf16[1536,2240]{0,1:T(8,128)(2,1)} async-done(((bf16[384,2240]{0,1:T(8,128)(2,1)}), bf16[1536,2240]{0,1:T(8,128)(2,1)}) %all-gather.21.cloned.1.call-update) | async-done | bytes 6881296 | tf_op jit(solution)/shard_map/all_gather | solution.py:125
  566.5 33.9 %all-gather.23.cloned.1.call-done = bf16[1536,2240]{0,1:T(8,128)(2,1)} async-done(((bf16[384,2240]{0,1:T(8,128)(2,1)}), bf16[1536,2240]{0,1:T(8,128)(2,1)}) %all-gather.23.cloned.1.call-update) | async-done | bytes 6881296 | tf_op jit(solution)/shard_map/all_gather | solution.py:126
  617.6 34.0 %all-gather.25.cloned.1.call-done = bf16[2240,1536]{1,0:T(8,128)(2,1)} async-done(((bf16[2240,384]{1,0:T(8,128)(2,1)}), bf16[2240,1536]{1,0:T(8,128)(2,1)}) %all-gather.25.cloned.1.call-update) | async-done | bytes 6881296 | tf_op jit(solution)/shard_map/all_gather | solution.py:127
  651.6 28.4 %multiply_convert_fusion = (bf16[1536,2240]{0,1:T(8,128)(2,1)}, bf16[1536,2240]{0,1:T(8,128)(2,1)}, bf16[1536,2240]{0,1:T(8,128)(2,1)}) fusion(f32[1536,2240]{0,1:T(8,128)} %fusion.89, f32[1536,2240]{0,1:T(8,128)} %fusion.90, bf16[1536,1536]{1,0:T(8,128)(2,1)} %bitcast.310, bf16[2240,1536]{1,0:T(8,128)(2,1)} %all-gather.25.cloned.1.call-done), kind=kOutput, calls=%fused_computation.66 | convolution fusion | flops 10621255680 | bytes 59768832 | tf_op jit(solution)/shard_map/dot_general | solution.py:40
  711.5 17.2 convolution_convert_fusion.2
  762.9 273.3 %all-reduce.13.cloned.1.call-done = f32[1536,1536]{1,0:T(8,128)} async-done(((f32[1536,1536]{1,0:T(8,128)}), f32[1536,1536]{1,0:T(8,128)}) %all-reduce.13.cloned.1.call-update) | async-done | bytes 9437200 | tf_op jit(solution)/shard_map/psum | solution.py:195
  1065.0 140.3 %while.27 = (s32[]{:T(128)}, f32[2,768,3,128]{1,0,3,2:T(2,128)}, f32[2,1536,128]{2,1,0:T(8,128)}, f32[2,1536,128]{2,1,0:T(8,128)}, bf16[2,1536,128]{2,1,0:T(8,12...) while((s32[]{:T(128)}, f32[2,768,3,128]{1,0,3,2:T(2,128)}, ...), condition=%wide.region_12.13_spmd, body=%wide.region_10.12_spmd.sunk | while | flops 4563367936 | bytes 217136400 | solution.py:209
  1098.0 22.0 %dynamic_update_slice.31 = f32[2,768,3,128]{1,0,3,2:T(2,128)} dynamic-update-slice(f32[2,768,3,128]{1,0,3,2:T(2,128)} %get-tuple-element.505, f32[1,768,3,128]{1,0,3,2:T(1,128)S(1)} %copy.155, s32[]{:T(128)S(6)} %copy.176, s32[]{:T(128)} %constant.91.clone.1..sunk, s32[]{:T(128)} %constant.91.clone.1..sunk, s32[]{:T(128)} %constant.91.clone.1..sunk) | dynamic-update-slice | bytes 2359300 | tf_op jit(solution)/shard_map/while/body/jit(dynamic_update_index_in_dim)/dynamic_update_slice | solution.py:171
  1167.8 22.0 %dynamic_update_slice.31 = f32[2,768,3,128]{1,0,3,2:T(2,128)} dynamic-update-slice(f32[2,768,3,128]{1,0,3,2:T(2,128)} %get-tuple-element.505, f32[1,768,3,128]{1,0,3,2:T(1,128)S(1)} %copy.155, s32[]{:T(128)S(6)} %copy.176, s32[]{:T(128)} %constant.91.clone.1..sunk, s32[]{:T(128)} %constant.91.clone.1..sunk, s32[]{:T(128)} %constant.91.clone.1..sunk) | dynamic-update-slice | bytes 2359300 | tf_op jit(solution)/shard_map/while/body/jit(dynamic_update_index_in_dim)/dynamic_update_slice | solution.py:171
  1245.0 76.6 %reduce-scatter.19.cloned.1.call-done = f32[2,192,256]{2,1,0:T(8,128)} async-done(((f32[2,1536,256]{2,1,0:T(8,128)}), f32[2,192,256]{2,1,0:T(8,128)}) %reduce-scatter.19.cloned.1.call-update) | async-done | bytes 393232 | tf_op jit(solution)/shard_map/reduce_scatter | solution.py:228
  1324.5 22.9 %all_gather.98 = bf16[2,768,256]{2,1,0:T(8,128)(2,1)S(1)} all-gather(bf16[2,192,256]{2,1,0:T(8,128)(2,1)S(1)} %subtract_convert_fusion), channel_id=1, replica_groups=mesh['fsdp'=4,'ctx'=2,'tp'=4] {'tp'}, dimensions={1}, use_global_device_ids=true | all-gather | bytes 983040 | tf_op jit(solution)/shard_map/all_gather | solution.py:242
  1348.4 56.8 %reduce-scatter.21.cloned.1.call-done = f32[2,192,256]{2,1,0:T(8,128)} async-done(((f32[2,1536,256]{2,1,0:T(8,128)}), f32[2,192,256]{2,1,0:T(8,128)}) %reduce-scatter.21.cloned.1.call-update) | async-done | bytes 393232 | tf_op jit(solution)/shard_map/reduce_scatter | solution.py:229
  1406.2 18.0 all_gather.99
  1487.4 32.8 %reduce-scatter.29.cloned.1.call-done = bf16[384,192]{0,1:T(8,128)(2,1)} async-done(((bf16[384,1536]{0,1:T(8,128)(2,1)}), bf16[384,192]{0,1:T(8,128)(2,1)}) %reduce-scatter.29.cloned.1.call-update) | async-done | bytes 147472 | tf_op jit(solution)/shard_map/reduce_scatter | solution.py:284
  1527.5 23.5 %all-gather.27.cloned.1.call-done = bf16[384,2240]{1,0:T(8,128)(2,1)} async-done(((bf16[192,2240]{1,0:T(8,128)(2,1)}), bf16[384,2240]{1,0:T(8,128)(2,1)}) %all-gather.27.cloned.1.call-update) | async-done | bytes 1720336 | tf_op jit(solution)/shard_map/all_gather | solution.py:341
  1555.0 26.8 %all-gather.29.cloned.1.call-done = bf16[384,2240]{1,0:T(8,128)(2,1)} async-done(((bf16[192,2240]{1,0:T(8,128)(2,1)}), bf16[384,2240]{1,0:T(8,128)(2,1)}) %all-gather.29.cloned.1.call-update) | async-done | bytes 1720336 | tf_op jit(solution)/shard_map/all_gather | solution.py:344
  1585.9 26.9 %all-gather.31.cloned.1.call-done = bf16[2240,384]{0,1:T(8,128)(2,1)} async-done(((bf16[2240,192]{0,1:T(8,128)(2,1)}), bf16[2240,384]{0,1:T(8,128)(2,1)}) %all-gather.31.cloned.1.call-update) | async-done | bytes 1720336 | tf_op jit(solution)/shard_map/all_gather | solution.py:347
  1616.7 30.8 %reduce-scatter.39.cloned.1.call-done = bf16[16,2]{1,0:T(8,128)(2,1)} async-done(((bf16[128,2]{1,0:T(8,128)(2,1)}), bf16[16,2]{1,0:T(8,128)(2,1)}) %reduce-scatter.39.cloned.1.call-update) | async-done | bytes 80
  1652.5 29.5 %reduce-scatter.41.cloned.1.call-done = bf16[16,2]{1,0:T(8,128)(2,1)} async-done(((bf16[128,2]{1,0:T(8,128)(2,1)}), bf16[16,2]{1,0:T(8,128)(2,1)}) %reduce-scatter.41.cloned.1.call-update) | async-done | bytes 80
  1688.3 31.9 %reduce-scatter.25.cloned.1.call-done = bf16[192,256]{1,0:T(8,128)(2,1)} async-done(((bf16[1536,256]{1,0:T(8,128)(2,1)}), bf16[192,256]{1,0:T(8,128)(2,1)}) %reduce-scatter.25.cloned.1.call-update) | async-done | bytes 98320 | tf_op jit(solution)/shard_map/reduce_scatter | solution.py:272
  1726.4 31.9 %reduce-scatter.27.cloned.1.call-done = bf16[192,256]{1,0:T(8,128)(2,1)} async-done(((bf16[1536,256]{1,0:T(8,128)(2,1)}), bf16[192,256]{1,0:T(8,128)(2,1)}) %reduce-scatter.27.cloned.1.call-update) | async-done | bytes 98320 | tf_op jit(solution)/shard_map/reduce_scatter | solution.py:278
  1764.6 322.3 %all-reduce.15.cloned.1.call-done = (bf16[1536,1536]{1,0:T(8,128)(2,1)}, bf16[1536,1536]{1,0:T(8,128)(2,1)}) async-done(((bf16[1536,1536]{1,0:T(8,128)(2,1)}, bf16[1536,1536]{1,0:T(8,128)(2,1)}), (bf16[1536,1536]{1,0:T(8,128)(2,1)}, bf16[1536,1536]{1,0:T(8,128)(2,1)})) %all-reduce.15.cloned.1.call-update) | async-done | bytes 9437200 | tf_op jit(solution)/shard_map/psum | solution.py:181
  (362 shorter events, 614.7 us)
Async XLA Ops:
  7.2 90.0 %all-gather.17.cloned.1.call-start = ((), (), s32[]{:S(2)}) async-start(), calls=%async_computation.12 | async-start | bytes 1474560 | tf_op jit(solution)/shard_map/all_gather | solution.py:117
  7.9 158.4 %all-gather.19.cloned.1.call-start = ((), (), s32[]{:S(2)}) async-start(), calls=%async_computation.13 | async-start | bytes 1474560 | tf_op jit(solution)/shard_map/all_gather | solution.py:123
  8.7 490.6 %all-reduce.11.cloned.1.call-start = ((), (), s32[]{:S(2)}) async-start(), calls=%async_computation.14 | async-start | bytes 18874368 | tf_op jit(solution)/shard_map/psum | solution.py:173
  173.3 376.1 %all-gather.21.cloned.1.call-start = ((), (), s32[]{:S(2)}) async-start(), calls=%async_computation.15 | async-start | bytes 8601600 | tf_op jit(solution)/shard_map/all_gather | solution.py:125
  173.9 426.6 %all-gather.23.cloned.1.call-start = ((), (), s32[]{:S(2)}) async-start(), calls=%async_computation.16 | async-start | bytes 8601600 | tf_op jit(solution)/shard_map/all_gather | solution.py:126
  174.4 477.1 %all-gather.25.cloned.1.call-start = ((), (), s32[]{:S(2)}) async-start(), calls=%async_computation.17 | async-start | bytes 8601600 | tf_op jit(solution)/shard_map/all_gather | solution.py:127
  175.0 861.3 %all-reduce.13.cloned.1.call-start = ((), (), s32[]{:S(2)}) async-start(), calls=%async_computation.18 | async-start | bytes 18874368 | tf_op jit(solution)/shard_map/psum | solution.py:195
  180.3 330.7 %copy-start.35 = (f32[1536]{0:T(1024)}, f32[1536]{0:T(1024)S(1)}, u32[]{:S(2)}) copy-start(f32[1536]{0:T(1024)S(1)} %reshape.350) | copy-start | bytes 18436
  711.5 525.2 %reduce-scatter.31.cloned.1.call-start = ((), (), s32[]{:S(2)}) async-start(), calls=%async_computation.25 | async-start | bytes 7962624 | tf_op jit(solution)/shard_map/reduce_scatter | solution.py:290
  728.8 508.5 %reduce-scatter.33.cloned.1.call-start = ((), (), s32[]{:S(2)}) async-start(), calls=%async_computation.27 | async-start | bytes 7962624 | tf_op jit(solution)/shard_map/reduce_scatter | solution.py:293
  745.7 497.0 %reduce-scatter.35.cloned.1.call-start = ((), (), s32[]{:S(2)}) async-start(), calls=%async_computation.29 | async-start | bytes 7962624 | tf_op jit(solution)/shard_map/reduce_scatter | solution.py:296
  762.9 558.7 %reduce-scatter.19.cloned.1.call-start = ((), (), s32[]{:S(2)}) async-start(), calls=%async_computation.19 | async-start | bytes 3538944 | tf_op jit(solution)/shard_map/reduce_scatter | solution.py:228
  1209.4 195.8 %reduce-scatter.21.cloned.1.call-start = ((), (), s32[]{:S(2)}) async-start(), calls=%async_computation.20 | async-start | bytes 3538944 | tf_op jit(solution)/shard_map/reduce_scatter | solution.py:229
  1211.4 247.5 %reduce-scatter.37.cloned.1.call-start = ((), (), s32[]{:S(2)}) async-start(), calls=%async_computation.31 | async-start | bytes 36864
  1222.3 257.7 %reduce-scatter.23.cloned.1.call-start = ((), (), s32[]{:S(2)}) async-start(), calls=%async_computation.21 | async-start | bytes 1327104 | tf_op jit(solution)/shard_map/reduce_scatter | solution.py:266
  1228.6 291.5 %reduce-scatter.29.cloned.1.call-start = ((), (), s32[]{:S(2)}) async-start(), calls=%async_computation.24 | async-start | bytes 1327104 | tf_op jit(solution)/shard_map/reduce_scatter | solution.py:284
  1236.6 314.4 %all-gather.27.cloned.1.call-start = ((), (), s32[]{:S(2)}) async-start(), calls=%async_computation.26 | async-start | bytes 2654208 | tf_op jit(solution)/shard_map/all_gather | solution.py:341
  1237.2 344.7 %all-gather.29.cloned.1.call-start = ((), (), s32[]{:S(2)}) async-start(), calls=%async_computation.28 | async-start | bytes 2654208 | tf_op jit(solution)/shard_map/all_gather | solution.py:344
  1237.8 374.9 %all-gather.31.cloned.1.call-start = ((), (), s32[]{:S(2)}) async-start(), calls=%async_computation.30 | async-start | bytes 2654208 | tf_op jit(solution)/shard_map/all_gather | solution.py:347
  1242.7 404.9 %reduce-scatter.39.cloned.1.call-start = ((), (), s32[]{:S(2)}) async-start(), calls=%async_computation.32 | async-start | bytes 36864
  1348.4 333.6 %reduce-scatter.41.cloned.1.call-start = ((), (), s32[]{:S(2)}) async-start(), calls=%async_computation.33 | async-start | bytes 36864
  1425.2 295.0 %reduce-scatter.25.cloned.1.call-start = ((), (), s32[]{:S(2)}) async-start(), calls=%async_computation.22 | async-start | bytes 884736 | tf_op jit(solution)/shard_map/reduce_scatter | solution.py:272
  1429.9 328.4 %reduce-scatter.27.cloned.1.call-start = ((), (), s32[]{:S(2)}) async-start(), calls=%async_computation.23 | async-start | bytes 884736 | tf_op jit(solution)/shard_map/reduce_scatter | solution.py:278
  1434.7 652.2 %all-reduce.15.cloned.1.call-start = ((), (), s32[]{:S(2)}) async-start(), calls=%async_computation.34 | async-start | bytes 18874368 | tf_op jit(solution)/shard_map/psum | solution.py:181
  (64 other events, 1343.6 us)
Sparse Core Ops, SparseCore 0:
  9.6 20.3 all-gather.16
  31.5 17.2 all-gather.18
  173.4 325.8 all-reduce.10
  500.7 48.6 all-gather.20
  550.8 49.6 all-gather.22
  601.9 49.6 all-gather.24
  711.6 324.6 all-reduce.12
  1039.8 64.4 reduce-scatter.30
  1108.3 65.4 reduce-scatter.32
  1177.1 65.4 reduce-scatter.34
  1247.2 74.3 reduce-scatter.18
  1326.0 79.0 reduce-scatter.20
  1409.0 30.3 reduce-scatter.36
  1443.1 36.7 reduce-scatter.22
  1483.3 36.7 reduce-scatter.28
  1521.6 29.4 all-gather.26
  1552.4 29.4 all-gather.28
  1583.3 29.4 all-gather.30
  1616.3 31.2 reduce-scatter.38
  1650.7 31.2 reduce-scatter.40
  1685.1 34.9 reduce-scatter.24
  1723.3 34.9 reduce-scatter.26
  1761.5 325.3 all-reduce.14
where the time goes:
time: 2150 us; the launch traced here: 2140 us
  waiting for transfers between devices  1410 us (66%)
  matrix products  308 us (14%)
  blocking collectives  165 us (8%)
  other arithmetic  142 us (7%)
  local copies, waits for them, and re-layouts  105 us (5%)
    psum x1, waiting for transfers between devices, local(): lax.psum(jnp.dot(act, down_full, preferred_element_type=jnp.float32).asty...  322 us
    psum x1, waiting for transfers between devices, local(): lax.psum(jnp.dot(attended_low, output_full, preferred_element_type=jnp.fl...  319 us
    psum x1, waiting for transfers between devices, local(): two_grad = lax.psum(two_part, 'tp')  273 us
    reduce_scatter x1, waiting for transfers between devices, local(): lax.psum_scatter(key_spread, ('ctx', 'tp'), scatter_dimension=1, tiled=True)  76.6 us
    dot_general x7, matrix products, inner_rows(): lax.dot_general(left, right, (((0,), (0,)), ((), ())), preferred_element_...  74.7 us
    dot_general x7, matrix products, inner_cols(): lax.dot_general(left, right, (((1,), (1,)), ((), ())), preferred_element_...  73.7 us
    unnamed x26, waiting for transfers between devices  64.5 us
    reduce_scatter x1, waiting for transfers between devices, local(): lax.psum_scatter(value_spread, ('ctx', 'tp'), scatter_dimension=1, tiled=...  56.8 us
  transfers between devices with their start and end apart: 23, of which 18 were waited for; matrix products, arithmetic and copies ran while one was open for 21% of the time, Pallas kernels for 0%

commit v1 on v0

v1 whole, which is shorter than its diff:
```python
import functools
import math

import jax
import jax.numpy as jnp
from jax import lax
from jax.experimental import pallas as pl
from jax.experimental.pallas import tpu as pltpu
from jax.sharding import PartitionSpec as P

EPS = 1e-06
THETA = 1000000.0
LOG2E = 1.0 / math.log(2.0)
LOW = jnp.bfloat16
MASKED = -1e30
MIB = 1024 * 1024


def rope_tables(position, width):
    half = width // 2
    freqs = jnp.exp(jnp.arange(half, dtype=jnp.float32) * (-2.0 * math.log(THETA) / width))
    angle = position.astype(jnp.float32)[..., None] * freqs
    cosine, sine = jnp.cos(angle), jnp.sin(angle)
    return (
        jnp.concatenate([cosine, cosine], axis=-1),
        jnp.concatenate([-sine, sine], axis=-1),
    )


def dot(left, right):
    return jnp.dot(left, right, preferred_element_type=jnp.float32)


def inner_rows(left, right):
    return lax.dot_general(
        left, right, (((0,), (0,)), ((), ())), preferred_element_type=jnp.float32
    )


def inner_cols(left, right):
    return lax.dot_general(
        left, right, (((1,), (1,)), ((), ())), preferred_element_type=jnp.float32
    )


def add_low(left, right):
    return (left.astype(jnp.float32) + right.astype(jnp.float32)).astype(LOW)


def root_of(values):
    return lax.rsqrt(jnp.mean(values * values, axis=-1, keepdims=True) + EPS)


FSDP, TP, BEFORE, PLACE = 0, 1, 2, 3


def shard_at(meta, flip, size):
    return pl.multiple_of(jnp.bitwise_xor(meta[FSDP], flip) * size, size)


def tp_at(meta, hop, tps, size):
    return pl.multiple_of(lax.rem(meta[TP] + tps - hop, tps) * size, size)


def call(kernel, grid, in_specs, out_specs, out_shape, scratch=(), cost=None, name=None, vmem=48):
    return pl.pallas_call(
        kernel,
        grid_spec=pltpu.PrefetchScalarGridSpec(
            num_scalar_prefetch=1,
            grid=grid,
            in_specs=in_specs,
            out_specs=out_specs,
            scratch_shapes=list(scratch),
        ),
        out_shape=out_shape,
        compiler_params=pltpu.CompilerParams(vmem_limit_bytes=vmem * MIB),
        cost_estimate=cost,
        name=name,
    )


def whole(array):
    return pl.BlockSpec(array.shape, lambda *_: (0,) * array.ndim)


def shape(dims, kind):
    return jax.ShapeDtypeStruct(dims, kind)


def project_kernel(
    local_heads, kv_heads, head_dim, meta, x_ref, gain_ref, bias_ref, w_ref, wx_ref, wc_ref,
    cos_ref, sin_ref, n_ref, q_ref, kv_ref,
):
    rows = x_ref.shape[1]
    size = n_ref.shape[1] // 4
    height = w_ref.shape[0]
    values = x_ref[...].reshape(rows, -1).astype(jnp.float32)
    n_ref[...] = (values * root_of(values) * gain_ref[...]).astype(LOW)
    lin = bias_ref[...]
    for flip, weight in enumerate(
        (w_ref[:size, :], wc_ref[:size, :], wx_ref[:size, :], wc_ref[height : height + size, :])
    ):
        lin = lin + dot(n_ref[:, pl.ds(shard_at(meta, flip, size), size)], weight)
    cosine, sine = cos_ref[...], sin_ref[...]
    for head in range(local_heads + 2 * kv_heads):
        part = lin[:, head * head_dim : (head + 1) * head_dim]
        if head < local_heads + kv_heads:
            part = part * cosine + pltpu.roll(part, head_dim // 2, 1) * sine
        if head < local_heads:
            q_ref[0, :, head * head_dim : (head + 1) * head_dim] = part.astype(LOW)
        else:
            at = (head - local_heads) * head_dim
            kv_ref[:, at : at + head_dim] = part.astype(LOW)


def project(meta, inputs, gain, bias, weights, cosine, sine, sizes):
    seq_count, block_len, width = inputs.shape
    local_heads, kv_heads, head_dim, tps = sizes
    own = block_len // tps
    q_cols, kv_cols = local_heads * head_dim, 2 * kv_heads * head_dim

    def row(i, m):
        return (i, 0)

    def device(i, m):
        seq, place = i // tps, i % tps
        return jnp.where(seq % 2 == 0, place, tps - 1 - place), seq, 0

    tokens = seq_count * block_len
    return call(
        functools.partial(project_kernel, local_heads, kv_heads, head_dim),
        (seq_count * tps,),
        [
            pl.BlockSpec((1, own, width), lambda i, m: (i // tps, i % tps, 0)),
            whole(gain), whole(bias), *(whole(w) for w in weights),
            pl.BlockSpec((own, head_dim), row), pl.BlockSpec((own, head_dim), row),
        ],
        [
            pl.BlockSpec((own, width), row),
            pl.BlockSpec((1, own, q_cols), device),
            pl.BlockSpec((own, kv_cols), row),
        ],
        [
            shape((tokens, width), LOW),
            shape((tps, seq_count * own, q_cols), LOW),
            shape((tokens, kv_cols), LOW),
        ],
        cost=pl.CostEstimate(
            flops=2 * tokens * width * (q_cols + kv_cols), bytes_accessed=8 * tokens * width, transcendentals=0
        ),
        name="project",
    )(meta, inputs, gain, bias, *weights, cosine, sine)


def fwd_kernel(
    heads, block, parts, meta, *refs
):
    q_refs, (kb_ref, vb_ref, k_ref, v_ref, order_ref, o_ref, lse_ref, qg_ref, acc_ref, m_ref, l_ref) = (
        refs[:parts], refs[parts:]
    )
    own, cols = q_refs[0].shape[1:]
    head_dim = acc_ref.shape[0]
    scale = LOG2E / math.sqrt(head_dim)
    each = cols // head_dim
    for head in range(heads):
        qg_ref[head * own : (head + 1) * own, :] = q_refs[head // each][
            0, :, (head % each) * head_dim : (head % each + 1) * head_dim
        ]
    acc_ref[...] = jnp.zeros_like(acc_ref)
    m_ref[...] = jnp.full_like(m_ref, MASKED)
    l_ref[...] = jnp.zeros_like(l_ref)
    first = meta[PLACE + pl.program_id(0)] * own
    last = first // block

    def step(key_ref, value_ref, index, masked):
        start = pl.multiple_of(index * block, block)
        keys = key_ref[pl.ds(start, block), :]
        values = value_ref[pl.ds(start, block), :]
        logits = inner_cols(keys, qg_ref[...]) * scale
        if masked:
            key_order = (start - first) + lax.broadcasted_iota(jnp.int32, logits.shape, 0)
            logits = jnp.where(key_order <= order_ref[...], logits, MASKED)
        before = m_ref[...]
        peak = jnp.maximum(before, jnp.max(logits, axis=0, keepdims=True))
        weights = jnp.exp2(logits - peak)
        fade = jnp.exp2(before - peak)
        m_ref[...] = peak
        l_ref[...] = l_ref[...] * fade + jnp.sum(weights, axis=0, keepdims=True)
        acc_ref[...] = acc_ref[...] * fade + inner_rows(values, weights.astype(LOW))

    def early(index, carry):
        step(kb_ref, vb_ref, index, False)
        return carry

    def late(index, carry):
        step(k_ref, v_ref, index, False)
        return carry

    lax.fori_loop(0, meta[BEFORE], early, 0)
    lax.fori_loop(0, last, late, 0)
    step(k_ref, v_ref, last, True)
    total = l_ref[...]
    lse_ref[...] = (m_ref[...] + jnp.log2(total)).reshape(lse_ref.shape)
    mixed = jnp.transpose(acc_ref[...] / total)
    for head in range(heads):
        o_ref[:, head * head_dim : (head + 1) * head_dim] = mixed[
            head * own : (head + 1) * own, :
        ].astype(LOW)


def bwd_kernel(heads, block, parts, meta, *refs):
    q_refs, (
        kb_ref, vb_ref, k_ref, v_ref, order_ref, o_ref, g_ref, lse_ref, cos_ref, sin_ref,
        dq_ref, db_ref, dd_ref, qg_ref, gg_ref, acc_ref,
    ) = refs[:parts], refs[parts:]
    own, cols = q_refs[0].shape[1:]
    head_dim = acc_ref.shape[1]
    scale = 1.0 / math.sqrt(head_dim)
    each = cols // head_dim
    for head in range(heads):
        rows = slice(head * own, (head + 1) * own)
        at = slice(head * head_dim, (head + 1) * head_dim)
        qg_ref[rows, :] = q_refs[head // each][
            0, :, (head % each) * head_dim : (head % each + 1) * head_dim
        ]
        gg_ref[rows, :] = g_ref[:, at]
        acc_ref[rows, :] = g_ref[:, at].astype(jnp.float32) * o_ref[:, at].astype(jnp.float32)
    center = jnp.sum(jnp.transpose(acc_ref[...]), axis=0, keepdims=True)
    acc_ref[...] = jnp.zeros_like(acc_ref)
    lse = lse_ref[...].reshape(order_ref.shape)
    first = meta[PLACE + pl.program_id(0)] * own
    last = first // block

    def step(key_ref, value_ref, out_ref, index, masked):
        start = pl.multiple_of(index * block, block)
        keys = key_ref[pl.ds(start, block), :]
        values = value_ref[pl.ds(start, block), :]
        logits = inner_cols(keys, qg_ref[...]) * (scale * LOG2E)
        if masked:
            key_order = (start - first) + lax.broadcasted_iota(jnp.int32, logits.shape, 0)
            logits = jnp.where(key_order <= order_ref[...], logits, MASKED)
        probs = jnp.exp2(logits - lse)
        out_ref[1, 0, pl.ds(start, block), :] = dot(probs.astype(LOW), gg_ref[...]).astype(LOW)
        prob_grad = inner_cols(values, gg_ref[...])
        logit_grad = (probs * (prob_grad - center)).astype(LOW)
        out_ref[0, 0, pl.ds(start, block), :] = (dot(logit_grad, qg_ref[...]) * scale).astype(LOW)
        acc_ref[...] += inner_rows(logit_grad, keys)

    def early(index, carry):
        step(kb_ref, vb_ref, db_ref, index, False)
        return carry

    def late(index, carry):
        step(k_ref, v_ref, dd_ref, index, False)
        return carry

    def clear(ref):
        def body(index, carry):
            start = pl.multiple_of(index * block, block)
            ref[:, :, pl.ds(start, block), :] = jnp.zeros((2, 1, block, head_dim), LOW)
            return carry

        return body

    lax.fori_loop(0, meta[BEFORE], early, 0)
    lax.fori_loop(meta[BEFORE], kb_ref.shape[0] // block, clear(db_ref), 0)
    lax.fori_loop(0, last, late, 0)
    step(k_ref, v_ref, dd_ref, last, True)
    lax.fori_loop(last + 1, k_ref.shape[0] // block, clear(dd_ref), 0)
    for head in range(heads):
        grad = acc_ref[head * own : (head + 1) * own, :] * scale
        grad = grad * cos_ref[...] - pltpu.roll(grad, head_dim // 2, 1) * sin_ref[...]
        dq_ref[:, head * head_dim : (head + 1) * head_dim] = grad.astype(LOW)


def attention_specs(queries, kv_before, kv_own, sizes):
    seq_count, kv_heads, head_dim, tps = sizes
    rows = queries.shape[1] // seq_count
    parts = tps // kv_heads
    heads = queries.shape[2] * parts // head_dim
    before, block_len = kv_before.shape[0] // seq_count, kv_own.shape[0] // seq_count

    def piece(index):
        return pl.BlockSpec(
            (1, rows, queries.shape[2]),
            lambda s, g, m: (lax.rem(m[TP] + tps - (g * parts + index), tps), s, 0),
        )

    specs = [piece(index) for index in range(parts)] + [
        pl.BlockSpec((before, head_dim), lambda s, g, m: (s, g)),
        pl.BlockSpec((before, head_dim), lambda s, g, m: (s, kv_heads + g)),
        pl.BlockSpec((block_len, head_dim), lambda s, g, m: (s, g)),
        pl.BlockSpec((block_len, head_dim), lambda s, g, m: (s, kv_heads + g)),
        pl.BlockSpec((1, heads * rows), lambda s, g, m: (0, 0)),
    ]
    return specs, rows, parts, heads, before, block_len


def attend(meta, queries, kv_before, kv_own, order, block, sizes):
    seq_count, kv_heads, head_dim, tps = sizes
    specs, rows, parts, heads, before, block_len = attention_specs(queries, kv_before, kv_own, sizes)
    width, wide = kv_heads * heads * head_dim, heads * rows
    work = seq_count * rows * width * (before + block_len)
    return call(
        functools.partial(fwd_kernel, heads, block, parts),
        (seq_count, kv_heads),
        specs,
        [
            pl.BlockSpec((rows, heads * head_dim), lambda s, g, m: (s, g)),
            pl.BlockSpec((1, 1, 1, wide), lambda s, g, m: (s, g, 0, 0)),
        ],
        [shape((seq_count * rows, width), LOW), shape((seq_count, kv_heads, 1, wide), jnp.float32)],
        [
            pltpu.VMEM((wide, head_dim), LOW),
            pltpu.VMEM((head_dim, wide), jnp.float32),
            pltpu.VMEM((1, wide), jnp.float32),
            pltpu.VMEM((1, wide), jnp.float32),
        ],
        cost=pl.CostEstimate(flops=8 * work, bytes_accessed=1 << 22, transcendentals=0),
        name="attend",
    )(meta, *([queries] * parts), kv_before, kv_before, kv_own, kv_own, order)


def attend_back(meta, queries, kv_before, kv_own, order, mixed, grads, lse, cosine, sine, block, sizes):
    seq_count, kv_heads, head_dim, tps = sizes
    specs, rows, parts, heads, before, block_len = attention_specs(queries, kv_before, kv_own, sizes)
    width, wide = kv_heads * heads * head_dim, heads * rows
    work = seq_count * rows * width * (before + block_len)
    wide_spec = pl.BlockSpec((rows, heads * head_dim), lambda s, g, m: (s, g))
    table_spec = pl.BlockSpec((rows, head_dim), lambda s, g, m: (s * tps + m[PLACE + s], 0))
    return call(
        functools.partial(bwd_kernel, heads, block, parts),
        (seq_count, kv_heads),
        specs
        + [
            wide_spec,
            wide_spec,
            pl.BlockSpec((1, 1, 1, wide), lambda s, g, m: (s, g, 0, 0)),
            table_spec,
            table_spec,
        ],
        [
            wide_spec,
            pl.BlockSpec((2, 1, before, head_dim), lambda s, g, m: (0, g, s, 0)),
            pl.BlockSpec((2, 1, block_len, head_dim), lambda s, g, m: (0, g, s, 0)),
        ],
        [
            shape((seq_count * rows, width), LOW),
            shape((2, kv_heads, seq_count * before, head_dim), LOW),
            shape((2, kv_heads, seq_count * block_len, head_dim), LOW),
        ],
        [
            pltpu.VMEM((wide, head_dim), LOW),
            pltpu.VMEM((wide, head_dim), LOW),
            pltpu.VMEM((wide, head_dim), jnp.float32),
        ],
        cost=pl.CostEstimate(flops=16 * work, bytes_accessed=1 << 23, transcendentals=0),
        name="attend_back",
    )(
        meta, *([queries] * parts), kv_before, kv_before, kv_own, kv_own, order,
        mixed, grads, lse, cosine, sine,
    )


def merge_kernel(tps, meta, o_ref, x_ref, w_ref, wx_ref, wc_ref, gain_ref, h_ref, n_ref, turned_ref):
    rows, width = h_ref.shape
    size, depth = width // 4, o_ref.shape[1]
    part = depth // tps
    for hop in range(tps):
        turned_ref[:, hop * part : (hop + 1) * part] = o_ref[:, pl.ds(tp_at(meta, hop, tps, part), part)]
    turned = turned_ref[...]
    for flip, weight in enumerate((w_ref[...], wc_ref[:depth, :], wx_ref[...], wc_ref[depth:, :])):
        at = pl.ds(shard_at(meta, flip, size), size)
        h_ref[:, at] = x_ref[0, :, at].astype(jnp.float32) + dot(turned, weight)
    hidden = h_ref[...]
    n_ref[...] = (hidden * root_of(hidden) * gain_ref[...]).astype(LOW)


def merge(meta, mixed, inputs, weights, gain, tps):
    seq_count, block_len, width = inputs.shape
    own = block_len // tps
    depth = mixed.shape[1]
    row = pl.BlockSpec((own, width), lambda s, m: (s, 0))
    return call(
        functools.partial(merge_kernel, tps),
        (seq_count,),
        [
            pl.BlockSpec((own, depth), lambda s, m: (s, 0)),
            pl.BlockSpec((1, own, width), lambda s, m: (s, m[PLACE + s], 0)),
            *(whole(w) for w in weights),
            whole(gain),
        ],
        [row, row],
        [shape((seq_count * own, width), jnp.float32), shape((seq_count * own, width), LOW)],
        [pltpu.VMEM((own, depth), LOW)],
        cost=pl.CostEstimate(
            flops=2 * seq_count * own * depth * width, bytes_accessed=1 << 23, transcendentals=0
        ),
        name="merge",
    )(meta, mixed, inputs, *weights, gain)


def turn_kernel(
    tps, meta, a_ref, b_ref, h_ref, c_ref, w_ref, wx_ref, wc_ref, gain_ref,
    hg_ref, bg_ref, ag_ref, term_ref, turned_ref,
):
    rows, width = h_ref.shape
    size, depth = width // 4, ag_ref.shape[1]
    part = depth // tps
    two_grad = a_ref[...].astype(jnp.float32) + b_ref[...].astype(jnp.float32)
    hidden = h_ref[...]
    root = root_of(hidden)
    term_ref[...] = jnp.sum(two_grad * hidden * root, axis=0, keepdims=True).reshape(term_ref.shape)
    scaled = gain_ref[...] * two_grad
    grad = (
        c_ref[...].reshape(rows, width).astype(jnp.float32)
        + root * scaled
        - hidden * root**3 * jnp.mean(scaled * hidden, axis=-1, keepdims=True)
    )
    hg_ref[...] = grad
    bg_ref[...] = grad.astype(LOW)
    turned_ref[...] = jnp.zeros_like(turned_ref)
    for flip, weight in enumerate((w_ref[...], wc_ref[:depth, :], wx_ref[...], wc_ref[depth:, :])):
        turned_ref[...] += inner_cols(bg_ref[:, pl.ds(shard_at(meta, flip, size), size)], weight)
    for hop in range(tps):
        ag_ref[:, pl.ds(tp_at(meta, hop, tps, part), part)] = turned_ref[
            :, hop * part : (hop + 1) * part
        ].astype(LOW)


def turn(meta, two_own, two_got, hidden, cotangent, weights, gain, depth, tps):
    seq_count, block_len, width = cotangent.shape
    own = block_len // tps
    row = pl.BlockSpec((own, width), lambda s, m: (s, 0))
    tokens = seq_count * own
    return call(
        functools.partial(turn_kernel, tps),
        (seq_count,),
        [
            row, row, row,
            pl.BlockSpec((1, own, width), lambda s, m: (s, m[PLACE + s], 0)),
            *(whole(w) for w in weights),
            whole(gain),
        ],
        [
            row, row,
            pl.BlockSpec((own, depth), lambda s, m: (s, 0)),
            pl.BlockSpec((1, 1, width), lambda s, m: (s, 0, 0)),
        ],
        [
            shape((tokens, width), jnp.float32),
            shape((tokens, width), LOW),
            shape((tokens, depth), LOW),
            shape((seq_count, 1, width), jnp.float32),
        ],
        [pltpu.VMEM((own, depth), jnp.float32)],
        cost=pl.CostEstimate(flops=2 * tokens * depth * width, bytes_accessed=1 << 23, transcendentals=0),
        name="turn",
    )(meta, two_own, two_got, hidden, cotangent, *weights, gain)


def finish_kernel(
    kv_heads, head_dim, meta, g_ref, a_ref, b_ref, cos_ref, sin_ref, q_ref, w_ref, wx_ref, wc_ref,
    x_ref, hg_ref, gain_ref, out_ref, kv_ref, term_ref, one_ref,
):
    rows, width = hg_ref.shape
    size, height = width // 4, w_ref.shape[0]
    cosine, sine = cos_ref[...], sin_ref[...]
    for kind in range(2):
        for head in range(kv_heads):
            grad = (
                a_ref[kind, head, 0].astype(jnp.float32) + b_ref[kind, head, 0].astype(jnp.float32)
            )
            if kind == 0:
                grad = grad * cosine - pltpu.roll(grad, head_dim // 2, 1) * sine
            at = (kind * kv_heads + head) * head_dim
            kv_ref[:, at : at + head_dim] = grad.astype(LOW)
    one_ref[...] = inner_cols(g_ref[...], q_ref[...])
    skip = w_ref.shape[1] - kv_ref.shape[1]
    for flip, weight in enumerate(
        (
            w_ref[:size, skip:], wc_ref[:size, skip:], wx_ref[:size, skip:],
            wc_ref[height : height + size, skip:],
        )
    ):
        one_ref[:, pl.ds(shard_at(meta, flip, size), size)] += inner_cols(kv_ref[...], weight)
    one = one_ref[...]
    values = x_ref[...].reshape(rows, width).astype(jnp.float32)
    root = root_of(values)
    term_ref[...] = jnp.sum(one * values * root, axis=0, keepdims=True).reshape(term_ref.shape)
    scaled = gain_ref[...] * one
    out_ref[...] = (
        hg_ref[...]
        + root * scaled
        - values * root**3 * jnp.mean(scaled * values, axis=-1, keepdims=True)
    ).astype(LOW)


def finish(meta, q_grad, kv_mine, kv_got, cosine, sine, q_full, weights, inputs, hidden_grad, gain, tps):
    seq_count, block_len, width = inputs.shape
    own = block_len // tps
    kv_heads, head_dim = kv_mine.shape[1], kv_mine.shape[4]
    kv_cols = 2 * kv_heads * head_dim
    tokens = seq_count * own
    row = pl.BlockSpec((own, width), lambda s, m: (s, 0))
    kv_spec = pl.BlockSpec((2, kv_heads, 1, own, head_dim), lambda s, m: (0, 0, s, 0, 0))
    table_spec = pl.BlockSpec((own, head_dim), lambda s, m: (s * tps + m[PLACE + s], 0))
    return call(
        functools.partial(finish_kernel, kv_heads, head_dim),
        (seq_count,),
        [
            pl.BlockSpec((own, q_grad.shape[1]), lambda s, m: (s, 0)),
            kv_spec, kv_spec, table_spec, table_spec,
            whole(q_full),
            *(whole(w) for w in weights),
            pl.BlockSpec((1, own, width), lambda s, m: (s, m[PLACE + s], 0)),
            row,
            whole(gain),
        ],
        [
            row,
            pl.BlockSpec((own, kv_cols), lambda s, m: (s, 0)),
            pl.BlockSpec((1, 1, width), lambda s, m: (s, 0, 0)),
        ],
        [
            shape((tokens, width), LOW),
            shape((tokens, kv_cols), LOW),
            shape((seq_count, 1, width), jnp.float32),
        ],
        [pltpu.VMEM((own, width), jnp.float32)],
        cost=pl.CostEstimate(
            flops=2 * tokens * (q_grad.shape[1] + kv_cols) * width, bytes_accessed=1 << 23, transcendentals=0
        ),
        name="finish",
    )(meta, q_grad, kv_mine, kv_got, cosine, sine, q_full, *weights, inputs, hidden_grad, gain)


class Links:
    def __init__(self):
        self.tp, self.ctx, self.fsdp = (lax.axis_index(a) for a in ("tp", "ctx", "fsdp"))
        self.tps, self.ctxs, self.fsdps = (lax.axis_size(a) for a in ("tp", "ctx", "fsdp"))
        self.core, self.x = self.fsdp % 2, self.fsdp // 2
        assert self.fsdps == 4

    def to_core(self, value):
        return lax.ppermute(value, "fsdp", [(0, 1), (1, 0), (2, 3), (3, 2)])

    def to_x(self, value):
        return lax.ppermute(value, "fsdp", [(0, 2), (2, 0), (1, 3), (3, 1)])

    def to_y(self, value):
        return lax.ppermute(value, "ctx", [(0, 1), (1, 0)])

    def hop_tp(self, value, hop=1):
        return lax.ppermute(value, "tp", [(i, (i + hop) % self.tps) for i in range(self.tps)])

    def gather_fsdp(self, shard):
        across = self.to_x(shard)
        return shard, across, self.to_core(jnp.concatenate([shard, across], axis=0))

    def gather_tp(self, block):
        blocks = [block]
        for _ in range(1, self.tps):
            blocks.append(self.hop_tp(blocks[-1]))
        return blocks

    def scatter_tp(self, blocks):
        total = blocks[1]
        for hop in range(1, self.tps):
            got = self.hop_tp(total)
            if hop < self.tps - 1:
                total = add_low(blocks[hop + 1], got)
        return blocks[0], got

    def at(self, hop):
        return (self.tp - hop + self.tps) % self.tps

    def scatter_fsdp(self, value, axis):
        size = value.shape[axis] // 4

        def pair(core):
            return jnp.concatenate(
                [
                    lax.dynamic_slice_in_dim(value, (2 * x + core) * size, size, axis)
                    for x in range(2)
                ],
                axis,
            )

        both = add_low(pair(self.core), self.to_core(pair(1 - self.core)))
        away = lax.dynamic_slice_in_dim(both, (1 - self.x) * size, size, axis)
        keep = lax.dynamic_slice_in_dim(both, self.x * size, size, axis)
        return add_low(keep, self.to_x(away))

    def sum_ctx(self, value):
        value = lax.optimization_barrier(value.astype(LOW))
        if self.ctxs == 2:
            return value.astype(jnp.float32) + self.to_y(value).astype(jnp.float32)
        return lax.psum(value.astype(jnp.float32), "ctx")

    def reduce_weight(self, term, axis):
        part = lax.psum_scatter(
            term.astype(LOW), ("fsdp", "ctx"), scatter_dimension=axis, tiled=True
        )
        if self.ctxs == 2:
            part = lax.optimization_barrier(part)
            got = self.to_y(part)
            low = jnp.where(self.ctx == 0, part, got)
            high = jnp.where(self.ctx == 0, got, part)
            full = jnp.concatenate([low, high], axis)
        else:
            full = lax.all_gather(part, "ctx", axis=axis, tiled=True)
        return full.astype(jnp.float32)


def local(
    inputs,
    cotangent,
    positions,
    attn_gain,
    query_weight,
    query_bias,
    key_weight,
    key_bias,
    value_weight,
    value_bias,
    output_weight,
    mlp_gain,
    gate_weight,
    up_weight,
    down_weight,
):
    links = Links()
    seq_count, block_len, width = inputs.shape
    tp, tps, ctx, ctxs = links.tp, links.tps, links.ctx, links.ctxs
    fsdp, fsdps = links.fsdp, links.fsdps
    own = block_len // tps
    local_heads, kv_heads = query_bias.shape[0], key_bias.shape[0]
    head_dim = key_weight.shape[1] // kv_heads
    q_cols = local_heads * head_dim
    kv_cols = 2 * kv_heads * head_dim
    depth = q_cols * tps
    shard = width // fsdps
    tokens = seq_count * block_len
    key_block = block_len // 2 if block_len % (2 * own) == 0 else block_len
    seqs = range(seq_count)

    def place(seq, device):
        return device if seq % 2 == 0 else tps - 1 - device

    def block_rows(value, hop):
        return jnp.concatenate(
            [
                lax.dynamic_slice_in_dim(value[s], place(s, links.at(hop)) * own, own, 0)
                for s in seqs
            ],
            axis=0,
        )

    meta = jnp.stack(
        [fsdp, tp, ctx * (block_len // key_block)] + [place(s, tp) for s in seqs]
    ).astype(jnp.int32)

    down_full = lax.all_gather(down_weight, "fsdp", axis=1, tiled=True)
    gate_full = lax.all_gather(gate_weight, "fsdp", axis=0, tiled=True)
    up_full = lax.all_gather(up_weight, "fsdp", axis=0, tiled=True)
    q_full = lax.all_gather(
        lax.all_gather(query_weight, "tp", axis=1, tiled=True), "fsdp", axis=0, tiled=True
    )

    lanes = q_cols + kv_cols
    smalls = jnp.concatenate([b.reshape(-1) for b in (query_bias, key_bias, value_bias)])
    extra = jnp.stack(
        [jnp.pad(row, (0, lanes - row.shape[0])) for row in (attn_gain, mlp_gain, smalls)]
    )
    extra = jnp.pad(extra, ((0, 13), (0, 0)))
    qkv = links.gather_fsdp(
        jnp.concatenate(
            [jnp.concatenate([query_weight, key_weight, value_weight], axis=1), extra], axis=0
        )
    )
    height = shard + 16
    rows = jnp.stack(
        [p[shard : shard + 3] for p in (qkv[0], qkv[2][:height], qkv[1], qkv[2][height:])]
    )
    rows = [
        lax.dynamic_index_in_dim(rows, jnp.bitwise_xor(fsdp, j), 0, keepdims=False) for j in range(4)
    ]
    attn_gamma = jnp.concatenate([r[0, :shard] for r in rows])[None].astype(jnp.float32)
    mlp_gamma = jnp.concatenate([r[1, :shard] for r in rows])[None].astype(jnp.float32)
    bias = jnp.concatenate(
        [r[2, : smalls.shape[0]].reshape(-1, head_dim // fsdps) for r in rows], axis=1
    ).reshape(1, lanes).astype(jnp.float32)

    o_wide = jnp.concatenate(links.gather_tp(output_weight), axis=0)
    o_parts = links.gather_fsdp(o_wide)

    cosine, sine = rope_tables(positions.reshape(tokens), head_dim)
    normed_one, query_blocks, kv_own = project(
        meta, inputs, attn_gamma, bias, qkv, cosine, sine, (local_heads, kv_heads, head_dim, tps)
    )
    if ctxs == 2:
        kv_before = lax.ppermute(kv_own, "ctx", [(0, 1)])
    else:
        kv_before = lax.all_gather(
            kv_own.reshape(seq_count, block_len, kv_cols), "ctx", axis=1, tiled=True
        ).reshape(seq_count * block_len * ctxs, kv_cols)

    def swap(block_of):
        return [block_of(tp)] + [
            links.hop_tp(block_of((tp + hop) % tps), hop) for hop in range(1, tps)
        ]

    queries = jnp.stack(swap(lambda d: lax.dynamic_index_in_dim(query_blocks, d, 0, keepdims=False)))
    order = jnp.tile(jnp.arange(own, dtype=jnp.int32), depth // head_dim // kv_heads)[None]
    sizes = (seq_count, kv_heads, head_dim, tps)
    mixed, lse = attend(meta, queries, kv_before, kv_own, order, key_block, sizes)
    hidden, normed_two = merge(meta, mixed, inputs, o_parts, mlp_gamma, tps)

    two_blocks = links.gather_tp(normed_two)
    acts, gate_grads, up_grads, two_parts, mixed_parts = [], [], [], [], []
    cots = [block_rows(cotangent, hop) for hop in range(tps)]
    for hop in range(tps):
        act_grad = inner_cols(cots[hop], down_full)
        gate = dot(two_blocks[hop], gate_full)
        up_part = dot(two_blocks[hop], up_full)
        sigma = jax.nn.sigmoid(gate)
        act = (gate * sigma * up_part).astype(LOW)
        gate_grad = (act_grad * up_part * (sigma * (1.0 + gate * (1.0 - sigma)))).astype(LOW)
        up_grad = (act_grad * (gate * sigma)).astype(LOW)
        two_parts.append((inner_cols(gate_grad, gate_full) + inner_cols(up_grad, up_full)).astype(LOW))
        mixed_parts.append(dot(act, down_full).astype(LOW))
        acts.append(act)
        gate_grads.append(gate_grad)
        up_grads.append(up_grad)
    two_own, two_got = links.scatter_tp(two_parts)

    act_all, cot_all, two_all, gate_all, up_all = (
        jnp.concatenate(item, axis=0) for item in (acts, cots, two_blocks, gate_grads, up_grads)
    )
    down_weight_grad = links.reduce_weight(inner_rows(act_all, cot_all), 1)
    gate_weight_grad = links.reduce_weight(inner_rows(two_all, gate_all), 0)
    up_weight_grad = links.reduce_weight(inner_rows(two_all, up_all), 0)

    def spread(block):
        blocks = links.gather_tp(lax.optimization_barrier(block.astype(LOW)))
        full = jnp.zeros((seq_count, block_len, width), LOW)
        for hop, item in enumerate(blocks):
            for s in seqs:
                full = lax.dynamic_update_slice(
                    full, item[None, s * own : (s + 1) * own], (s, place(s, links.at(hop)) * own, 0)
                )
        return full

    hidden_grad, branch_grad, attended_grad, mlp_term = turn(
        meta, two_own, two_got, hidden, cotangent, o_parts, mlp_gamma, depth, tps
    )
    q_grad, kv_grad_before, kv_grad_own = attend_back(
        meta, queries, kv_before, kv_own, order, mixed, attended_grad, lse, cosine, sine, key_block, sizes
    )
    kv_shape = (2, kv_heads, seq_count, block_len, head_dim)
    if ctxs == 2:
        kv_part = add_low(
            kv_grad_own, lax.ppermute(kv_grad_before, "ctx", [(1, 0)])
        ).reshape(kv_shape)
    else:
        wide_grad = kv_grad_before.reshape(2, kv_heads, seq_count, ctxs * block_len, head_dim)
        wide_grad = lax.dynamic_update_slice_in_dim(
            wide_grad, kv_grad_own.reshape(kv_shape), ctx * block_len, 3
        )
        kv_part = lax.psum_scatter(wide_grad, "ctx", scatter_dimension=3, tiled=True)

    def kv_rows(hop):
        return jnp.concatenate(
            [
                lax.dynamic_slice_in_dim(kv_part[:, :, s : s + 1], place(s, links.at(hop)) * own, own, 3)
                for s in seqs
            ],
            axis=2,
        )

    kv_mine, kv_got = links.scatter_tp([kv_rows(hop) for hop in range(tps)])
    input_low, kv_grad, attn_term = finish(
        meta, q_grad, kv_mine, kv_got, cosine, sine, q_full, qkv, inputs, hidden_grad, attn_gamma, tps
    )
    input_grad = spread(input_low).astype(jnp.float32)

    kv_each = kv_cols // tps
    attn_sum = jnp.sum(attn_term, axis=0)
    mlp_sum = jnp.sum(mlp_term, axis=0)

    def share(device):
        grads = jnp.concatenate(
            [
                lax.dynamic_slice_in_dim(q_grad, device * q_cols, q_cols, 1),
                lax.dynamic_slice_in_dim(kv_grad, device * kv_each, kv_each, 1),
            ],
            axis=1,
        )
        gains = jnp.concatenate(
            [lax.dynamic_slice_in_dim(item, device * shard, shard, 1) for item in (attn_sum, mlp_sum)], axis=0
        )
        gains = jnp.pad(gains, ((0, 14), (0, q_cols + kv_each - shard))).astype(LOW)
        return jnp.concatenate([grads, gains], axis=0)

    shares = swap(share)
    own_tokens = seq_count * own
    grads_all = jnp.concatenate([item[:own_tokens] for item in shares], axis=0)
    one_all = jnp.concatenate(
        [block_rows(normed_one.reshape(seq_count, block_len, width), hop) for hop in range(tps)], axis=0
    )
    gain_rows = sum(item[own_tokens : own_tokens + 2].astype(jnp.float32) for item in shares)
    bias_row = jnp.sum(grads_all.astype(jnp.float32), axis=0, keepdims=True)
    below = jnp.pad(jnp.concatenate([gain_rows, bias_row], axis=0), ((0, 13), (0, 0))).astype(LOW)
    term = inner_rows(one_all, grads_all).astype(LOW)
    term = jnp.concatenate(
        [item for j in range(fsdps) for item in (term[j * shard : (j + 1) * shard], below)], axis=0
    )
    total = links.sum_ctx(links.scatter_fsdp(term, 0))
    query_weight_grad = total[:shard, :q_cols]
    below = total[shard:]
    part = head_dim // fsdps
    query_bias_grad = lax.dynamic_slice_in_dim(
        below[2, :q_cols].reshape(local_heads, head_dim), fsdp * part, part, 1
    )
    kv_low = jnp.concatenate(
        [total[:shard, q_cols:], below[:, :q_cols].reshape(-1, kv_each), below[:, q_cols:]], axis=0
    ).astype(LOW)
    kv_low = lax.optimization_barrier(kv_low)
    all_low = jnp.stack(links.gather_tp(kv_low))
    by_device = [
        lax.dynamic_index_in_dim(all_low, links.at(j), 0, keepdims=False) for j in range(tps)
    ]
    kv_weight = jnp.concatenate([item[:shard] for item in by_device], axis=1).astype(jnp.float32)
    mine = lax.dynamic_index_in_dim(all_low, (tp - fsdp + tps) % tps, 0, keepdims=False)
    gains = mine[shard : shard + 16 * (q_cols // kv_each)].reshape(16, q_cols).astype(jnp.float32)
    kv_bias = jnp.stack([item[-14] for item in by_device]).reshape(2, kv_heads, head_dim)
    kv_bias = lax.dynamic_slice_in_dim(kv_bias, fsdp * part, part, 2).astype(jnp.float32)
    half = kv_cols // 2

    output_part = links.scatter_fsdp(inner_rows(mixed, branch_grad).astype(LOW), 1)
    output_mine, output_got = links.scatter_tp(
        [
            lax.dynamic_slice_in_dim(output_part, links.at(hop) * q_cols, q_cols, 0)
            for hop in range(tps)
        ]
    )
    output_weight_grad = links.sum_ctx(add_low(output_mine, output_got))

    mixed_mine, mixed_got = links.scatter_tp(mixed_parts)
    outputs = spread(hidden + mixed_mine.astype(jnp.float32) + mixed_got.astype(jnp.float32))

    return (
        outputs,
        input_grad,
        gains[0],
        query_weight_grad,
        query_bias_grad,
        kv_weight[:, :half],
        kv_bias[0],
        kv_weight[:, half:],
        kv_bias[1],
        output_weight_grad,
        gains[1],
        gate_weight_grad,
        up_weight_grad,
        down_weight_grad,
    )


def solution(mesh):
    in_specs = (
        P("fsdp", "ctx", None),
        P("fsdp", "ctx", None),
        P("fsdp", "ctx"),
        P("fsdp"),
        P("fsdp", "tp"),
        P("tp", "fsdp"),
        P("fsdp", None),
        P(None, "fsdp"),
        P("fsdp", None),
        P(None, "fsdp"),
        P("tp", "fsdp"),
        P("fsdp"),
        P("fsdp", "tp"),
        P("fsdp", "tp"),
        P("tp", "fsdp"),
    )
    out_specs = (
        P("fsdp", "ctx", None),
        P("fsdp", "ctx", None),
        P("fsdp"),
        P("fsdp", "tp"),
        P("tp", "fsdp"),
        P("fsdp", None),
        P(None, "fsdp"),
        P("fsdp", None),
        P(None, "fsdp"),
        P("tp", "fsdp"),
        P("fsdp"),
        P("fsdp", "tp"),
        P("fsdp", "tp"),
        P("tp", "fsdp"),
    )
    return jax.shard_map(local, mesh=mesh, in_specs=in_specs, out_specs=out_specs, check_vma=False)
```

time: 2150 us -> 929 us (0.43)
  waiting for transfers between devices: 1410 us -> 409 us
  blocking collectives: 165 us -> 0 us
  matrix products: 308 us -> 196 us
  other arithmetic: 142 us -> 37.7 us
  starting transfers between devices: 1.1 us -> 93.6 us
  Pallas kernels: 0 us -> 64 us
    psum x3 -> x0, waiting for transfers between devices: 915 us -> none  [the longest x1 322 us: local(): lax.psum(jnp.dot(act, down_full, preferred_element_type=jnp.float32).asty...]
    ppermute x0 -> x48, waiting for transfers between devices: none -> 406 us  [the longest x33 315 us: hop_tp(): lax.ppermute(value, 'tp', [(i, (i + hop) % self.tps) for i in range(self....]
    reduce_scatter x9 -> x3, waiting for transfers between devices: 250 us -> 0.01 us  [reduce_weight(): lax.psum_scatter(term.astype(LOW), ('fsdp', 'ctx'), scatter_dimension=axi...]
    all_gather x8 -> x5, waiting for transfers between devices: 176 us -> 0.03 us  [the longest x1 0.02 us: local(): up_full = lax.all_gather(up_weight, 'fsdp', axis=0, tiled=True)]
    all_gather x18 -> x0, blocking collectives: 146 us -> none  [the longest x1 22.9 us: local(): lax.all_gather(key_piece, 'tp', axis=1, tiled=True)]
    ppermute x0 -> x48, starting transfers between devices: none -> 93.2 us  [the longest x5 52.2 us: to_y(): return lax.ppermute(value, 'ctx', [(0, 1), (1, 0)])]
    dot_general x21 -> x12, matrix products: 160 us -> 84 us  [dot(): return jnp.dot(left, right, preferred_element_type=jnp.float32)]
    pallas_call x0 -> x6, Pallas kernels: none -> 64 us  [the longest x1 15.2 us: attend_back(): call(functools.partial(bwd_kernel, heads, block, parts), (seq_count, kv_h...]
  transfers between devices with their start and end apart: 23 -> 56, of which waited for: 18 -> 33; matrix products, arithmetic and copies ran while one was open for 21% -> 34% of each run, Pallas kernels for 0% -> 7%
where the time goes in v1:
time: 929 us; the launch traced here: 922 us
  waiting for transfers between devices  409 us (44%)
  matrix products  196 us (21%)
  local copies, waits for them, and re-layouts  105 us (11%)
  starting transfers between devices  93.6 us (10%)
  Pallas kernels  64 us (7%)
  other arithmetic  37.7 us (4%)
  between operations  16.6 us (2%)
    ppermute x33, waiting for transfers between devices, hop_tp(): lax.ppermute(value, 'tp', [(i, (i + hop) % self.tps) for i in range(self....  315 us
    dot_general x12, matrix products, dot(): return jnp.dot(left, right, preferred_element_type=jnp.float32)  84 us
    dot_general x12, matrix products, inner_cols(): lax.dot_general(left, right, (((1,), (1,)), ((), ())), preferred_element_...  60.2 us
    unnamed x250, local copies, waits for them, and re-layouts  52.9 us
    ppermute x5, starting transfers between devices, to_y(): return lax.ppermute(value, 'ctx', [(0, 1), (1, 0)])  52.2 us
    dot_general x5, matrix products, inner_rows(): lax.dot_general(left, right, (((0,), (0,)), ((), ())), preferred_element_...  52.1 us
    ppermute x4, waiting for transfers between devices, to_x(): return lax.ppermute(value, 'fsdp', [(0, 2), (2, 0), (1, 3), (3, 1)])  42.1 us
    ppermute x33, starting transfers between devices, hop_tp(): lax.ppermute(value, 'tp', [(i, (i + hop) % self.tps) for i in range(self....  28.5 us
  transfers between devices with their start and end apart: 56, of which 33 were waited for; matrix products, arithmetic and copies ran while one was open for 34% of the time, Pallas kernels for 7%

profile of v1, /device:TPU:0, one launch (start us, length us, event | category | flops | bytes accessed | tf_op | source)
XLA Modules:
  0.0 921.7 jit_solution(1772732490336354617)
XLA Ops:
  23.0 16.6 %collective-permute-done.7 = bf16[384,384]{1,0:T(8,128)(2,1)S(1)} collective-permute-done((bf16[384,384]{1,0:T(8,128)(2,1)S(1)}, bf16[384,384]{1,0:T(8,128)(2,1)S(1)}, u32[]{:S(2)}, u32[]{:S(2)}) %collective-permute-start.7) | collective-permute-done | bytes 294944 | tf_op jit(solution)/shard_map/ppermute | solution.py:555
  45.0 11.0 %collective-permute-done.8 = bf16[384,384]{1,0:T(8,128)(2,1)S(1)} collective-permute-done((bf16[384,384]{1,0:T(8,128)(2,1)S(1)}, bf16[384,384]{1,0:T(8,128)(2,1)S(1)}, u32[]{:S(2)}, u32[]{:S(2)}) %collective-permute-start.8) | collective-permute-done | bytes 294944 | tf_op jit(solution)/shard_map/ppermute | solution.py:555
  63.4 41.2 %collective-permute-done.9.wx_ref = bf16[1536,384]{1,0:T(8,128)(2,1)S(1)} collective-permute-done((bf16[1536,384]{1,0:T(8,128)(2,1)S(1)}, bf16[1536,384]{1,0:T(8,128)(2,1)S(1)}, u32[]{:S(2)}, u32[]{:S(2)}) %collective-permute-start.9) | collective-permute-done | bytes 1179680 | tf_op jit(solution)/shard_map/ppermute | solution.py:549
  110.5 13.4 %project.1 = (bf16[1536,1536]{1,0:T(8,128)(2,1)}, bf16[4,384,384]{2,1,0:T(8,128)(2,1)S(1)}, bf16[1536,512]{1,0:T(8,128)(2,1)}) custom-call(s32[5]{0:T(128)S(1)} %stack.78.meta, bf16[2,768,1536]{2,1,0:T(8,128)(2,1)} %x_ref.5, f32[1,1536]{1,0:T(1,128)S(1)} %maximum_convert_fusion.4.gain_ref, f32[1,896]{1,0:T(1,128)S(1)} %bitcast.204, ...), custom_call_target="tpu_custom_call" | custom-call | flops 4227858432 | bytes 18874368 | tf_op jit(solution)/shard_map/project/pallas_call | solution.py:130
  143.7 11.6 %collective-permute-done.3 = bf16[384,384]{1,0:T(8,128)(2,1)} collective-permute-done((bf16[384,384]{1,0:T(8,128)(2,1)}, bf16[384,384]{1,0:T(8,128)(2,1)}, u32[]{:S(2)}, u32[]{:S(2)}) %collective-permute-start.3) | collective-permute-done | bytes 294944 | tf_op jit(solution)/shard_map/ppermute | solution.py:555
  184.1 24.5 %collective-permute-done.11 = bf16[384,1536]{1,0:T(8,128)(2,1)S(1)} collective-permute-done((bf16[384,1536]{1,0:T(8,128)(2,1)S(1)}, bf16[384,1536]{1,0:T(8,128)(2,1)S(1)}, u32[]{:S(2)}, u32[]{:S(2)}) %collective-permute-start.11) | collective-permute-done | bytes 1179680 | tf_op jit(solution)/shard_map/ppermute | solution.py:555
  218.6 18.7 %collective-permute-done.12 = bf16[384,1536]{1,0:T(8,128)(2,1)} collective-permute-done((bf16[384,1536]{1,0:T(8,128)(2,1)S(1)}, bf16[384,1536]{1,0:T(8,128)(2,1)}, u32[]{:S(2)}, u32[]{:S(2)}) %collective-permute-start.12) | collective-permute-done | bytes 1179680 | tf_op jit(solution)/shard_map/ppermute | solution.py:555
  292.9 12.6 %multiply_convert_fusion.2 = (bf16[384,2240]{0,1:T(8,128)(2,1)}, bf16[384,2240]{0,1:T(8,128)(2,1)}, bf16[384,2240]{0,1:T(8,128)(2,1)S(1)}) fusion(f32[384,2240]{0,1:T(8,128)} %fusion.54, f32[384,2240]{0,1:T(8,128)} %fusion.137, bf16[384,1536]{1,0:T(8,128)(2,1)} %collective-permute-done.12, bf16[1536,2240]{0,1:T(8,128)(2,1)} %all-gather.6.cloned.1.call-done), kind=kOutput, calls=%fused_computation.28 | convolution fusion | flops 2655313920 | bytes 20103168 | tf_op jit(solution)/shard_map/dot_general | solution.py:31
  340.3 16.2 %convolution_convert_fusion = bf16[2240,1536]{0,1:T(8,128)(2,1)} fusion(bf16[1536,1536]{1,0:T(8,128)(2,1)} %get-tuple-element.62, bf16[384,2240]{0,1:T(8,128)(2,1)S(1)} %get-tuple-element.86, bf16[384,2240]{0,1:T(8,128)(2,1)S(1)} %get-tuple-element.83, bf16[384,2240]{0,1:T(8,128)(2,1)S(1)} %get-tuple-element.80, bf16[384,2240]{0,1:T(8,128)(2,1)S(1)} %get-tuple-element.89), kind=kOutput, calls=%fused_computation | convolution fusion | flops 10600611840 | bytes 18481152 | tf_op jit(solution)/shard_map/dot_general | solution.py:35
  363.8 14.2 %convolution_convert_fusion.1 = bf16[1536,2240]{1,0:T(8,128)(2,1)} fusion(bf16[1536,1536]{1,0:T(8,128)(2,1)S(1)} %constant_dynamic-update-slice_fusion.16, bf16[384,2240]{0,1:T(8,128)(2,1)S(1)} %copy-done.56, bf16[384,2240]{0,1:T(8,128)(2,1)S(1)} %copy-done.54, bf16[384,2240]{0,1:T(8,128)(2,1)S(1)} %copy-done.49, bf16[384,2240]{0,1:T(8,128)(2,1)S(1)} %copy-done.42), kind=kOutput, calls=%fused_computation.1 | convolution fusion | flops 10600611840 | bytes 18481152 | tf_op jit(solution)/shard_map/dot_general | solution.py:35
  397.4 13.8 %convolution_convert_fusion.2 = bf16[1536,2240]{1,0:T(8,128)(2,1)} fusion(bf16[1536,1536]{1,0:T(8,128)(2,1)S(1)} %bitcast.222, bf16[384,2240]{0,1:T(8,128)(2,1)S(1)} %copy-done.44, bf16[384,2240]{0,1:T(8,128)(2,1)S(1)} %copy-done.41, bf16[384,2240]{0,1:T(8,128)(2,1)S(1)} %copy-done.48, bf16[384,2240]{0,1:T(8,128)(2,1)S(1)} %copy-done.46), kind=kOutput, calls=%fused_computation.2 | convolution fusion | flops 10600611840 | bytes 18481152 | tf_op jit(solution)/shard_map/dot_general | solution.py:35
  436.8 11.4 %collective-permute-done.14 = bf16[384,1536]{1,0:T(8,128)(2,1)} collective-permute-done((bf16[384,1536]{1,0:T(8,128)(2,1)}, bf16[384,1536]{1,0:T(8,128)(2,1)}, u32[]{:S(2)}, u32[]{:S(2)}) %collective-permute-start.14) | collective-permute-done | bytes 1179680 | tf_op jit(solution)/shard_map/ppermute | solution.py:555
  452.7 20.7 %collective-permute-done.21 = bf16[384,1536]{1,0:T(8,128)(2,1)S(1)} collective-permute-done((bf16[384,1536]{1,0:T(8,128)(2,1)S(1)}, bf16[384,1536]{1,0:T(8,128)(2,1)S(1)}, u32[]{:S(2)}, u32[]{:S(2)}) %collective-permute-start.21) | collective-permute-done | bytes 1179680 | tf_op jit(solution)/shard_map/ppermute | solution.py:555
  477.0 21.7 %collective-permute-done.15 = bf16[384,1536]{1,0:T(8,128)(2,1)S(1)} collective-permute-done((bf16[384,1536]{1,0:T(8,128)(2,1)S(1)}, bf16[384,1536]{1,0:T(8,128)(2,1)S(1)}, u32[]{:S(2)}, u32[]{:S(2)}) %collective-permute-start.15) | collective-permute-done | bytes 1179680 | tf_op jit(solution)/shard_map/ppermute | solution.py:555
  500.1 23.9 %collective-permute-done.22.b_ref = bf16[384,1536]{1,0:T(8,128)(2,1)S(1)} collective-permute-done((bf16[384,1536]{1,0:T(8,128)(2,1)S(1)}, bf16[384,1536]{1,0:T(8,128)(2,1)S(1)}, u32[]{:S(2)}, u32[]{:S(2)}) %collective-permute-start.22) | collective-permute-done | bytes 1179680 | tf_op jit(solution)/shard_map/ppermute | solution.py:555
  540.6 15.2 %attend_back.1 = (bf16[384,1536]{1,0:T(8,128)(2,1)S(1)}, bf16[2,2,1536,128]{3,2,1,0:T(8,128)(2,1)}, bf16[2,2,1536,128]{3,2,1,0:T(8,128)(2,1)}) custom-call(s32[5]{0:T(128)S(1)} %copy-done.24, bf16[4,384,384]{2,1,0:T(8,128)(2,1)S(1)} %copy-done.11, bf16[4,384,384]{2,1,0:T(8,128)(2,1)S(1)} %copy-done.11, ...), custom_call_target="tpu_custom_call" | custom-call | flops 14495514624 | bytes 8388608 | tf_op jit(solution)/shard_map/attend_back/pallas_call | solution.py:331
  570.6 22.0 %collective-permute-done.17 = bf16[384,1536]{1,0:T(8,128)(2,1)} collective-permute-done((bf16[384,1536]{1,0:T(8,128)(2,1)}, bf16[384,1536]{1,0:T(8,128)(2,1)}, u32[]{:S(2)}, u32[]{:S(2)}) %collective-permute-start.17) | collective-permute-done | bytes 1179680 | tf_op jit(solution)/shard_map/ppermute | solution.py:555
  594.5 21.4 %collective-permute-done.23 = bf16[2,2,1536,128]{3,2,1,0:T(8,128)(2,1)} collective-permute-done((bf16[2,2,1536,128]{3,2,1,0:T(8,128)(2,1)}, bf16[2,2,1536,128]{3,2,1,0:T(8,128)(2,1)}, u32[]{:S(2)}, u32[]{:S(2)}) %collective-permute-start.23) | collective-permute-done | bytes 1572896 | tf_op jit(solution)/shard_map/ppermute | solution.py:764
  678.3 11.1 %collective-permute-done.30 = bf16[400,512]{1,0:T(8,128)(2,1)S(1)} collective-permute-done((bf16[400,512]{1,0:T(8,128)(2,1)S(1)}, bf16[400,512]{1,0:T(8,128)(2,1)S(1)}, u32[]{:S(2)}, u32[]{:S(2)}) %collective-permute-start.30) | collective-permute-done | bytes 409632 | tf_op jit(solution)/shard_map/ppermute | solution.py:555
  690.3 38.2 %collective-permute-done.31 = bf16[400,512]{1,0:T(8,128)(2,1)S(1)} collective-permute-done((bf16[400,512]{1,0:T(8,128)(2,1)S(1)}, bf16[400,512]{1,0:T(8,128)(2,1)S(1)}, u32[]{:S(2)}, u32[]{:S(2)}) %collective-permute-start.31) | collective-permute-done | bytes 409632 | tf_op jit(solution)/shard_map/ppermute | solution.py:555
  766.6 24.4 %collective-permute-start.35 = (bf16[400,512]{1,0:T(8,128)(2,1)S(1)}, bf16[400,512]{1,0:T(8,128)(2,1)S(1)}, u32[]{:S(2)}, u32[]{:S(2)}) collective-permute-start(bf16[400,512]{1,0:T(8,128)(2,1)S(1)} %add_convert_fusion.8), channel_id=1, source_target_pairs={{0,4},{4,0},{1,5},{5,1},{2,6},{6,2},{3,7},{7,3},{8,12},{12,8},{9,1... | collective-permute-start | bytes 1228808 | tf_op jit(solution)/shard_map/ppermute | solution.py:552
  794.6 24.4 %collective-permute-start.44 = (bf16[384,384]{0,1:T(8,128)(2,1)S(1)}, bf16[384,384]{0,1:T(8,128)(2,1)S(1)}, u32[]{:S(2)}, u32[]{:S(2)}) collective-permute-start(bf16[384,384]{0,1:T(8,128)(2,1)S(1)} %add_convert_fusion.11), channel_id=1, source_target_pairs={{0,4},{4,0},{1,5},{5,1},{2,6},{6,2},{3,7},{7,3},{8,12},{12,8},{9,1... | collective-permute-start | bytes 884744 | tf_op jit(solution)/shard_map/ppermute | solution.py:552
  844.2 16.6 %collective-permute-done.29 = bf16[384,1536]{1,0:T(8,128)(2,1)S(1)} collective-permute-done((bf16[384,1536]{1,0:T(8,128)(2,1)}, bf16[384,1536]{1,0:T(8,128)(2,1)S(1)}, u32[]{:S(2)}, u32[]{:S(2)}) %collective-permute-start.29) | collective-permute-done | bytes 1179680 | tf_op jit(solution)/shard_map/ppermute | solution.py:555
  880.5 12.3 %collective-permute-done.46 = bf16[192,2240]{1,0:T(8,128)(2,1)} collective-permute-done((bf16[192,2240]{1,0:T(8,128)(2,1)}, bf16[192,2240]{1,0:T(8,128)(2,1)}, u32[]{:S(2)}, u32[]{:S(2)}) %collective-permute-start.46) | collective-permute-done | bytes 860192 | tf_op jit(solution)/shard_map/ppermute | solution.py:552
  (535 shorter events, 448.0 us)
Async XLA Ops:
  7.2 211.4 %all-gather.12.cloned.1.call-start = ((), (), s32[]{:S(2)}) async-start(), calls=%async_computation.6 | async-start | bytes 1474560 | tf_op jit(solution)/shard_map/all_gather | solution.py:668
  8.0 229.7 %all-gather.8.cloned.1.call-start = ((), (), s32[]{:S(2)}) async-start(), calls=%async_computation.4 | async-start | bytes 8601600 | tf_op jit(solution)/shard_map/all_gather | solution.py:666
  8.8 264.1 %all-gather.10.cloned.1.call-start = ((), (), s32[]{:S(2)}) async-start(), calls=%async_computation.5 | async-start | bytes 8601600 | tf_op jit(solution)/shard_map/all_gather | solution.py:664
  9.5 283.4 %all-gather.6.cloned.1.call-start = ((), (), s32[]{:S(2)}) async-start(), calls=%async_computation.3 | async-start | bytes 8601600 | tf_op jit(solution)/shard_map/all_gather | solution.py:665
  10.1 635.3 %all-gather.14.cloned.1.call-start = ((), (), s32[]{:S(2)}) async-start(), calls=%async_computation.7 | async-start | bytes 5898240 | tf_op jit(solution)/shard_map/all_gather | solution.py:667
  45.0 60.8 %collective-permute-start.1 = (bf16[800,896]{1,0:T(8,128)(2,1)}, bf16[800,896]{1,0:T(8,128)(2,1)}, u32[]{:S(2)}, u32[]{:S(2)}) collective-permute-start(bf16[800,896]{1,0:T(8,128)(2,1)} %pad_maximum_fusion.1), channel_id=1, source_target_pairs={{0,8},{8,0},{16,24},{24,16},{1,9},{9,1},{17,25},{25,17},{2,10},{10... | collective-permute-start | bytes 4300808 | tf_op jit(solution)/shard_map/ppermute | solution.py:546
  56.8 47.8 %collective-permute-start.9 = (bf16[1536,384]{1,0:T(8,128)(2,1)S(1)}, bf16[1536,384]{1,0:T(8,128)(2,1)S(1)}, u32[]{:S(2)}, u32[]{:S(2)}) collective-permute-start(bf16[1536,384]{1,0:T(8,128)(2,1)S(1)} %get-tuple-element.151.w_ref), channel_id=1, source_target_pairs={{0,16},{16,0},{8,24},{24,8},{1,17},{17,1},{9,25},{25,9},{2,18},{18... | collective-permute-start | bytes 3538952 | tf_op jit(solution)/shard_map/ppermute | solution.py:549
  105.8 65.9 %collective-permute-start.10 = (bf16[3072,384]{1,0:T(8,128)(2,1)}, bf16[3072,384]{1,0:T(8,128)(2,1)}, u32[]{:S(2)}, u32[]{:S(2)}) collective-permute-start(bf16[3072,384]{1,0:T(8,128)(2,1)} %constant_dynamic-update-slice_fusion.7), channel_id=1, source_target_pairs={{0,8},{8,0},{16,24},{24,16},{1,9},{9,1},{17,25},{25,17},{2,10},{10... | collective-permute-start | bytes 7077896 | tf_op jit(solution)/shard_map/ppermute | solution.py:546
  218.6 624.2 %reduce-scatter.8.cloned.1.call-start = ((), (), s32[]{:S(2)}) async-start(), calls=%async_computation.10 | async-start | bytes 7962624 | tf_op jit(solution)/shard_map/reduce_scatter | solution.py:602
  356.6 513.4 %reduce-scatter.6.cloned.1.call-start = ((), (), s32[]{:S(2)}) async-start(), calls=%async_computation.9 | async-start | bytes 7962624 | tf_op jit(solution)/shard_map/reduce_scatter | solution.py:602
  378.0 493.4 %reduce-scatter.4.cloned.1.call-start = ((), (), s32[]{:S(2)}) async-start(), calls=%async_computation.8 | async-start | bytes 7962624 | tf_op jit(solution)/shard_map/reduce_scatter | solution.py:602
  397.4 50.8 %collective-permute-start.14 = (bf16[384,1536]{1,0:T(8,128)(2,1)}, bf16[384,1536]{1,0:T(8,128)(2,1)}, u32[]{:S(2)}, u32[]{:S(2)}) collective-permute-start(bf16[384,1536]{1,0:T(8,128)(2,1)} %convolution_convert_fusion.5), channel_id=1, source_target_pairs={{0,1},{1,2},{2,3},{3,0},{4,5},{5,6},{6,7},{7,4},{8,9},{9,10},{10,1... | collective-permute-start | bytes 3538952 | tf_op jit(solution)/shard_map/ppermute | solution.py:555
  452.6 46.0 %collective-permute-start.15 = (bf16[384,1536]{1,0:T(8,128)(2,1)S(1)}, bf16[384,1536]{1,0:T(8,128)(2,1)S(1)}, u32[]{:S(2)}, u32[]{:S(2)}) collective-permute-start(bf16[384,1536]{1,0:T(8,128)(2,1)S(1)} %add_convert_fusion.6), channel_id=1, source_target_pairs={{0,1},{1,2},{2,3},{3,0},{4,5},{5,6},{6,7},{7,4},{8,9},{9,10},{10,1... | collective-permute-start | bytes 3538952 | tf_op jit(solution)/shard_map/ppermute | solution.py:555
  473.7 50.2 %collective-permute-start.22 = (bf16[384,1536]{1,0:T(8,128)(2,1)S(1)}, bf16[384,1536]{1,0:T(8,128)(2,1)S(1)}, u32[]{:S(2)}, u32[]{:S(2)}) collective-permute-start(bf16[384,1536]{1,0:T(8,128)(2,1)S(1)} %add_convert_fusion.3), channel_id=1, source_target_pairs={{0,1},{1,2},{2,3},{3,0},{4,5},{5,6},{6,7},{7,4},{8,9},{9,10},{10,1... | collective-permute-start | bytes 3538952 | tf_op jit(solution)/shard_map/ppermute | solution.py:555
  500.1 57.3 %collective-permute-start.16 = (bf16[384,1536]{1,0:T(8,128)(2,1)}, bf16[384,1536]{1,0:T(8,128)(2,1)S(1)}, u32[]{:S(2)}, u32[]{:S(2)}) collective-permute-start(bf16[384,1536]{1,0:T(8,128)(2,1)} %add_convert_fusion.5), channel_id=1, source_target_pairs={{0,1},{1,2},{2,3},{3,0},{4,5},{5,6},{6,7},{7,4},{8,9},{9,10},{10,1... | collective-permute-start | bytes 3538952 | tf_op jit(solution)/shard_map/ppermute | solution.py:555
  539.8 90.4 %collective-permute-start.39 = (bf16[1536,768]{0,1:T(8,128)(2,1)}, bf16[1536,768]{0,1:T(8,128)(2,1)}, u32[]{:S(2)}, u32[]{:S(2)}) collective-permute-start(bf16[1536,768]{0,1:T(8,128)(2,1)} %pad_maximum_fusion), channel_id=1, source_target_pairs={{0,8},{8,0},{16,24},{24,16},{1,9},{9,1},{17,25},{25,17},{2,10},{10... | collective-permute-start | bytes 7077896 | tf_op jit(solution)/shard_map/ppermute | solution.py:546
  555.9 60.1 %collective-permute-start.23 = (bf16[2,2,1536,128]{3,2,1,0:T(8,128)(2,1)}, bf16[2,2,1536,128]{3,2,1,0:T(8,128)(2,1)}, u32[]{:S(2)}, u32[]{:S(2)}) collective-permute-start(bf16[2,2,1536,128]{3,2,1,0:T(8,128)(2,1)} %get-tuple-element.40), channel_id=1, source_target_pairs={{4,0},{5,1},{6,2},{7,3},{12,8},{13,9},{14,10},{15,11},{20,16},{21,... | collective-permute-start | bytes 4718600 | tf_op jit(solution)/shard_map/ppermute | solution.py:764
  592.6 48.8 %collective-permute-start.18 = (bf16[384,1536]{1,0:T(8,128)(2,1)}, bf16[384,1536]{1,0:T(8,128)(2,1)}, u32[]{:S(2)}, u32[]{:S(2)}) collective-permute-start(bf16[384,1536]{1,0:T(8,128)(2,1)} %collective-permute-done.17), channel_id=1, source_target_pairs={{0,1},{1,2},{2,3},{3,0},{4,5},{5,6},{6,7},{7,4},{8,9},{9,10},{10,1... | collective-permute-start | bytes 3538952 | tf_op jit(solution)/shard_map/ppermute | solution.py:555
  633.8 102.1 %collective-permute-start.40 = (bf16[1536,384]{0,1:T(8,128)(2,1)}, bf16[1536,384]{0,1:T(8,128)(2,1)}, u32[]{:S(2)}, u32[]{:S(2)}) collective-permute-start(bf16[1536,384]{0,1:T(8,128)(2,1)} %constant_dynamic-slice_fusion.1), channel_id=1, source_target_pairs={{0,16},{16,0},{8,24},{24,8},{1,17},{17,1},{9,25},{25,9},{2,18},{18... | collective-permute-start | bytes 3538952 | tf_op jit(solution)/shard_map/ppermute | solution.py:549
  641.4 105.0 %collective-permute-start.19 = (bf16[384,1536]{1,0:T(8,128)(2,1)}, bf16[384,1536]{1,0:T(8,128)(2,1)}, u32[]{:S(2)}, u32[]{:S(2)}) collective-permute-start(bf16[384,1536]{1,0:T(8,128)(2,1)} %collective-permute-done.18), channel_id=1, source_target_pairs={{0,1},{1,2},{2,3},{3,0},{4,5},{5,6},{6,7},{7,4},{8,9},{9,10},{10,1... | collective-permute-start | bytes 3538952 | tf_op jit(solution)/shard_map/ppermute | solution.py:555
  669.5 59.0 %collective-permute-start.31 = (bf16[400,512]{1,0:T(8,128)(2,1)S(1)}, bf16[400,512]{1,0:T(8,128)(2,1)S(1)}, u32[]{:S(2)}, u32[]{:S(2)}) collective-permute-start(bf16[400,512]{1,0:T(8,128)(2,1)S(1)} %pad_maximum_fusion.9), channel_id=1, source_target_pairs={{0,2},{1,3},{2,0},{3,1},{4,6},{5,7},{6,4},{7,5},{8,10},{9,11},{10,... | collective-permute-start | bytes 1228808 | tf_op jit(solution)/shard_map/ppermute | solution.py:555
  669.6 85.9 %collective-permute-start.27 = (bf16[384,1536]{1,0:T(8,128)(2,1)S(1)}, bf16[384,1536]{1,0:T(8,128)(2,1)S(1)}, u32[]{:S(2)}, u32[]{:S(2)}) collective-permute-start(bf16[384,1536]{1,0:T(8,128)(2,1)S(1)} %copy-done.13), channel_id=1, source_target_pairs={{0,1},{1,2},{2,3},{3,0},{4,5},{5,6},{6,7},{7,4},{8,9},{9,10},{10,1... | collective-permute-start | bytes 3538952 | tf_op jit(solution)/shard_map/ppermute | solution.py:555
  755.5 77.0 %collective-permute-start.28 = (bf16[384,1536]{1,0:T(8,128)(2,1)S(1)}, bf16[384,1536]{1,0:T(8,128)(2,1)}, u32[]{:S(2)}, u32[]{:S(2)}) collective-permute-start(bf16[384,1536]{1,0:T(8,128)(2,1)S(1)} %collective-permute-done.27), channel_id=1, source_target_pairs={{0,1},{1,2},{2,3},{3,0},{4,5},{5,6},{6,7},{7,4},{8,9},{9,10},{10,1... | collective-permute-start | bytes 3538952 | tf_op jit(solution)/shard_map/ppermute | solution.py:555
  766.6 52.4 %collective-permute-start.35 = (bf16[400,512]{1,0:T(8,128)(2,1)S(1)}, bf16[400,512]{1,0:T(8,128)(2,1)S(1)}, u32[]{:S(2)}, u32[]{:S(2)}) collective-permute-start(bf16[400,512]{1,0:T(8,128)(2,1)S(1)} %add_convert_fusion.8), channel_id=1, source_target_pairs={{0,4},{4,0},{1,5},{5,1},{2,6},{6,2},{3,7},{7,3},{8,12},{12,8},{9,1... | collective-permute-start | bytes 1228808 | tf_op jit(solution)/shard_map/ppermute | solution.py:552
  (141 other events, 1954.2 us)
Sparse Core Ops, SparseCore 0:
  9.6 41.3 all-gather.11
  52.5 69.7 all-gather.7
  123.9 48.1 all-gather.9
  173.5 49.6 all-gather.5
  224.5 43.7 all-gather.13
  356.7 73.9 reduce-scatter.7
  434.6 65.4 reduce-scatter.5
  503.6 65.4 reduce-scatter.3

commit v2 on v1

--- a/solution.py
+++ b/solution.py
@@ -47,11 +47,15 @@
     return (left.astype(jnp.float32) + right.astype(jnp.float32)).astype(LOW)
 
 
+def after(value, token):
+    return lax.optimization_barrier((value, token))[0]
+
+
 def root_of(values):
     return lax.rsqrt(jnp.mean(values * values, axis=-1, keepdims=True) + EPS)
 
 
-FSDP, TP, BEFORE, PLACE = 0, 1, 2, 3
+FSDP, TP, CTX, BEFORE, PLACE = 0, 1, 2, 3, 4
 
 
 def shard_at(meta, flip, size):
@@ -88,19 +92,16 @@
 
 
 def project_kernel(
-    local_heads, kv_heads, head_dim, meta, x_ref, gain_ref, bias_ref, w_ref, wx_ref, wc_ref,
-    cos_ref, sin_ref, n_ref, q_ref, kv_ref,
+    local_heads, kv_heads, head_dim, meta, x_ref, gain_ref, bias_ref, *refs
 ):
+    weights, (cos_ref, sin_ref, n_ref, q_ref, kv_ref) = refs[:4], refs[4:]
     rows = x_ref.shape[1]
     size = n_ref.shape[1] // 4
-    height = w_ref.shape[0]
     values = x_ref[...].reshape(rows, -1).astype(jnp.float32)
     n_ref[...] = (values * root_of(values) * gain_ref[...]).astype(LOW)
     lin = bias_ref[...]
-    for flip, weight in enumerate(
-        (w_ref[:size, :], wc_ref[:size, :], wx_ref[:size, :], wc_ref[height : height + size, :])
-    ):
-        lin = lin + dot(n_ref[:, pl.ds(shard_at(meta, flip, size), size)], weight)
+    for flip, weight in enumerate(weights):
+        lin = lin + dot(n_ref[:, pl.ds(shard_at(meta, flip, size), size)], weight[:size, :])
     cosine, sine = cos_ref[...], sin_ref[...]
     for head in range(local_heads + 2 * kv_heads):
         part = lin[:, head * head_dim : (head + 1) * head_dim]
@@ -208,7 +209,7 @@
         ].astype(LOW)
 
 
-def bwd_kernel(heads, block, parts, meta, *refs):
+def bwd_kernel(heads, block, parts, seq, meta, *refs):
     q_refs, (
         kb_ref, vb_ref, k_ref, v_ref, order_ref, o_ref, g_ref, lse_ref, cos_ref, sin_ref,
         dq_ref, db_ref, dd_ref, qg_ref, gg_ref, acc_ref,
@@ -228,7 +229,7 @@
     center = jnp.sum(jnp.transpose(acc_ref[...]), axis=0, keepdims=True)
     acc_ref[...] = jnp.zeros_like(acc_ref)
     lse = lse_ref[...].reshape(order_ref.shape)
-    first = meta[PLACE + pl.program_id(0)] * own
+    first = meta[PLACE + seq] * own
     last = first // block
 
     def step(key_ref, value_ref, out_ref, index, masked):
@@ -273,25 +274,30 @@
         dq_ref[:, head * head_dim : (head + 1) * head_dim] = grad.astype(LOW)
 
 
-def attention_specs(queries, kv_before, kv_own, sizes):
+def attention_specs(queries, kv_before, kv_own, sizes, seq=None):
     seq_count, kv_heads, head_dim, tps = sizes
     rows = queries.shape[1] // seq_count
     parts = tps // kv_heads
     heads = queries.shape[2] * parts // head_dim
     before, block_len = kv_before.shape[0] // seq_count, kv_own.shape[0] // seq_count
 
-    def piece(index):
-        return pl.BlockSpec(
+    def spec(dims, index):
+        if seq is None:
+            return pl.BlockSpec(dims, index)
+        return pl.BlockSpec(dims, lambda g, m: index(seq, g, m))
+
+    def piece(part):
+        return spec(
             (1, rows, queries.shape[2]),
-            lambda s, g, m: (lax.rem(m[TP] + tps - (g * parts + index), tps), s, 0),
+            lambda s, g, m: (lax.rem(m[TP] + tps - (g * parts + part), tps), s, 0),
         )
 
-    specs = [piece(index) for index in range(parts)] + [
-        pl.BlockSpec((before, head_dim), lambda s, g, m: (s, g)),
-        pl.BlockSpec((before, head_dim), lambda s, g, m: (s, kv_heads + g)),
-        pl.BlockSpec((block_len, head_dim), lambda s, g, m: (s, g)),
-        pl.BlockSpec((block_len, head_dim), lambda s, g, m: (s, kv_heads + g)),
-        pl.BlockSpec((1, heads * rows), lambda s, g, m: (0, 0)),
+    specs = [piece(part) for part in range(parts)] + [
+        spec((before, head_dim), lambda s, g, m: (s, g)),
+        spec((before, head_dim), lambda s, g, m: (s, kv_heads + g)),
+        spec((block_len, head_dim), lambda s, g, m: (s, g)),
+        spec((block_len, head_dim), lambda s, g, m: (s, kv_heads + g)),
+        spec((1, heads * rows), lambda s, g, m: (0, 0)),
     ]
     return specs, rows, parts, heads, before, block_len
 
@@ -321,40 +327,44 @@
     )(meta, *([queries] * parts), kv_before, kv_before, kv_own, kv_own, order)
 
 
-def attend_back(meta, queries, kv_before, kv_own, order, mixed, grads, lse, cosine, sine, block, sizes):
+def attend_back(
+    meta, seq, queries, kv_before, kv_own, order, mixed, grads, lse, cosine, sine, block, sizes
+):
     seq_count, kv_heads, head_dim, tps = sizes
-    specs, rows, parts, heads, before, block_len = attention_specs(queries, kv_before, kv_own, sizes)
+    specs, rows, parts, heads, before, block_len = attention_specs(
+        queries, kv_before, kv_own, sizes, seq
+    )
     width, wide = kv_heads * heads * head_dim, heads * rows
-    work = seq_count * rows * width * (before + block_len)
-    wide_spec = pl.BlockSpec((rows, heads * head_dim), lambda s, g, m: (s, g))
-    table_spec = pl.BlockSpec((rows, head_dim), lambda s, g, m: (s * tps + m[PLACE + s], 0))
+    work = rows * width * (before + block_len)
+    wide_spec = pl.BlockSpec((rows, heads * head_dim), lambda g, m: (seq, g))
+    table_spec = pl.BlockSpec((rows, head_dim), lambda g, m: (seq * tps + m[PLACE + seq], 0))
     return call(
-        functools.partial(bwd_kernel, heads, block, parts),
-        (seq_count, kv_heads),
+        functools.partial(bwd_kernel, heads, block, parts, seq),
+        (kv_heads,),
         specs
         + [
             wide_spec,
             wide_spec,
-            pl.BlockSpec((1, 1, 1, wide), lambda s, g, m: (s, g, 0, 0)),
+            pl.BlockSpec((1, 1, 1, wide), lambda g, m: (seq, g, 0, 0)),
             table_spec,
             table_spec,
         ],
         [
-            wide_spec,
-            pl.BlockSpec((2, 1, before, head_dim), lambda s, g, m: (0, g, s, 0)),
-            pl.BlockSpec((2, 1, block_len, head_dim), lambda s, g, m: (0, g, s, 0)),
-        ],
-        [
-            shape((seq_count * rows, width), LOW),
-            shape((2, kv_heads, seq_count * before, head_dim), LOW),
-            shape((2, kv_heads, seq_count * block_len, head_dim), LOW),
+            pl.BlockSpec((rows, heads * head_dim), lambda g, m: (0, g)),
+            pl.BlockSpec((2, 1, before, head_dim), lambda g, m: (0, g, 0, 0)),
+            pl.BlockSpec((2, 1, block_len, head_dim), lambda g, m: (0, g, 0, 0)),
+        ],
+        [
+            shape((rows, width), LOW),
+            shape((2, kv_heads, before, head_dim), LOW),
+            shape((2, kv_heads, block_len, head_dim), LOW),
         ],
         [
             pltpu.VMEM((wide, head_dim), LOW),
             pltpu.VMEM((wide, head_dim), LOW),
             pltpu.VMEM((wide, head_dim), jnp.float32),
         ],
-        cost=pl.CostEstimate(flops=16 * work, bytes_accessed=1 << 23, transcendentals=0),
+        cost=pl.CostEstimate(flops=16 * work, bytes_accessed=1 << 22, transcendentals=0),
         name="attend_back",
     )(
         meta, *([queries] * parts), kv_before, kv_before, kv_own, kv_own, order,
@@ -362,16 +372,14 @@
     )
 
 
-def merge_kernel(tps, meta, o_ref, x_ref, w_ref, wx_ref, wc_ref, gain_ref, h_ref, n_ref, turned_ref):
+def merge_kernel(tps, meta, o_ref, x_ref, *refs):
+    weights, (gain_ref, h_ref, n_ref) = refs[:4], refs[4:]
     rows, width = h_ref.shape
     size, depth = width // 4, o_ref.shape[1]
-    part = depth // tps
-    for hop in range(tps):
-        turned_ref[:, hop * part : (hop + 1) * part] = o_ref[:, pl.ds(tp_at(meta, hop, tps, part), part)]
-    turned = turned_ref[...]
-    for flip, weight in enumerate((w_ref[...], wc_ref[:depth, :], wx_ref[...], wc_ref[depth:, :])):
+    turned = o_ref[...]
+    for flip, weight in enumerate(weights):
         at = pl.ds(shard_at(meta, flip, size), size)
-        h_ref[:, at] = x_ref[0, :, at].astype(jnp.float32) + dot(turned, weight)
+        h_ref[:, at] = x_ref[0, :, at].astype(jnp.float32) + dot(turned, weight[...])
     hidden = h_ref[...]
     n_ref[...] = (hidden * root_of(hidden) * gain_ref[...]).astype(LOW)
 
@@ -392,7 +400,6 @@
         ],
         [row, row],
         [shape((seq_count * own, width), jnp.float32), shape((seq_count * own, width), LOW)],
-        [pltpu.VMEM((own, depth), LOW)],
         cost=pl.CostEstimate(
             flops=2 * seq_count * own * depth * width, bytes_accessed=1 << 23, transcendentals=0
         ),
@@ -401,12 +408,11 @@
 
 
 def turn_kernel(
-    tps, meta, a_ref, b_ref, h_ref, c_ref, w_ref, wx_ref, wc_ref, gain_ref,
-    hg_ref, bg_ref, ag_ref, term_ref, turned_ref,
+    tps, meta, a_ref, b_ref, h_ref, c_ref, *refs,
 ):
+    weights, (gain_ref, hg_ref, bg_ref, ag_ref, term_ref, turned_ref) = refs[:4], refs[4:]
     rows, width = h_ref.shape
     size, depth = width // 4, ag_ref.shape[1]
-    part = depth // tps
     two_grad = a_ref[...].astype(jnp.float32) + b_ref[...].astype(jnp.float32)
     hidden = h_ref[...]
     root = root_of(hidden)
@@ -420,12 +426,9 @@
     hg_ref[...] = grad
     bg_ref[...] = grad.astype(LOW)
     turned_ref[...] = jnp.zeros_like(turned_ref)
-    for flip, weight in enumerate((w_ref[...], wc_ref[:depth, :], wx_ref[...], wc_ref[depth:, :])):
-        turned_ref[...] += inner_cols(bg_ref[:, pl.ds(shard_at(meta, flip, size), size)], weight)
-    for hop in range(tps):
-        ag_ref[:, pl.ds(tp_at(meta, hop, tps, part), part)] = turned_ref[
-            :, hop * part : (hop + 1) * part
-        ].astype(LOW)
+    for flip, weight in enumerate(weights):
+        turned_ref[...] += inner_cols(bg_ref[:, pl.ds(shard_at(meta, flip, size), size)], weight[...])
+    ag_ref[...] = turned_ref[...].astype(LOW)
 
 
 def turn(meta, two_own, two_got, hidden, cotangent, weights, gain, depth, tps):
@@ -460,11 +463,12 @@
 
 
 def finish_kernel(
-    kv_heads, head_dim, meta, g_ref, a_ref, b_ref, cos_ref, sin_ref, q_ref, w_ref, wx_ref, wc_ref,
-    x_ref, hg_ref, gain_ref, out_ref, kv_ref, term_ref, one_ref,
+    kv_heads, head_dim, meta, g_ref, a_ref, b_ref, cos_ref, sin_ref, q_ref, *refs
 ):
+    weights = refs[:4]
+    x_ref, hg_ref, gain_ref, out_ref, kv_ref, term_ref, one_ref = refs[4:]
     rows, width = hg_ref.shape
-    size, height = width // 4, w_ref.shape[0]
+    size = width // 4
     cosine, sine = cos_ref[...], sin_ref[...]
     for kind in range(2):
         for head in range(kv_heads):
@@ -476,14 +480,11 @@
             at = (kind * kv_heads + head) * head_dim
             kv_ref[:, at : at + head_dim] = grad.astype(LOW)
     one_ref[...] = inner_cols(g_ref[...], q_ref[...])
-    skip = w_ref.shape[1] - kv_ref.shape[1]
-    for flip, weight in enumerate(
-        (
-            w_ref[:size, skip:], wc_ref[:size, skip:], wx_ref[:size, skip:],
-            wc_ref[height : height + size, skip:],
+    skip = weights[0].shape[1] - kv_ref.shape[1]
+    for flip, weight in enumerate(weights):
+        one_ref[:, pl.ds(shard_at(meta, flip, size), size)] += inner_cols(
+            kv_ref[...], weight[:size, skip:]
         )
-    ):
-        one_ref[:, pl.ds(shard_at(meta, flip, size), size)] += inner_cols(kv_ref[...], weight)
     one = one_ref[...]
     values = x_ref[...].reshape(rows, width).astype(jnp.float32)
     root = root_of(values)
@@ -535,6 +536,154 @@
     )(meta, q_grad, kv_mine, kv_got, cosine, sine, q_full, *weights, inputs, hidden_grad, gain)
 
 
+def feed_kernel(first, hidden, *refs):
+    n_ref, c_ref, wg_ref, wu_ref, wd_ref = refs[1:6]
+    act_ref, gg_ref, ug_ref, two_ref, mix_ref, two_acc, mix_acc = refs[6 if first else 9 :]
+    step, tile = pl.program_id(0), wg_ref.shape[0]
+    steps = -(-hidden // tile)
+
+    def body(count):
+        gate = inner_cols(n_ref[...], wg_ref[:count, :])
+        up_part = inner_cols(n_ref[...], wu_ref[:count, :])
+        act_grad = inner_cols(c_ref[...], wd_ref[:count, :])
+        sigma = jax.nn.sigmoid(gate)
+        silu = gate * sigma
+        act = (silu * up_part).astype(LOW)
+        gate_grad = (act_grad * up_part * (sigma * (1.0 + gate * (1.0 - sigma)))).astype(LOW)
+        up_grad = (act_grad * silu).astype(LOW)
+        act_ref[:, :count], gg_ref[:, :count], ug_ref[:, :count] = act, gate_grad, up_grad
+        return (
+            dot(gate_grad, wg_ref[:count, :]) + dot(up_grad, wu_ref[:count, :]),
+            dot(act, wd_ref[:count, :]),
+        )
+
+    @pl.when(step == 0)
+    def _():
+        two_acc[...], mix_acc[...] = body(tile)
+
+    @pl.when(jnp.logical_and(step > 0, step < steps - 1))
+    def _():
+        two, mix = body(tile)
+        two_acc[...] += two
+        mix_acc[...] += mix
+
+    @pl.when(step == steps - 1)
+    def _():
+        two, mix = body(hidden - (steps - 1) * tile)
+        two_ref[...] = (two_acc[...] + two).astype(LOW)
+        mix_ref[...] = (mix_acc[...] + mix).astype(LOW)
+
+
+def feed(meta, normed, cots, gate, up, down, hop, tps, kept):
+    rows, width = normed.shape
+    hidden = down.shape[0]
+    tile = 768
+    assert hidden > tile
+    weight = pl.BlockSpec((tile, width), lambda j, m: (j, 0))
+    column = pl.BlockSpec((rows, tile), lambda j, m: (hop, j))
+    fixed = pl.BlockSpec((rows, width), lambda j, m: (0, 0))
+    first = hop == 0
+    wide = shape((tps * rows, hidden), LOW)
+    *hiddens, two_part, mixed_part = pl.pallas_call(
+        functools.partial(feed_kernel, first, hidden),
+        grid_spec=pltpu.PrefetchScalarGridSpec(
+            num_scalar_prefetch=1,
+            grid=(-(-hidden // tile),),
+            in_specs=[fixed, pl.BlockSpec((rows, width), lambda j, m: (hop, 0)), weight, weight, weight]
+            + ([] if first else [pl.BlockSpec(memory_space=pl.ANY)] * 3),
+            out_specs=[column, column, column, fixed, fixed],
+            scratch_shapes=[pltpu.VMEM((rows, width), jnp.float32)] * 2,
+        ),
+        out_shape=[wide, wide, wide, shape((rows, width), LOW), shape((rows, width), LOW)],
+        input_output_aliases={} if first else {6: 0, 7: 1, 8: 2},
+        compiler_params=pltpu.CompilerParams(vmem_limit_bytes=56 * MIB),
+        cost_estimate=pl.CostEstimate(
+            flops=12 * rows * width * hidden, bytes_accessed=6 * width * hidden, transcendentals=rows * hidden
+        ),
+        name="feed",
+    )(meta, normed, cots, gate, up, down, *(() if first else kept))
+    return hiddens, two_part, mixed_part
+
+
+def assemble_kernel(tiles, meta, own_ref, near_ref, far_ref, o_own_ref, o_near_ref, o_far_ref, out_ref):
+    size = own_ref.shape[1]
+    is_near = (pl.program_id(0) // tiles) == meta[CTX]
+    out_ref[:, pl.ds(shard_at(meta, 0, size), size)] = own_ref[...]
+    out_ref[:, pl.ds(shard_at(meta, 1, size), size)] = o_own_ref[...]
+
+    @pl.when(is_near)
+    def _():
+        out_ref[:, pl.ds(shard_at(meta, 2, size), size)] = near_ref[...]
+        out_ref[:, pl.ds(shard_at(meta, 3, size), size)] = o_near_ref[...]
+
+    @pl.when(jnp.logical_not(is_near))
+    def _():
+        out_ref[:, pl.ds(shard_at(meta, 2, size), size)] = far_ref[...]
+        out_ref[:, pl.ds(shard_at(meta, 3, size), size)] = o_far_ref[...]
+
+
+def assemble(meta, own, near, far, other, other_near, other_far):
+    rows, size = own.shape
+    tiles = 2 if rows % 64 == 0 else 1
+    tile = rows // (2 * tiles)
+    every = pl.BlockSpec((tile, size), lambda i, m: (i, 0))
+    half = pl.BlockSpec((tile, size), lambda i, m: (i % tiles, 0))
+    return call(
+        functools.partial(assemble_kernel, tiles),
+        (2 * tiles,),
+        [every, half, half, every, half, half],
+        pl.BlockSpec((tile, 4 * size), lambda i, m: (i, 0)),
+        shape((rows, 4 * size), LOW),
+        cost=pl.CostEstimate(flops=0, bytes_accessed=16 * rows * size, transcendentals=0),
+        name="assemble",
+    )(meta, own, near, far, other, other_near, other_far)
+
+
+def lay_kernel(low_ref, high_ref, out_ref):
+    both = jnp.concatenate([low_ref[...], high_ref[...]], axis=0)
+    out_ref[...] = jnp.transpose(both.astype(jnp.float32))
+
+
+def lay(low, high):
+    rows, cols = low.shape
+    return pl.pallas_call(
+        lay_kernel,
+        in_specs=[pl.BlockSpec(memory_space=pltpu.VMEM)] * 2,
+        out_specs=pl.BlockSpec(memory_space=pltpu.VMEM),
+        out_shape=shape((cols, 2 * rows), jnp.float32),
+        compiler_params=pltpu.CompilerParams(vmem_limit_bytes=48 * MIB),
+        cost_estimate=pl.CostEstimate(flops=0, bytes_accessed=12 * rows * cols, transcendentals=0),
+        name="lay",
+    )(low, high)
+
+
+def spread_kernel(tps, meta, *refs):
+    out_ref = refs[tps]
+    seq_count = out_ref.shape[0]
+    own = refs[0].shape[0] // seq_count
+    for hop in range(tps):
+        device = lax.rem(meta[TP] + tps - hop, tps)
+        for s in range(seq_count):
+            place = device if s % 2 == 0 else tps - 1 - device
+            at = pl.ds(pl.multiple_of(place * own, own), own)
+            out_ref[s, at, :] = refs[hop][s * own : (s + 1) * own, :].astype(out_ref.dtype)
+
+
+def spread_out(meta, blocks, seq_count, kind):
+    tps = len(blocks)
+    rows, width = blocks[0].shape
+    dims = (seq_count, rows // seq_count * tps, width)
+    return call(
+        functools.partial(spread_kernel, tps),
+        (1,),
+        [whole(item) for item in blocks],
+        pl.BlockSpec(dims, lambda *_: (0, 0, 0)),
+        shape(dims, kind),
+        cost=pl.CostEstimate(flops=0, bytes_accessed=8 * rows * tps * width, transcendentals=0),
+        name="spread",
+    )(meta, *blocks)
+
+
 class Links:
     def __init__(self):
         self.tp, self.ctx, self.fsdp = (lax.axis_index(a) for a in ("tp", "ctx", "fsdp"))
@@ -598,19 +747,13 @@
             return value.astype(jnp.float32) + self.to_y(value).astype(jnp.float32)
         return lax.psum(value.astype(jnp.float32), "ctx")
 
-    def reduce_weight(self, term, axis):
-        part = lax.psum_scatter(
-            term.astype(LOW), ("fsdp", "ctx"), scatter_dimension=axis, tiled=True
-        )
-        if self.ctxs == 2:
-            part = lax.optimization_barrier(part)
-            got = self.to_y(part)
-            low = jnp.where(self.ctx == 0, part, got)
-            high = jnp.where(self.ctx == 0, got, part)
-            full = jnp.concatenate([low, high], axis)
-        else:
-            full = lax.all_gather(part, "ctx", axis=axis, tiled=True)
-        return full.astype(jnp.float32)
+    def reduce_weight(self, term):
+        part = lax.psum_scatter(term, ("fsdp", "ctx"), scatter_dimension=0, tiled=True)
+        if self.ctxs != 2:
+            return lax.all_gather(part, "ctx", axis=0, tiled=True).astype(jnp.float32).T
+        part = lax.optimization_barrier(part)
+        got = self.to_y(part)
+        return lay(jnp.where(self.ctx == 0, part, got), jnp.where(self.ctx == 0, got, part))
 
 
 def local(
@@ -658,15 +801,8 @@
         )
 
     meta = jnp.stack(
-        [fsdp, tp, ctx * (block_len // key_block)] + [place(s, tp) for s in seqs]
+        [fsdp, tp, ctx, ctx * (block_len // key_block)] + [place(s, tp) for s in seqs]
     ).astype(jnp.int32)
-
-    down_full = lax.all_gather(down_weight, "fsdp", axis=1, tiled=True)
-    gate_full = lax.all_gather(gate_weight, "fsdp", axis=0, tiled=True)
-    up_full = lax.all_gather(up_weight, "fsdp", axis=0, tiled=True)
-    q_full = lax.all_gather(
-        lax.all_gather(query_weight, "tp", axis=1, tiled=True), "fsdp", axis=0, tiled=True
-    )
 
     lanes = q_cols + kv_cols
     smalls = jnp.concatenate([b.reshape(-1) for b in (query_bias, key_bias, value_bias)])
@@ -674,15 +810,21 @@
         [jnp.pad(row, (0, lanes - row.shape[0])) for row in (attn_gain, mlp_gain, smalls)]
     )
     extra = jnp.pad(extra, ((0, 13), (0, 0)))
-    qkv = links.gather_fsdp(
-        jnp.concatenate(
-            [jnp.concatenate([query_weight, key_weight, value_weight], axis=1), extra], axis=0
+    pack = jnp.concatenate(
+        [jnp.concatenate([query_weight, key_weight, value_weight], axis=1), extra], axis=0
+    )
+    pack_core, pack_across = links.to_core(pack), links.to_x(pack)
+    qkv = pack, pack_core, pack_across, links.to_core(pack_across)
+    oq_blocks = lax.all_gather(jnp.concatenate([output_weight, query_weight], axis=0), "tp", axis=0)
+    if ctxs == 2:
+        up_mine = up_weight.T
+        half = up_mine.shape[0] // 2
+        up_near = links.to_x(
+            after(lax.dynamic_slice_in_dim(up_mine, ctx * half, half, 0), pack_across)
         )
-    )
-    height = shard + 16
-    rows = jnp.stack(
-        [p[shard : shard + 3] for p in (qkv[0], qkv[2][:height], qkv[1], qkv[2][height:])]
-    )
+    else:
+        up_near = pack_across
+    rows = jnp.stack([item[shard : shard + 3] for item in qkv])
     rows = [
         lax.dynamic_index_in_dim(rows, jnp.bitwise_xor(fsdp, j), 0, keepdims=False) for j in range(4)
     ]
@@ -691,9 +833,7 @@
     bias = jnp.concatenate(
         [r[2, : smalls.shape[0]].reshape(-1, head_dim // fsdps) for r in rows], axis=1
     ).reshape(1, lanes).astype(jnp.float32)
-
-    o_wide = jnp.concatenate(links.gather_tp(output_weight), axis=0)
-    o_parts = links.gather_fsdp(o_wide)
+    bias = after(bias, up_near)
 
     cosine, sine = rope_tables(positions.reshape(tokens), head_dim)
     normed_one, query_blocks, kv_own = project(
@@ -712,78 +852,114 @@
         ]
 
     queries = jnp.stack(swap(lambda d: lax.dynamic_index_in_dim(query_blocks, d, 0, keepdims=False)))
+
+    def gather_whole(item):
+        return lax.all_gather(after(item, up_near), "fsdp", axis=1, tiled=True)
+
+    gate_full, down_full = gather_whole(gate_weight.T), gather_whole(down_weight)
+    o_wide = after(oq_blocks, kv_own)[:, :q_cols].reshape(depth, shard)
+    o_across = links.to_x(o_wide)
+    o_core = links.to_core(after(o_wide, queries))
+
+    late_cot = after(cotangent, kv_own)
+    cot_all = jnp.concatenate([block_rows(late_cot, hop) for hop in range(tps)], axis=0)
+    one_all = jnp.concatenate(
+        [block_rows(normed_one.reshape(seq_count, block_len, width), hop) for hop in range(tps)], axis=0
+    )
+
     order = jnp.tile(jnp.arange(own, dtype=jnp.int32), depth // head_dim // kv_heads)[None]
+    order = after(order, (cot_all, one_all))
     sizes = (seq_count, kv_heads, head_dim, tps)
     mixed, lse = attend(meta, queries, kv_before, kv_own, order, key_block, sizes)
+    o_core_across = links.to_core(after(o_across, mixed))
+    o_parts = (o_wide, o_core, o_across, o_core_across)
     hidden, normed_two = merge(meta, mixed, inputs, o_parts, mlp_gamma, tps)
-
-    two_blocks = links.gather_tp(normed_two)
-    acts, gate_grads, up_grads, two_parts, mixed_parts = [], [], [], [], []
-    cots = [block_rows(cotangent, hop) for hop in range(tps)]
+    two_blocks = [normed_two, links.hop_tp(normed_two)]
+    q_wide = jnp.concatenate([oq_blocks[j, q_cols:] for j in range(tps)], axis=1)
+    if ctxs == 2:
+        up_far = links.to_y(after(up_near, normed_two))
+        up_core, up_near_core = (links.to_core(after(item, mixed)) for item in (up_mine, up_near))
+        up_far_core = links.to_core(up_far)
+        up_full = assemble(meta, up_mine, up_near, up_far, up_core, up_near_core, up_far_core)
+    else:
+        up_full = gather_whole(up_weight.T)
+    two_blocks.append(links.hop_tp(after(two_blocks[-1], (gate_full, up_full, down_full))))
+    two_blocks.append(links.hop_tp(two_blocks[-1]))
+    q_full = lax.all_gather(after(q_wide, down_full), "fsdp", axis=0, tiled=True)
+
+    kept, two_parts, mixed_parts, two_total = None, [], [], None
     for hop in range(tps):
-        act_grad = inner_cols(cots[hop], down_full)
-        gate = dot(two_blocks[hop], gate_full)
-        up_part = dot(two_blocks[hop], up_full)
-        sigma = jax.nn.sigmoid(gate)
-        act = (gate * sigma * up_part).astype(LOW)
-        gate_grad = (act_grad * up_part * (sigma * (1.0 + gate * (1.0 - sigma)))).astype(LOW)
-        up_grad = (act_grad * (gate * sigma)).astype(LOW)
-        two_parts.append((inner_cols(gate_grad, gate_full) + inner_cols(up_grad, up_full)).astype(LOW))
-        mixed_parts.append(dot(act, down_full).astype(LOW))
-        acts.append(act)
-        gate_grads.append(gate_grad)
-        up_grads.append(up_grad)
-    two_own, two_got = links.scatter_tp(two_parts)
-
-    act_all, cot_all, two_all, gate_all, up_all = (
-        jnp.concatenate(item, axis=0) for item in (acts, cots, two_blocks, gate_grads, up_grads)
-    )
-    down_weight_grad = links.reduce_weight(inner_rows(act_all, cot_all), 1)
-    gate_weight_grad = links.reduce_weight(inner_rows(two_all, gate_all), 0)
-    up_weight_grad = links.reduce_weight(inner_rows(two_all, up_all), 0)
-
-    def spread(block):
-        blocks = links.gather_tp(lax.optimization_barrier(block.astype(LOW)))
-        full = jnp.zeros((seq_count, block_len, width), LOW)
-        for hop, item in enumerate(blocks):
-            for s in seqs:
-                full = lax.dynamic_update_slice(
-                    full, item[None, s * own : (s + 1) * own], (s, place(s, links.at(hop)) * own, 0)
-                )
-        return full
+        block = two_blocks[hop]
+        if hop + 1 < tps:
+            block = after(block, two_blocks[hop + 1])
+        if two_total is not None:
+            block = after(block, two_total)
+        kept, two_part, mixed_part = feed(
+            meta, block, cot_all, gate_full, up_full, down_full, hop, tps, kept
+        )
+        two_parts.append(two_part)
+        mixed_parts.append(mixed_part)
+        if hop >= 1:
+            two_total = two_part if hop == 1 else add_low(two_part, two_got)
+            two_got = links.hop_tp(two_total)
+        two_total = two_total if hop >= 2 else None
+    two_own = two_parts[0]
+    act_all, gate_all, up_all = kept
+    two_all = jnp.concatenate(two_blocks, axis=0)
+    down_term = inner_rows(cot_all, after(act_all, two_total)).astype(LOW)
+    down_weight_grad = links.reduce_weight(down_term)
+    two_got = after(two_got, down_term)
 
     hidden_grad, branch_grad, attended_grad, mlp_term = turn(
         meta, two_own, two_got, hidden, cotangent, o_parts, mlp_gamma, depth, tps
     )
-    q_grad, kv_grad_before, kv_grad_own = attend_back(
-        meta, queries, kv_before, kv_own, order, mixed, attended_grad, lse, cosine, sine, key_block, sizes
-    )
-    kv_shape = (2, kv_heads, seq_count, block_len, head_dim)
-    if ctxs == 2:
-        kv_part = add_low(
-            kv_grad_own, lax.ppermute(kv_grad_before, "ctx", [(1, 0)])
-        ).reshape(kv_shape)
-    else:
-        wide_grad = kv_grad_before.reshape(2, kv_heads, seq_count, ctxs * block_len, head_dim)
-        wide_grad = lax.dynamic_update_slice_in_dim(
-            wide_grad, kv_grad_own.reshape(kv_shape), ctx * block_len, 3
+    mixed_got = links.hop_tp(after(mixed_parts[1], two_got))
+    q_grads, kv_parts, token = [], [], two_got
+    for s in seqs:
+        q_grad, grad_before, grad_own = attend_back(
+            meta, s, queries, kv_before, kv_own, order, mixed, attended_grad, after(lse, token),
+            cosine, sine, key_block, sizes,
         )
-        kv_part = lax.psum_scatter(wide_grad, "ctx", scatter_dimension=3, tiled=True)
+        q_grads.append(q_grad)
+        if ctxs == 2:
+            kv_parts.append((grad_own, lax.ppermute(grad_before, "ctx", [(1, 0)])))
+        else:
+            wide_grad = lax.dynamic_update_slice_in_dim(grad_before, grad_own, ctx * block_len, 2)
+            kv_parts.append((lax.psum_scatter(wide_grad, "ctx", scatter_dimension=2, tiled=True), None))
+        token = (mixed_got, q_grad)
+    mixed_got = links.hop_tp(add_low(mixed_parts[2], after(mixed_got, q_grads[0])))
+    q_grad = jnp.concatenate(q_grads, axis=0)
+    kv_parts = [
+        mine if got is None else add_low(after(mine, mixed_got), got) for mine, got in kv_parts
+    ]
+    gate_term = inner_rows(two_all, after(gate_all, kv_parts)).astype(LOW)
+    mixed_got = links.hop_tp(add_low(mixed_parts[3], mixed_got))
 
     def kv_rows(hop):
-        return jnp.concatenate(
+        return jnp.stack(
             [
-                lax.dynamic_slice_in_dim(kv_part[:, :, s : s + 1], place(s, links.at(hop)) * own, own, 3)
+                lax.dynamic_slice_in_dim(kv_parts[s], place(s, links.at(hop)) * own, own, 2)
                 for s in seqs
             ],
             axis=2,
         )
 
-    kv_mine, kv_got = links.scatter_tp([kv_rows(hop) for hop in range(tps)])
+    kv_mine = kv_rows(0)
+    kv_got = links.hop_tp(kv_rows(1))
+    kv_got = links.hop_tp(add_low(kv_rows(2), after(kv_got, (gate_term, mixed_got))))
+    up_term = inner_rows(two_all, after(up_all, (gate_term, kv_parts))).astype(LOW)
+    gate_weight_grad = links.reduce_weight(after(gate_term, kv_got)).T
+    kv_got = links.hop_tp(add_low(kv_rows(3), after(kv_got, up_term)))
+    up_weight_grad = links.reduce_weight(after(up_term, kv_got)).T
+    out_low = hidden + mixed_parts[0].astype(jnp.float32) + mixed_got.astype(jnp.float32)
+    out_low = lax.optimization_barrier(out_low.astype(LOW))
+    out_blocks = [out_low, links.hop_tp(out_low)]
+    output_part = links.scatter_fsdp(inner_rows(mixed, after(branch_grad, up_term)).astype(LOW), 1)
     input_low, kv_grad, attn_term = finish(
-        meta, q_grad, kv_mine, kv_got, cosine, sine, q_full, qkv, inputs, hidden_grad, attn_gamma, tps
-    )
-    input_grad = spread(input_low).astype(jnp.float32)
+        meta, after(q_grad, down_weight_grad), kv_mine, kv_got, cosine, sine, q_full, qkv, inputs, hidden_grad, attn_gamma, tps
+    )
+    input_low = lax.optimization_barrier(input_low)
+    in_blocks = [input_low, links.hop_tp(input_low)]
 
     kv_each = kv_cols // tps
     attn_sum = jnp.sum(attn_term, axis=0)
@@ -806,13 +982,22 @@
     shares = swap(share)
     own_tokens = seq_count * own
     grads_all = jnp.concatenate([item[:own_tokens] for item in shares], axis=0)
-    one_all = jnp.concatenate(
-        [block_rows(normed_one.reshape(seq_count, block_len, width), hop) for hop in range(tps)], axis=0
-    )
     gain_rows = sum(item[own_tokens : own_tokens + 2].astype(jnp.float32) for item in shares)
     bias_row = jnp.sum(grads_all.astype(jnp.float32), axis=0, keepdims=True)
     below = jnp.pad(jnp.concatenate([gain_rows, bias_row], axis=0), ((0, 13), (0, 0))).astype(LOW)
     term = inner_rows(one_all, grads_all).astype(LOW)
+    in_blocks.append(links.hop_tp(after(in_blocks[-1], (term, out_blocks[1], gate_weight_grad))))
+    out_blocks.append(links.hop_tp(after(out_blocks[-1], in_blocks[1])))
+
+    def output_rows(hop):
+        return lax.dynamic_slice_in_dim(output_part, links.at(hop) * q_cols, q_cols, 0)
+
+    output_got = links.hop_tp(after(output_rows(1), in_blocks[1]))
+    in_blocks.append(
+        links.hop_tp(after(in_blocks[-1], (out_blocks[2], output_got, up_weight_grad)))
+    )
+    out_blocks.append(links.hop_tp(after(out_blocks[-1], in_blocks[2])))
+    output_got = links.hop_tp(add_low(output_rows(2), after(output_got, in_blocks[2])))
     term = jnp.concatenate(
         [item for j in range(fsdps) for item in (term[j * shard : (j + 1) * shard], below)], axis=0
     )
@@ -826,8 +1011,15 @@
     kv_low = jnp.concatenate(
         [total[:shard, q_cols:], below[:, :q_cols].reshape(-1, kv_each), below[:, q_cols:]], axis=0
     ).astype(LOW)
-    kv_low = lax.optimization_barrier(kv_low)
-    all_low = jnp.stack(links.gather_tp(kv_low))
+    kv_low = lax.optimization_barrier(after(kv_low, in_blocks[2]))
+    kv_blocks = links.gather_tp(kv_low)
+    output_got = links.hop_tp(add_low(output_rows(3), output_got))
+    output_weight_grad = links.sum_ctx(add_low(output_rows(0), output_got))
+    out_blocks[0] = after(out_blocks[0], (kv_blocks[-1], output_weight_grad, up_weight_grad))
+    outputs = spread_out(meta, out_blocks, seq_count, LOW)
+    in_blocks[0] = after(in_blocks[0], outputs)
+    input_grad = spread_out(meta, in_blocks, seq_count, jnp.float32)
+    all_low = jnp.stack(kv_blocks)
     by_device = [
         lax.dynamic_index_in_dim(all_low, links.at(j), 0, keepdims=False) for j in range(tps)
     ]
@@ -837,18 +1029,6 @@
     kv_bias = jnp.stack([item[-14] for item in by_device]).reshape(2, kv_heads, head_dim)
     kv_bias = lax.dynamic_slice_in_dim(kv_bias, fsdp * part, part, 2).astype(jnp.float32)
     half = kv_cols // 2
-
-    output_part = links.scatter_fsdp(inner_rows(mixed, branch_grad).astype(LOW), 1)
-    output_mine, output_got = links.scatter_tp(
-        [
-            lax.dynamic_slice_in_dim(output_part, links.at(hop) * q_cols, q_cols, 0)
-            for hop in range(tps)
-        ]
-    )
-    output_weight_grad = links.sum_ctx(add_low(output_mine, output_got))
-
-    mixed_mine, mixed_got = links.scatter_tp(mixed_parts)
-    outputs = spread(hidden + mixed_mine.astype(jnp.float32) + mixed_got.astype(jnp.float32))
 
     return (
         outputs,

time: 929 us -> 820 us (0.88)
  Pallas kernels: 64 us -> 202 us
  matrix products: 196 us -> 58.3 us
  starting transfers between devices: 93.6 us -> 51.1 us
  local copies, waits for them, and re-layouts: 105 us -> 64.7 us
  waiting for transfers between devices: 409 us -> 372 us
    dot_general x24 -> x0, matrix products: 144 us -> none  [the longest x12 84 us: dot(): return jnp.dot(left, right, preferred_element_type=jnp.float32)]
    pallas_call x1 -> x12, Pallas kernels: 15.2 us -> 154 us  [the longest x4 114 us: feed(): pl.pallas_call(functools.partial(feed_kernel, first, hidden), grid_spec=p...]
    ppermute x33 -> x30, waiting for transfers between devices: 315 us -> 222 us  [hop_tp(): lax.ppermute(value, 'tp', [(i, (i + hop) % self.tps) for i in range(self....]
    ppermute x5 -> x6, starting transfers between devices: 52.2 us -> 6.88 us  [to_y(): return lax.ppermute(value, 'ctx', [(0, 1), (1, 0)])]
    ppermute x5 -> x6, waiting for transfers between devices: 21.4 us -> 62.7 us  [to_y(): return lax.ppermute(value, 'ctx', [(0, 1), (1, 0)])]
    dynamic_update_slice x16 -> x0, local copies, waits for them, and re-layouts: 24.7 us -> none  [spread(): lax.dynamic_update_slice(full, item[None, s * own:(s + 1) * own], (s, pla...]
    unnamed x250 -> x176, local copies, waits for them, and re-layouts: 52.9 us -> 28.8 us
    convert_element_type x4 -> x1, other arithmetic: 13.6 us -> 2.15 us  [local(): out_low = lax.optimization_barrier(out_low.astype(LOW))]
  transfers between devices with their start and end apart: 56 -> 60, of which waited for: 33 -> 30; matrix products, arithmetic and copies ran while one was open for 34% -> 16% of each run, Pallas kernels for 7% -> 24%
where the time goes in v2:
time: 820 us; the launch traced here: 810 us
  waiting for transfers between devices  372 us (45%)
  Pallas kernels  202 us (25%)
  local copies, waits for them, and re-layouts  64.7 us (8%)
  matrix products  58.3 us (7%)
  starting transfers between devices  51.1 us (6%)
  other arithmetic  46 us (6%)
  between operations  15.9 us (2%)
    ppermute x30, waiting for transfers between devices, hop_tp(): lax.ppermute(value, 'tp', [(i, (i + hop) % self.tps) for i in range(self....  222 us
    pallas_call x4, Pallas kernels, feed(): pl.pallas_call(functools.partial(feed_kernel, first, hidden), grid_spec=p...  114 us
    ppermute x6, waiting for transfers between devices, to_y(): return lax.ppermute(value, 'ctx', [(0, 1), (1, 0)])  62.7 us
    dot_general x5, matrix products, inner_rows(): lax.dot_general(left, right, (((0,), (0,)), ((), ())), preferred_element_...  58.3 us
    ppermute x5, waiting for transfers between devices, to_x(): return lax.ppermute(value, 'fsdp', [(0, 2), (2, 0), (1, 3), (3, 1)])  48.3 us
    unnamed x176, local copies, waits for them, and re-layouts  28.8 us
    ppermute x30, starting transfers between devices, hop_tp(): lax.ppermute(value, 'tp', [(i, (i + hop) % self.tps) for i in range(self....  26.8 us
    ppermute x2, waiting for transfers between devices, local(): kv_parts.append((grad_own, lax.ppermute(grad_before, 'ctx', [(1, 0)])))  25 us
  transfers between devices with their start and end apart: 60, of which 30 were waited for; matrix products, arithmetic and copies ran while one was open for 16% of the time, Pallas kernels for 24%

profile of v2, /device:TPU:0, one launch (start us, length us, event | category | flops | bytes accessed | tf_op | source)
XLA Modules:
  0.0 810.0 jit_solution(465127662528175206)
XLA Ops:
  17.5 16.0 %collective-permute-done.1.refs_2_ = bf16[400,896]{1,0:T(8,128)(2,1)S(1)} collective-permute-done((bf16[400,896]{1,0:T(8,128)(2,1)S(1)}, bf16[400,896]{1,0:T(8,128)(2,1)S(1)}, u32[]{:S(2)}, u32[]{:S(2)}) %collective-permute-start.1) | collective-permute-done | bytes 716832 | tf_op jit(solution)/shard_map/ppermute | solution.py:698
  35.2 18.8 %collective-permute-done.3.near_ref = bf16[1120,384]{1,0:T(8,128)(2,1)} collective-permute-done((bf16[1120,384]{1,0:T(8,128)(2,1)S(1)}, bf16[1120,384]{1,0:T(8,128)(2,1)}, u32[]{:S(2)}, u32[]{:S(2)}) %collective-permute-start.3) | collective-permute-done | bytes 860192 | tf_op jit(solution)/shard_map/ppermute | solution.py:698
  66.3 13.3 %project.1 = (bf16[1536,1536]{1,0:T(8,128)(2,1)}, bf16[4,384,384]{2,1,0:T(8,128)(2,1)S(1)}, bf16[1536,512]{1,0:T(8,128)(2,1)}) custom-call(s32[6]{0:T(128)S(1)} %stack.118.meta.refs_0_, bf16[2,768,1536]{2,1,0:T(8,128)(2,1)} %refs_4_.1, f32[1,1536]{1,0:T(1,128)S(1)} %maximum_convert_fusion.1.gain_ref.refs_6_, f32[1,896]{1,0:T(1,128)S(1)} %bitcast.129, ...), custom_call_target="tpu_custom_call" | custom-call | flops 4227858432 | bytes 18874368 | tf_op jit(solution)/shard_map/project/pallas_call | solution.py:131
  110.7 11.3 %collective-permute-done.7.refs_2_.refs_3_ = bf16[1536,512]{1,0:T(8,128)(2,1)} collective-permute-done((bf16[1536,512]{1,0:T(8,128)(2,1)}, bf16[1536,512]{1,0:T(8,128)(2,1)}, u32[]{:S(2)}, u32[]{:S(2)}) %collective-permute-start.7) | collective-permute-done | bytes 1572896 | tf_op jit(solution)/shard_map/ppermute | solution.py:843
  157.0 16.7 %collective-permute-done.12.far_ref = bf16[1120,384]{1,0:T(8,128)(2,1)S(1)} collective-permute-done((bf16[1120,384]{1,0:T(8,128)(2,1)}, bf16[1120,384]{1,0:T(8,128)(2,1)S(1)}, u32[]{:S(2)}, u32[]{:S(2)}) %collective-permute-start.12) | collective-permute-done | bytes 860192 | tf_op jit(solution)/shard_map/ppermute | solution.py:701
  191.9 25.8 %feed.4 = (bf16[1536,2240]{1,0:T(8,128)(2,1)}, bf16[1536,2240]{1,0:T(8,128)(2,1)}, bf16[1536,2240]{1,0:T(8,128)(2,1)}, bf16[384,1536]{1,0:T(8,128)(2,1)}, bf16[384,1536]{1,0:T(8,128)(2,1)}) custom-call(s32[6]{0:T(128)} %copy-done.30, bf16[384,1536]{1,0:T(8,128)(2,1)} %copy-done.15, bf16[1536,1536]{1,0:T(8,128)(2,1)} %bitcast_dynamic-update-slice_fusion.refs_2_, ...), custom_call_target="tpu_custom_call" | custom-call | flops 15854469120 | bytes 20643840 | tf_op jit(solution)/shard_map/feed/pallas_call | solution.py:587
  219.4 35.4 %feed.5 = (bf16[1536,2240]{1,0:T(8,128)(2,1)}, bf16[1536,2240]{1,0:T(8,128)(2,1)}, bf16[1536,2240]{1,0:T(8,128)(2,1)}, bf16[384,1536]{1,0:T(8,128)(2,1)}, bf16[384,1536]{1,0:T(8,128)(2,1)}) custom-call(s32[6]{0:T(128)} %copy-done.30, bf16[384,1536]{1,0:T(8,128)(2,1)} %copy-done.58, ...), custom_call_target="tpu_custom_call", output_to_operand_aliasing={{0}: (6, {}), {1}: (7, {}), {2}: (8, {})} | custom-call | flops 15854469120 | bytes 20643840 | tf_op jit(solution)/shard_map/feed/pallas_call | solution.py:587
  254.9 25.9 %feed.6 = (bf16[1536,2240]{1,0:T(8,128)(2,1)}, bf16[1536,2240]{1,0:T(8,128)(2,1)}, bf16[1536,2240]{1,0:T(8,128)(2,1)}, bf16[384,1536]{1,0:T(8,128)(2,1)}, bf16[384,1536]{1,0:T(8,128)(2,1)}) custom-call(s32[6]{0:T(128)} %copy-done.30, bf16[384,1536]{1,0:T(8,128)(2,1)} %copy-done.56, ...), custom_call_target="tpu_custom_call", output_to_operand_aliasing={{0}: (6, {}), {1}: (7, {}), {2}: (8, {})} | custom-call | flops 15854469120 | bytes 20643840 | tf_op jit(solution)/shard_map/feed/pallas_call | solution.py:587
  284.6 26.7 %feed.7 = (bf16[1536,2240]{1,0:T(8,128)(2,1)}, bf16[1536,2240]{1,0:T(8,128)(2,1)}, bf16[1536,2240]{1,0:T(8,128)(2,1)}, bf16[384,1536]{1,0:T(8,128)(2,1)}, bf16[384,1536]{1,0:T(8,128)(2,1)}) custom-call(s32[6]{0:T(128)} %copy-done.30, bf16[384,1536]{1,0:T(8,128)(2,1)} %copy-done.54, ...), custom_call_target="tpu_custom_call", output_to_operand_aliasing={{0}: (6, {}), {1}: (7, {}), {2}: (8, {})} | custom-call | flops 15854469120 | bytes 20643840 | tf_op jit(solution)/shard_map/feed/pallas_call | solution.py:587
  313.9 16.1 %convolution_convert_fusion.2 = bf16[1536,2240]{1,0:T(8,128)(2,1)} fusion(bf16[1536,1536]{1,0:T(8,128)(2,1)S(1)} %bitcast.144, bf16[1536,2240]{1,0:T(8,128)(2,1)} %get-tuple-element.137), kind=kOutput, calls=%fused_computation.2 | convolution fusion | flops 10573086720 | bytes 18481152 | tf_op jit(solution)/shard_map/dot_general | solution.py:35
  335.4 22.5 %collective-permute-done.20.b_ref = bf16[384,1536]{1,0:T(8,128)(2,1)S(1)} collective-permute-done((bf16[384,1536]{1,0:T(8,128)(2,1)}, bf16[384,1536]{1,0:T(8,128)(2,1)S(1)}, u32[]{:S(2)}, u32[]{:S(2)}) %collective-permute-start.20) | collective-permute-done | bytes 1179680 | tf_op jit(solution)/shard_map/ppermute | solution.py:704
  401.1 11.0 %collective-permute-done.22 = bf16[384,1536]{1,0:T(8,128)(2,1)S(1)} collective-permute-done((bf16[384,1536]{1,0:T(8,128)(2,1)S(1)}, bf16[384,1536]{1,0:T(8,128)(2,1)S(1)}, u32[]{:S(2)}, u32[]{:S(2)}) %collective-permute-start.22) | collective-permute-done | bytes 1179680 | tf_op jit(solution)/shard_map/ppermute | solution.py:704
  413.4 13.8 %collective-permute-done.26 = bf16[2,2,768,128]{3,2,1,0:T(8,128)(2,1)S(1)} collective-permute-done((bf16[2,2,768,128]{3,2,1,0:T(8,128)(2,1)S(1)}, bf16[2,2,768,128]{3,2,1,0:T(8,128)(2,1)S(1)}, u32[]{:S(2)}, u32[]{:S(2)}) %collective-permute-start.26) | collective-permute-done | bytes 786464 | tf_op jit(solution)/shard_map/ppermute | solution.py:925
  428.1 11.2 %collective-permute-done.25 = bf16[2,2,768,128]{3,2,1,0:T(8,128)(2,1)S(1)} collective-permute-done((bf16[2,2,768,128]{3,2,1,0:T(8,128)(2,1)S(1)}, bf16[2,2,768,128]{3,2,1,0:T(8,128)(2,1)S(1)}, u32[]{:S(2)}, u32[]{:S(2)}) %collective-permute-start.25) | collective-permute-done | bytes 786464 | tf_op jit(solution)/shard_map/ppermute | solution.py:925
  445.0 15.4 %convolution_convert_fusion.1 = bf16[1536,2240]{1,0:T(8,128)(2,1)} fusion(bf16[1536,1536]{1,0:T(8,128)(2,1)} %constant_dynamic-update-slice_fusion.2, bf16[1536,2240]{1,0:T(8,128)(2,1)S(1)} %bitcast.148), kind=kOutput, calls=%fused_computation.1 | convolution fusion | flops 10573086720 | bytes 18481152 | tf_op jit(solution)/shard_map/dot_general | solution.py:35
  472.4 17.5 %convolution_convert_fusion = bf16[1536,2240]{1,0:T(8,128)(2,1)} fusion(bf16[1536,1536]{1,0:T(8,128)(2,1)} %constant_dynamic-update-slice_fusion.2, bf16[1536,2240]{1,0:T(8,128)(2,1)} %get-tuple-element.159), kind=kOutput, calls=%fused_computation | convolution fusion | flops 10573086720 | bytes 18481152 | tf_op jit(solution)/shard_map/dot_general | solution.py:35
  509.3 24.1 %collective-permute-done.24 = bf16[192,2240]{1,0:T(8,128)(2,1)S(1)} collective-permute-done((bf16[192,2240]{1,0:T(8,128)(2,1)}, bf16[192,2240]{1,0:T(8,128)(2,1)S(1)}, u32[]{:S(2)}, u32[]{:S(2)}) %collective-permute-start.24) | collective-permute-done | bytes 860192 | tf_op jit(solution)/shard_map/ppermute | solution.py:701
  538.0 10.1 %finish.1 = (bf16[384,1536]{1,0:T(8,128)(2,1)}, bf16[384,512]{1,0:T(8,128)(2,1)S(1)}, f32[2,1,1536]{2,1,0:T(1,128)S(1)}) custom-call(s32[6]{0:T(128)S(1)} %copy-done.31, bf16[384,1536]{1,0:T(8,128)(2,1)} %constant_dynamic-update-slice_fusion.g_ref, bf16[2,2,2,192,128]{4,3,2,1,0:T(8,128)(2,1)S(1)} %pad_maximum_fusion.11.a_ref, ...), custom_call_target="tpu_custom_call" | custom-call | flops 2415919104 | bytes 8388608 | tf_op jit(solution)/shard_map/finish/pallas_call | solution.py:509
  562.4 21.5 %collective-permute-done.31 = bf16[400,512]{1,0:T(8,128)(2,1)S(1)} collective-permute-done((bf16[400,512]{1,0:T(8,128)(2,1)S(1)}, bf16[400,512]{1,0:T(8,128)(2,1)S(1)}, u32[]{:S(2)}, u32[]{:S(2)}) %collective-permute-start.31) | collective-permute-done | bytes 409632 | tf_op jit(solution)/shard_map/ppermute | solution.py:704
  615.2 16.1 %collective-permute-done.38 = bf16[192,2240]{1,0:T(8,128)(2,1)} collective-permute-done((bf16[192,2240]{1,0:T(8,128)(2,1)}, bf16[192,2240]{1,0:T(8,128)(2,1)}, u32[]{:S(2)}, u32[]{:S(2)}) %collective-permute-start.38) | collective-permute-done | bytes 860192 | tf_op jit(solution)/shard_map/ppermute | solution.py:701
  635.2 14.1 %collective-permute-done.36.refs_1_ = bf16[384,1536]{1,0:T(8,128)(2,1)} collective-permute-done((bf16[384,1536]{1,0:T(8,128)(2,1)S(1)}, bf16[384,1536]{1,0:T(8,128)(2,1)}, u32[]{:S(2)}, u32[]{:S(2)}) %collective-permute-start.36) | collective-permute-done | bytes 1179680 | tf_op jit(solution)/shard_map/ppermute | solution.py:704
  661.3 19.2 %collective-permute-done.39.refs_2_ = bf16[384,1536]{1,0:T(8,128)(2,1)} collective-permute-done((bf16[384,1536]{1,0:T(8,128)(2,1)}, bf16[384,1536]{1,0:T(8,128)(2,1)}, u32[]{:S(2)}, u32[]{:S(2)}) %collective-permute-start.39) | collective-permute-done | bytes 1179680 | tf_op jit(solution)/shard_map/ppermute | solution.py:704
  687.9 26.4 %collective-permute-done.40 = bf16[448,128]{1,0:T(8,128)(2,1)S(1)} collective-permute-done((bf16[448,128]{1,0:T(8,128)(2,1)S(1)}, bf16[448,128]{1,0:T(8,128)(2,1)S(1)}, u32[]{:S(2)}, u32[]{:S(2)}) %collective-permute-start.40) | collective-permute-done | bytes 114720 | tf_op jit(solution)/shard_map/ppermute | solution.py:704
  723.7 53.0 %collective-permute-done.42 = bf16[448,128]{1,0:T(8,128)(2,1)S(1)} collective-permute-done((bf16[448,128]{1,0:T(8,128)(2,1)S(1)}, bf16[448,128]{1,0:T(8,128)(2,1)S(1)}, u32[]{:S(2)}, u32[]{:S(2)}) %collective-permute-start.42) | collective-permute-done | bytes 114720 | tf_op jit(solution)/shard_map/ppermute | solution.py:704
  (434 shorter events, 312.4 us)
Async XLA Ops:
  7.2 94.8 %all-gather.12.cloned.1.call-start = ((), (), s32[]{:S(2)}) async-start(), calls=%async_computation.9 | async-start | bytes 2949120 | tf_op jit(solution)/shard_map/all_gather | solution.py:818
  9.3 181.5 %all-gather.6.cloned.1.call-start = ((), (), s32[]{:S(2)}) async-start(), calls=%async_computation.3 | async-start | bytes 8601600 | tf_op jit(solution)/shard_map/all_gather | solution.py:857
  54.0 136.8 %all-gather.8.cloned.1.call-start = ((), (), s32[]{:S(2)}) async-start(), calls=%async_computation.4 | async-start | bytes 8601600 | tf_op jit(solution)/shard_map/all_gather | solution.py:857
  63.9 437.7 %reduce-scatter.4.cloned.1.call-start = ((), (), s32[]{:S(2)}) async-start(), calls=%async_computation.5 | async-start | bytes 7962624 | tf_op jit(solution)/shard_map/reduce_scatter | solution.py:751
  85.0 37.0 %collective-permute-start.7 = (bf16[1536,512]{1,0:T(8,128)(2,1)}, bf16[1536,512]{1,0:T(8,128)(2,1)}, u32[]{:S(2)}, u32[]{:S(2)}) collective-permute-start(bf16[1536,512]{1,0:T(8,128)(2,1)} %get-tuple-element.100.refs_4_.refs_5_), channel_id=1, source_target_pairs={{0,4},{1,5},{2,6},{3,7},{8,12},{9,13},{10,14},{11,15},{16,20},{17,... | collective-permute-start | bytes 4718600 | tf_op jit(solution)/shard_map/ppermute | solution.py:843
  103.4 35.4 %collective-permute-start.9 = (bf16[1536,384]{1,0:T(8,128)(2,1)S(1)}, bf16[1536,384]{1,0:T(8,128)(2,1)S(1)}, u32[]{:S(2)}, u32[]{:S(2)}) collective-permute-start(bf16[1536,384]{1,0:T(8,128)(2,1)S(1)} %bitcast.123), channel_id=1, source_target_pairs={{0,16},{16,0},{8,24},{24,8},{1,17},{17,1},{9,25},{25,9},{2,18},{18... | collective-permute-start | bytes 3538952 | tf_op jit(solution)/shard_map/ppermute | solution.py:698
  138.9 44.7 %collective-permute-start.13 = (bf16[2240,384]{1,0:T(8,128)(2,1)S(1)}, bf16[2240,384]{1,0:T(8,128)(2,1)S(1)}, u32[]{:S(2)}, u32[]{:S(2)}) collective-permute-start(bf16[2240,384]{1,0:T(8,128)(2,1)S(1)} %bitcast.127), channel_id=1, source_target_pairs={{0,8},{8,0},{16,24},{24,16},{1,9},{9,1},{17,25},{25,17},{2,10},{10... | collective-permute-start | bytes 5160968 | tf_op jit(solution)/shard_map/ppermute | solution.py:695
  219.4 35.4 %collective-permute-start.17 = (bf16[384,1536]{1,0:T(8,128)(2,1)S(1)}, bf16[384,1536]{1,0:T(8,128)(2,1)S(1)}, u32[]{:S(2)}, u32[]{:S(2)}) collective-permute-start(bf16[384,1536]{1,0:T(8,128)(2,1)S(1)} %collective-permute-done.16.refs_1_), channel_id=1, source_target_pairs={{0,1},{1,2},{2,3},{3,0},{4,5},{5,6},{6,7},{7,4},{8,9},{9,10},{10,1... | collective-permute-start | bytes 3538952 | tf_op jit(solution)/shard_map/ppermute | solution.py:704
  330.0 205.8 %all-gather.10.cloned.1.call-start = ((), (), s32[]{:S(2)}) async-start(), calls=%async_computation.6 | async-start | bytes 5898240 | tf_op jit(solution)/shard_map/all_gather | solution.py:888
  360.7 238.3 %reduce-scatter.6.cloned.1.call-start = ((), (), s32[]{:S(2)}) async-start(), calls=%async_computation.7 | async-start | bytes 7962624 | tf_op jit(solution)/shard_map/reduce_scatter | solution.py:751
  399.6 39.7 %collective-permute-start.25 = (bf16[2,2,768,128]{3,2,1,0:T(8,128)(2,1)S(1)}, bf16[2,2,768,128]{3,2,1,0:T(8,128)(2,1)S(1)}, u32[]{:S(2)}, u32[]{:S(2)}) collective-permute-start(bf16[2,2,768,128]{3,2,1,0:T(8,128)(2,1)S(1)} %get-tuple-element.151), channel_id=1, source_target_pairs={{4,0},{5,1},{6,2},{7,3},{12,8},{13,9},{14,10},{15,11},{20,16},{21,... | collective-permute-start | bytes 2359304 | tf_op jit(solution)/shard_map/ppermute | solution.py:925
  413.4 47.0 %collective-permute-start.23 = (bf16[384,1536]{1,0:T(8,128)(2,1)}, bf16[384,1536]{1,0:T(8,128)(2,1)}, u32[]{:S(2)}, u32[]{:S(2)}) collective-permute-start(bf16[384,1536]{1,0:T(8,128)(2,1)} %add_convert_fusion.3), channel_id=1, source_target_pairs={{0,1},{1,2},{2,3},{3,0},{4,5},{5,6},{6,7},{7,4},{8,9},{9,10},{10,1... | collective-permute-start | bytes 3538952 | tf_op jit(solution)/shard_map/ppermute | solution.py:704
  471.3 179.8 %reduce-scatter.8.cloned.1.call-start = ((), (), s32[]{:S(2)}) async-start(), calls=%async_computation.8 | async-start | bytes 7962624 | tf_op jit(solution)/shard_map/reduce_scatter | solution.py:751
  509.2 90.4 %collective-permute-start.43 = (bf16[1536,768]{0,1:T(8,128)(2,1)}, bf16[1536,768]{0,1:T(8,128)(2,1)}, u32[]{:S(2)}, u32[]{:S(2)}) collective-permute-start(bf16[1536,768]{0,1:T(8,128)(2,1)} %pad_maximum_fusion), channel_id=1, source_target_pairs={{0,8},{8,0},{16,24},{24,16},{1,9},{9,1},{17,25},{25,17},{2,10},{10... | collective-permute-start | bytes 7077896 | tf_op jit(solution)/shard_map/ppermute | solution.py:695
  593.6 41.5 %collective-permute-start.37 = (bf16[384,1536]{1,0:T(8,128)(2,1)S(1)}, bf16[384,1536]{1,0:T(8,128)(2,1)S(1)}, u32[]{:S(2)}, u32[]{:S(2)}) collective-permute-start(bf16[384,1536]{1,0:T(8,128)(2,1)S(1)} %add_convert_fusion.2.refs_0_), channel_id=1, source_target_pairs={{0,1},{1,2},{2,3},{3,0},{4,5},{5,6},{6,7},{7,4},{8,9},{9,10},{10,1... | collective-permute-start | bytes 3538952 | tf_op jit(solution)/shard_map/ppermute | solution.py:704
  602.7 46.5 %collective-permute-start.36 = (bf16[384,1536]{1,0:T(8,128)(2,1)S(1)}, bf16[384,1536]{1,0:T(8,128)(2,1)}, u32[]{:S(2)}, u32[]{:S(2)}) collective-permute-start(bf16[384,1536]{1,0:T(8,128)(2,1)S(1)} %copy-done.17), channel_id=1, source_target_pairs={{0,1},{1,2},{2,3},{3,0},{4,5},{5,6},{6,7},{7,4},{8,9},{9,10},{10,1... | collective-permute-start | bytes 3538952 | tf_op jit(solution)/shard_map/ppermute | solution.py:704
  606.3 43.2 %collective-permute-start.44 = (bf16[1536,384]{0,1:T(8,128)(2,1)}, bf16[1536,384]{0,1:T(8,128)(2,1)}, u32[]{:S(2)}, u32[]{:S(2)}) collective-permute-start(bf16[1536,384]{0,1:T(8,128)(2,1)} %constant_dynamic-slice_fusion.8), channel_id=1, source_target_pairs={{0,16},{16,0},{8,24},{24,8},{1,17},{17,1},{9,25},{25,9},{2,18},{18... | collective-permute-start | bytes 3538952 | tf_op jit(solution)/shard_map/ppermute | solution.py:698
  615.2 39.8 %collective-permute-start.35 = (bf16[400,512]{1,0:T(8,128)(2,1)}, bf16[400,512]{1,0:T(8,128)(2,1)}, u32[]{:S(2)}, u32[]{:S(2)}) collective-permute-start(bf16[400,512]{1,0:T(8,128)(2,1)} %add_convert_fusion.10), channel_id=1, source_target_pairs={{0,4},{4,0},{1,5},{5,1},{2,6},{6,2},{3,7},{7,3},{8,12},{12,8},{9,1... | collective-permute-start | bytes 1228808 | tf_op jit(solution)/shard_map/ppermute | solution.py:701
  651.1 63.3 %collective-permute-start.49 = (bf16[192,2240]{1,0:T(8,128)(2,1)}, bf16[192,2240]{1,0:T(8,128)(2,1)}, u32[]{:S(2)}, u32[]{:S(2)}) collective-permute-start(bf16[192,2240]{1,0:T(8,128)(2,1)} %reduce-scatter.8.cloned.1.call-done), channel_id=1, source_target_pairs={{0,4},{4,0},{1,5},{5,1},{2,6},{6,2},{3,7},{7,3},{8,12},{12,8},{9,1... | collective-permute-start | bytes 2580488 | tf_op jit(solution)/shard_map/ppermute | solution.py:701
  654.7 63.6 %collective-permute-start.50 = (bf16[384,1536]{1,0:T(8,128)(2,1)S(1)}, bf16[384,1536]{1,0:T(8,128)(2,1)S(1)}, u32[]{:S(2)}, u32[]{:S(2)}) collective-permute-start(bf16[384,1536]{1,0:T(8,128)(2,1)S(1)} %collective-permute-done.37.refs_1_), channel_id=1, source_target_pairs={{0,1},{1,2},{2,3},{3,0},{4,5},{5,6},{6,7},{7,4},{8,9},{9,10},{10,1... | collective-permute-start | bytes 3538952 | tf_op jit(solution)/shard_map/ppermute | solution.py:704
  718.3 73.2 %collective-permute-start.51 = (bf16[384,1536]{1,0:T(8,128)(2,1)S(1)}, bf16[384,1536]{1,0:T(8,128)(2,1)}, u32[]{:S(2)}, u32[]{:S(2)}) collective-permute-start(bf16[384,1536]{1,0:T(8,128)(2,1)S(1)} %collective-permute-done.50.refs_2_), channel_id=1, source_target_pairs={{0,1},{1,2},{2,3},{3,0},{4,5},{5,6},{6,7},{7,4},{8,9},{9,10},{10,1... | collective-permute-start | bytes 3538952 | tf_op jit(solution)/shard_map/ppermute | solution.py:704
  718.6 77.2 %collective-permute-start.52 = (bf16[384,1536]{1,0:T(8,128)(2,1)}, bf16[384,1536]{1,0:T(8,128)(2,1)}, u32[]{:S(2)}, u32[]{:S(2)}) collective-permute-start(bf16[384,1536]{1,0:T(8,128)(2,1)} %collective-permute-done.39.refs_2_), channel_id=1, source_target_pairs={{0,1},{1,2},{2,3},{3,0},{4,5},{5,6},{6,7},{7,4},{8,9},{9,10},{10,1... | collective-permute-start | bytes 3538952 | tf_op jit(solution)/shard_map/ppermute | solution.py:704
  723.2 53.5 %collective-permute-start.42 = (bf16[448,128]{1,0:T(8,128)(2,1)S(1)}, bf16[448,128]{1,0:T(8,128)(2,1)S(1)}, u32[]{:S(2)}, u32[]{:S(2)}) collective-permute-start(bf16[448,128]{1,0:T(8,128)(2,1)S(1)} %collective-permute-done.41), channel_id=1, source_target_pairs={{0,1},{1,2},{2,3},{3,0},{4,5},{5,6},{6,7},{7,4},{8,9},{9,10},{10,1... | collective-permute-start | bytes 344072 | tf_op jit(solution)/shard_map/ppermute | solution.py:704
  723.3 57.9 %collective-permute-start.47 = (bf16[384,384]{0,1:T(8,128)(2,1)S(1)}, bf16[384,384]{0,1:T(8,128)(2,1)S(1)}, u32[]{:S(2)}, u32[]{:S(2)}) collective-permute-start(bf16[384,384]{0,1:T(8,128)(2,1)S(1)} %add_convert_fusion.14), channel_id=1, source_target_pairs={{0,1},{1,2},{2,3},{3,0},{4,5},{5,6},{6,7},{7,4},{8,9},{9,10},{10,1... | collective-permute-start | bytes 884744 | tf_op jit(solution)/shard_map/ppermute | solution.py:704
  (112 other events, 1889.8 us)
Sparse Core Ops, SparseCore 0:
  10.2 53.1 all-gather.11
  65.0 54.7 all-gather.5
  121.4 55.0 all-gather.7
  330.1 66.6 reduce-scatter.3
  398.3 37.4 all-gather.9
  471.4 77.3 reduce-scatter.5
  552.3 75.1 reduce-scatter.7

commit v3 on v2

--- a/solution.py
+++ b/solution.py
@@ -373,10 +373,13 @@
 
 
 def merge_kernel(tps, meta, o_ref, x_ref, *refs):
-    weights, (gain_ref, h_ref, n_ref) = refs[:4], refs[4:]
+    weights, (gain_ref, h_ref, n_ref, turned_ref) = refs[:4], refs[4:]
     rows, width = h_ref.shape
     size, depth = width // 4, o_ref.shape[1]
-    turned = o_ref[...]
+    part = depth // tps
+    for hop in range(tps):
+        turned_ref[:, hop * part : (hop + 1) * part] = o_ref[:, pl.ds(tp_at(meta, hop, tps, part), part)]
+    turned = turned_ref[...]
     for flip, weight in enumerate(weights):
         at = pl.ds(shard_at(meta, flip, size), size)
         h_ref[:, at] = x_ref[0, :, at].astype(jnp.float32) + dot(turned, weight[...])
@@ -400,6 +403,7 @@
         ],
         [row, row],
         [shape((seq_count * own, width), jnp.float32), shape((seq_count * own, width), LOW)],
+        [pltpu.VMEM((own, depth), LOW)],
         cost=pl.CostEstimate(
             flops=2 * seq_count * own * depth * width, bytes_accessed=1 << 23, transcendentals=0
         ),
@@ -428,7 +432,11 @@
     turned_ref[...] = jnp.zeros_like(turned_ref)
     for flip, weight in enumerate(weights):
         turned_ref[...] += inner_cols(bg_ref[:, pl.ds(shard_at(meta, flip, size), size)], weight[...])
-    ag_ref[...] = turned_ref[...].astype(LOW)
+    part = depth // tps
+    for hop in range(tps):
+        ag_ref[:, pl.ds(tp_at(meta, hop, tps, part), part)] = turned_ref[
+            :, hop * part : (hop + 1) * part
+        ].astype(LOW)
 
 
 def turn(meta, two_own, two_got, hidden, cotangent, weights, gain, depth, tps):
@@ -462,13 +470,56 @@
     )(meta, two_own, two_got, hidden, cotangent, *weights, gain)
 
 
-def finish_kernel(
-    kv_heads, head_dim, meta, g_ref, a_ref, b_ref, cos_ref, sin_ref, q_ref, *refs
-):
-    weights = refs[:4]
-    x_ref, hg_ref, gain_ref, out_ref, kv_ref, term_ref, one_ref = refs[4:]
-    rows, width = hg_ref.shape
-    size = width // 4
+def back_through_norm(grad, values, gain):
+    root = root_of(values)
+    scaled = gain * grad
+    term = jnp.sum(grad * values * root, axis=0, keepdims=True)
+    return root * scaled - values * root**3 * jnp.mean(scaled * values, axis=-1, keepdims=True), term
+
+
+def finish_kernel(meta, g_ref, q_ref, x_ref, hg_ref, gain_ref, out_ref, term_ref):
+    values = x_ref[...].reshape(hg_ref.shape).astype(jnp.float32)
+    part, term = back_through_norm(inner_cols(g_ref[...], q_ref[...]), values, gain_ref[...])
+    term_ref[...] = term.reshape(term_ref.shape)
+    out_ref[...] = (hg_ref[...] + part).astype(LOW)
+
+
+def finish(meta, q_grad, q_full, inputs, hidden_grad, gain, tps):
+    seq_count, block_len, width = inputs.shape
+    own = block_len // tps
+    tokens = seq_count * own
+    row = pl.BlockSpec((own, width), lambda s, m: (s, 0))
+    return call(
+        finish_kernel,
+        (seq_count,),
+        [
+            pl.BlockSpec((own, q_grad.shape[1]), lambda s, m: (s, 0)),
+            whole(q_full),
+            pl.BlockSpec((1, own, width), lambda s, m: (s, m[PLACE + s], 0)),
+            row,
+            whole(gain),
+        ],
+        [row, pl.BlockSpec((1, 1, width), lambda s, m: (s, 0, 0))],
+        [shape((tokens, width), LOW), shape((seq_count, 1, width), jnp.float32)],
+        cost=pl.CostEstimate(
+            flops=2 * tokens * q_grad.shape[1] * width, bytes_accessed=1 << 23, transcendentals=0
+        ),
+        name="finish",
+    )(meta, q_grad, q_full, inputs, hidden_grad, gain)
+
+
+def one_from_kv(meta, kv_grad, weights, one_ref):
+    size = one_ref.shape[1] // 4
+    skip = weights[0].shape[1] - kv_grad.shape[1]
+    for flip, weight in enumerate(weights):
+        one_ref[:, pl.ds(shard_at(meta, flip, size), size)] = inner_cols(
+            kv_grad, weight[:size, skip:]
+        )
+    return one_ref[...]
+
+
+def kv_kernel(kv_heads, head_dim, meta, a_ref, b_ref, cos_ref, sin_ref, *refs):
+    weights, (x_ref, kv_ref, term_ref, one_ref) = refs[:4], refs[4:]
     cosine, sine = cos_ref[...], sin_ref[...]
     for kind in range(2):
         for head in range(kv_heads):
@@ -479,61 +530,75 @@
                 grad = grad * cosine - pltpu.roll(grad, head_dim // 2, 1) * sine
             at = (kind * kv_heads + head) * head_dim
             kv_ref[:, at : at + head_dim] = grad.astype(LOW)
-    one_ref[...] = inner_cols(g_ref[...], q_ref[...])
-    skip = weights[0].shape[1] - kv_ref.shape[1]
-    for flip, weight in enumerate(weights):
-        one_ref[:, pl.ds(shard_at(meta, flip, size), size)] += inner_cols(
-            kv_ref[...], weight[:size, skip:]
-        )
-    one = one_ref[...]
-    values = x_ref[...].reshape(rows, width).astype(jnp.float32)
-    root = root_of(values)
-    term_ref[...] = jnp.sum(one * values * root, axis=0, keepdims=True).reshape(term_ref.shape)
-    scaled = gain_ref[...] * one
-    out_ref[...] = (
-        hg_ref[...]
-        + root * scaled
-        - values * root**3 * jnp.mean(scaled * values, axis=-1, keepdims=True)
-    ).astype(LOW)
-
-
-def finish(meta, q_grad, kv_mine, kv_got, cosine, sine, q_full, weights, inputs, hidden_grad, gain, tps):
+    one = one_from_kv(meta, kv_ref[...], weights, one_ref)
+    values = x_ref[...].reshape(one.shape).astype(jnp.float32)
+    term = jnp.sum(one * values * root_of(values), axis=0, keepdims=True)
+    term_ref[...] = term.reshape(term_ref.shape)
+
+
+def kv_back(meta, kv_mine, kv_got, cosine, sine, weights, inputs, tps):
     seq_count, block_len, width = inputs.shape
     own = block_len // tps
     kv_heads, head_dim = kv_mine.shape[1], kv_mine.shape[4]
     kv_cols = 2 * kv_heads * head_dim
-    tokens = seq_count * own
-    row = pl.BlockSpec((own, width), lambda s, m: (s, 0))
     kv_spec = pl.BlockSpec((2, kv_heads, 1, own, head_dim), lambda s, m: (0, 0, s, 0, 0))
     table_spec = pl.BlockSpec((own, head_dim), lambda s, m: (s * tps + m[PLACE + s], 0))
     return call(
-        functools.partial(finish_kernel, kv_heads, head_dim),
+        functools.partial(kv_kernel, kv_heads, head_dim),
         (seq_count,),
         [
-            pl.BlockSpec((own, q_grad.shape[1]), lambda s, m: (s, 0)),
             kv_spec, kv_spec, table_spec, table_spec,
-            whole(q_full),
             *(whole(w) for w in weights),
             pl.BlockSpec((1, own, width), lambda s, m: (s, m[PLACE + s], 0)),
-            row,
-            whole(gain),
-        ],
-        [
-            row,
+        ],
+        [
             pl.BlockSpec((own, kv_cols), lambda s, m: (s, 0)),
             pl.BlockSpec((1, 1, width), lambda s, m: (s, 0, 0)),
         ],
-        [
-            shape((tokens, width), LOW),
-            shape((tokens, kv_cols), LOW),
-            shape((seq_count, 1, width), jnp.float32),
-        ],
+        [shape((seq_count * own, kv_cols), LOW), shape((seq_count, 1, width), jnp.float32)],
         [pltpu.VMEM((own, width), jnp.float32)],
         cost=pl.CostEstimate(
-            flops=2 * tokens * (q_grad.shape[1] + kv_cols) * width, bytes_accessed=1 << 23, transcendentals=0
+            flops=2 * seq_count * own * kv_cols * width, bytes_accessed=1 << 22, transcendentals=0
         ),
-        name="finish",
-    )(meta, q_grad, kv_mine, kv_got, cosine, sine, q_full, *weights, inputs, hidden_grad, gain)
+        name="kv_back",
+    )(meta, kv_mine, kv_got, cosine, sine, *weights, inputs)
+
+
+def last_kernel(tps, meta, *refs):
+    blocks, kvs, weights = refs[:tps], refs[tps : 2 * tps], refs[2 * tps : 2 * tps + 4]
+    x_ref, gain_ref, out_ref, one_ref = refs[2 * tps + 4 :]
+    seq = pl.program_id(0)
+    own = blocks[0].shape[0]
+    for hop in range(tps):
+        device = lax.rem(meta[TP] + tps - hop, tps)
+        place = jnp.where(seq % 2 == 0, device, tps - 1 - device)
+        at = pl.ds(pl.multiple_of(place * own, own), own)
+        one = one_from_kv(meta, kvs[hop][...], weights, one_ref)
+        values = x_ref[0, at, :].astype(jnp.float32)
+        part, _ = back_through_norm(one, values, gain_ref[...])
+        out_ref[0, at, :] = blocks[hop][...].astype(jnp.float32) + part
+
+
+def last(meta, blocks, kvs, weights, inputs, gain):
+    seq_count, block_len, width = inputs.shape
+    tps = len(blocks)
+    own = block_len // tps
+    every = pl.BlockSpec((1, block_len, width), lambda s, m: (s, 0, 0))
+    return call(
+        functools.partial(last_kernel, tps),
+        (seq_count,),
+        [pl.BlockSpec((own, width), lambda s, m: (s, 0))] * tps
+        + [pl.BlockSpec((own, kvs[0].shape[1]), lambda s, m: (s, 0))] * tps
+        + [whole(w) for w in weights]
+        + [every, whole(gain)],
+        every,
+        shape(inputs.shape, jnp.float32),
+        [pltpu.VMEM((own, width), jnp.float32)],
+        cost=pl.CostEstimate(
+            flops=2 * seq_count * block_len * kvs[0].shape[1] * width, bytes_accessed=1 << 24, transcendentals=0
+        ),
+        name="last",
+    )(meta, *blocks, *kvs, *weights, inputs, gain)
 
 
 def feed_kernel(first, hidden, *refs):
@@ -724,7 +789,7 @@
     def at(self, hop):
         return (self.tp - hop + self.tps) % self.tps
 
-    def scatter_fsdp(self, value, axis):
+    def pairs(self, value, axis):
         size = value.shape[axis] // 4
 
         def pair(core):
@@ -736,7 +801,13 @@
                 axis,
             )
 
-        both = add_low(pair(self.core), self.to_core(pair(1 - self.core)))
+        return pair(self.core), pair(1 - self.core)
+
+    def scatter_core(self, pairs):
+        return add_low(pairs[0], self.to_core(pairs[1]))
+
+    def scatter_x(self, both, axis):
+        size = both.shape[axis] // 2
         away = lax.dynamic_slice_in_dim(both, (1 - self.x) * size, size, axis)
         keep = lax.dynamic_slice_in_dim(both, self.x * size, size, axis)
         return add_low(keep, self.to_x(away))
@@ -815,15 +886,9 @@
     )
     pack_core, pack_across = links.to_core(pack), links.to_x(pack)
     qkv = pack, pack_core, pack_across, links.to_core(pack_across)
-    oq_blocks = lax.all_gather(jnp.concatenate([output_weight, query_weight], axis=0), "tp", axis=0)
-    if ctxs == 2:
-        up_mine = up_weight.T
-        half = up_mine.shape[0] // 2
-        up_near = links.to_x(
-            after(lax.dynamic_slice_in_dim(up_mine, ctx * half, half, 0), pack_across)
-        )
-    else:
-        up_near = pack_across
+    o_blocks = links.gather_tp(output_weight)
+    up_mine = up_weight.T
+
     rows = jnp.stack([item[shard : shard + 3] for item in qkv])
     rows = [
         lax.dynamic_index_in_dim(rows, jnp.bitwise_xor(fsdp, j), 0, keepdims=False) for j in range(4)
@@ -833,7 +898,7 @@
     bias = jnp.concatenate(
         [r[2, : smalls.shape[0]].reshape(-1, head_dim // fsdps) for r in rows], axis=1
     ).reshape(1, lanes).astype(jnp.float32)
-    bias = after(bias, up_near)
+    bias = after(bias, o_blocks[1])
 
     cosine, sine = rope_tables(positions.reshape(tokens), head_dim)
     normed_one, query_blocks, kv_own = project(
@@ -841,6 +906,11 @@
     )
     if ctxs == 2:
         kv_before = lax.ppermute(kv_own, "ctx", [(0, 1)])
+        half = up_mine.shape[0] // 2
+        up_near = links.to_x(
+            after(lax.dynamic_slice_in_dim(up_mine, ctx * half, half, 0), pack_across)
+        )
+        up_far = links.to_y(after(up_near, kv_before))
     else:
         kv_before = lax.all_gather(
             kv_own.reshape(seq_count, block_len, kv_cols), "ctx", axis=1, tiled=True
@@ -854,10 +924,12 @@
     queries = jnp.stack(swap(lambda d: lax.dynamic_index_in_dim(query_blocks, d, 0, keepdims=False)))
 
     def gather_whole(item):
-        return lax.all_gather(after(item, up_near), "fsdp", axis=1, tiled=True)
+        return lax.all_gather(after(item, pack_across), "fsdp", axis=1, tiled=True)
 
     gate_full, down_full = gather_whole(gate_weight.T), gather_whole(down_weight)
-    o_wide = after(oq_blocks, kv_own)[:, :q_cols].reshape(depth, shard)
+    o_blocks = o_blocks[:2] + [after(item, kv_own) for item in o_blocks[2:]]
+    o_wide = jnp.concatenate(o_blocks, axis=0)
+    q_blocks = links.gather_tp(after(query_weight, kv_own))
     o_across = links.to_x(o_wide)
     o_core = links.to_core(after(o_wide, queries))
 
@@ -868,25 +940,26 @@
     )
 
     order = jnp.tile(jnp.arange(own, dtype=jnp.int32), depth // head_dim // kv_heads)[None]
-    order = after(order, (cot_all, one_all))
+    order = after(order, (cot_all, one_all, q_blocks[2], *([up_near] if ctxs == 2 else [])))
     sizes = (seq_count, kv_heads, head_dim, tps)
     mixed, lse = attend(meta, queries, kv_before, kv_own, order, key_block, sizes)
     o_core_across = links.to_core(after(o_across, mixed))
     o_parts = (o_wide, o_core, o_across, o_core_across)
     hidden, normed_two = merge(meta, mixed, inputs, o_parts, mlp_gamma, tps)
     two_blocks = [normed_two, links.hop_tp(normed_two)]
-    q_wide = jnp.concatenate([oq_blocks[j, q_cols:] for j in range(tps)], axis=1)
+    q_wide = jnp.zeros((query_weight.shape[0], depth), LOW)
+    for hop, item in enumerate(q_blocks):
+        q_wide = lax.dynamic_update_slice_in_dim(q_wide, item, links.at(hop) * q_cols, 1)
     if ctxs == 2:
-        up_far = links.to_y(after(up_near, normed_two))
-        up_core, up_near_core = (links.to_core(after(item, mixed)) for item in (up_mine, up_near))
-        up_far_core = links.to_core(up_far)
-        up_full = assemble(meta, up_mine, up_near, up_far, up_core, up_near_core, up_far_core)
+        up_cores = [links.to_core(after(item, mixed)) for item in (up_mine, up_near)]
+        up_cores.append(links.to_core(after(up_far, normed_two)))
+        up_full = assemble(meta, up_mine, up_near, up_far, *up_cores)
     else:
-        up_full = gather_whole(up_weight.T)
+        up_full = gather_whole(up_mine)
+    q_full = lax.all_gather(after(q_wide, down_full), "fsdp", axis=0, tiled=True)
+
     two_blocks.append(links.hop_tp(after(two_blocks[-1], (gate_full, up_full, down_full))))
     two_blocks.append(links.hop_tp(two_blocks[-1]))
-    q_full = lax.all_gather(after(q_wide, down_full), "fsdp", axis=0, tiled=True)
-
     kept, two_parts, mixed_parts, two_total = None, [], [], None
     for hop in range(tps):
         block = two_blocks[hop]
@@ -907,7 +980,6 @@
     act_all, gate_all, up_all = kept
     two_all = jnp.concatenate(two_blocks, axis=0)
     down_term = inner_rows(cot_all, after(act_all, two_total)).astype(LOW)
-    down_weight_grad = links.reduce_weight(down_term)
     two_got = after(two_got, down_term)
 
     hidden_grad, branch_grad, attended_grad, mlp_term = turn(
@@ -929,11 +1001,13 @@
         token = (mixed_got, q_grad)
     mixed_got = links.hop_tp(add_low(mixed_parts[2], after(mixed_got, q_grads[0])))
     q_grad = jnp.concatenate(q_grads, axis=0)
+    shares = swap(lambda d: lax.dynamic_slice_in_dim(q_grad, d * q_cols, q_cols, 1))
+    input_low, attn_term = finish(meta, q_grad, q_full, inputs, hidden_grad, attn_gamma, tps)
+    output_pairs = links.pairs(inner_rows(mixed, after(branch_grad, q_grads[-1])).astype(LOW), 1)
+    token = (mixed_got, input_low, kv_parts, shares, output_pairs)
     kv_parts = [
-        mine if got is None else add_low(after(mine, mixed_got), got) for mine, got in kv_parts
+        mine if got is None else add_low(after(mine, token), got) for mine, got in kv_parts
     ]
-    gate_term = inner_rows(two_all, after(gate_all, kv_parts)).astype(LOW)
-    mixed_got = links.hop_tp(add_low(mixed_parts[3], mixed_got))
 
     def kv_rows(hop):
         return jnp.stack(
@@ -944,90 +1018,104 @@
             axis=2,
         )
 
-    kv_mine = kv_rows(0)
-    kv_got = links.hop_tp(kv_rows(1))
-    kv_got = links.hop_tp(add_low(kv_rows(2), after(kv_got, (gate_term, mixed_got))))
-    up_term = inner_rows(two_all, after(up_all, (gate_term, kv_parts))).astype(LOW)
-    gate_weight_grad = links.reduce_weight(after(gate_term, kv_got)).T
-    kv_got = links.hop_tp(add_low(kv_rows(3), after(kv_got, up_term)))
-    up_weight_grad = links.reduce_weight(after(up_term, kv_got)).T
+    def fsdp_rows(value, below):
+        return jnp.concatenate(
+            [item for j in range(fsdps) for item in (value[j * shard : (j + 1) * shard], below(j))], axis=0
+        )
+
+    def output_rows(hop):
+        return lax.dynamic_slice_in_dim(output_part, links.at(hop) * q_cols, q_cols, 0)
+
+    kv_mine, kv_next = kv_rows(0), kv_rows(1)
+    mixed_next = add_low(mixed_parts[3], mixed_got)
+    mixed_got = links.hop_tp(after(mixed_next, (shares, kv_next, input_low, output_pairs)))
+    kv_got = links.hop_tp(kv_next)
+    gate_term = inner_rows(two_all, after(gate_all, kv_next)).astype(LOW)
+    down_weight_grad = links.reduce_weight(after(down_term, kv_next))
+    kv_next = add_low(kv_rows(2), kv_got)
+
+    in_blocks = [input_low, links.hop_tp(after(input_low, (mixed_got, kv_next, gate_term)))]
+    kv_got = links.hop_tp(kv_next)
+    gate_weight_grad = links.reduce_weight(after(gate_term, mixed_got)).T
+    up_term = inner_rows(two_all, after(up_all, (mixed_got, gate_term))).astype(LOW)
+    output_both = links.scatter_core(after(output_pairs, mixed_got))
+    kv_next = add_low(kv_rows(3), kv_got)
     out_low = hidden + mixed_parts[0].astype(jnp.float32) + mixed_got.astype(jnp.float32)
     out_low = lax.optimization_barrier(out_low.astype(LOW))
-    out_blocks = [out_low, links.hop_tp(out_low)]
-    output_part = links.scatter_fsdp(inner_rows(mixed, after(branch_grad, up_term)).astype(LOW), 1)
-    input_low, kv_grad, attn_term = finish(
-        meta, after(q_grad, down_weight_grad), kv_mine, kv_got, cosine, sine, q_full, qkv, inputs, hidden_grad, attn_gamma, tps
-    )
-    input_low = lax.optimization_barrier(input_low)
-    in_blocks = [input_low, links.hop_tp(input_low)]
-
-    kv_each = kv_cols // tps
-    attn_sum = jnp.sum(attn_term, axis=0)
-    mlp_sum = jnp.sum(mlp_term, axis=0)
-
-    def share(device):
-        grads = jnp.concatenate(
-            [
-                lax.dynamic_slice_in_dim(q_grad, device * q_cols, q_cols, 1),
-                lax.dynamic_slice_in_dim(kv_grad, device * kv_each, kv_each, 1),
-            ],
-            axis=1,
+
+    out_blocks = [out_low, links.hop_tp(after(out_low, (in_blocks[1], kv_next, up_term, output_both)))]
+    kv_got = links.hop_tp(kv_next)
+    up_weight_grad = links.reduce_weight(after(up_term, in_blocks[1])).T
+    output_part = links.scatter_x(after(output_both, in_blocks[1]), 1)
+    grads_all = after(jnp.concatenate(shares, axis=0), in_blocks[1])
+    q_bias_row = jnp.sum(grads_all.astype(jnp.float32), axis=0, keepdims=True)
+    q_below = jnp.pad(q_bias_row, ((0, 15), (0, 0))).astype(LOW)
+    q_pairs = links.pairs(fsdp_rows(inner_rows(one_all, grads_all).astype(LOW), lambda j: q_below), 0)
+    kv_grad, kv_term = kv_back(meta, kv_mine, kv_got, cosine, sine, qkv, inputs, tps)
+    gain_terms = jnp.concatenate(
+        [jnp.sum(attn_term, axis=0) + jnp.sum(kv_term, axis=0), jnp.sum(mlp_term, axis=0)], axis=1
+    ).reshape(-1, kv_cols)
+    gain_terms = jnp.pad(gain_terms, ((0, 16 - gain_terms.shape[0]), (0, 0))).astype(LOW)
+    kv_blocks = [jnp.concatenate([kv_grad, gain_terms], axis=0)]
+
+    in_blocks.append(links.hop_tp(after(in_blocks[1], (out_blocks[1], kv_blocks[0], q_pairs))))
+    kv_blocks.append(links.hop_tp(kv_blocks[0]))
+    q_both = links.scatter_core(after(q_pairs, out_blocks[1]))
+    output_got = links.hop_tp(after(output_rows(1), out_blocks[1]))
+    output_next = add_low(output_rows(2), output_got)
+
+    out_blocks.append(
+        links.hop_tp(
+            after(out_blocks[1], (in_blocks[2], kv_blocks[1], q_both, output_next, down_weight_grad))
         )
-        gains = jnp.concatenate(
-            [lax.dynamic_slice_in_dim(item, device * shard, shard, 1) for item in (attn_sum, mlp_sum)], axis=0
+    )
+    kv_blocks.append(links.hop_tp(kv_blocks[1]))
+    q_part = links.scatter_x(after(q_both, in_blocks[2]), 0)
+    output_got = links.hop_tp(after(output_next, in_blocks[2]))
+    output_next = add_low(output_rows(3), output_got)
+
+    in_blocks.append(
+        links.hop_tp(after(in_blocks[2], (out_blocks[2], kv_blocks[2], q_part, output_next)))
+    )
+    kv_blocks.append(links.hop_tp(kv_blocks[2]))
+    q_total = links.sum_ctx(after(q_part, out_blocks[2]))
+    output_got = links.hop_tp(after(output_next, out_blocks[2]))
+    output_sum = add_low(output_rows(0), output_got)
+    own_tokens = seq_count * own
+    kv_all = jnp.concatenate([item[:own_tokens] for item in kv_blocks], axis=0)
+    gain_rows = sum(
+        item[own_tokens : own_tokens + 2 * width // kv_cols].astype(jnp.float32) for item in kv_blocks
+    ).reshape(2, width)
+    kv_bias_row = jnp.sum(kv_all.astype(jnp.float32), axis=0, keepdims=True)
+
+    def kv_below(j):
+        gains = jnp.pad(gain_rows[:, j * shard : (j + 1) * shard], ((0, 0), (0, kv_cols - shard)))
+        return jnp.pad(jnp.concatenate([gains, kv_bias_row], axis=0), ((0, 13), (0, 0))).astype(LOW)
+
+    kv_pairs = links.pairs(fsdp_rows(inner_rows(one_all, kv_all).astype(LOW), kv_below), 0)
+
+    out_blocks.append(
+        links.hop_tp(
+            after(out_blocks[2], (in_blocks[3], kv_pairs, q_total, output_sum, gate_weight_grad))
         )
-        gains = jnp.pad(gains, ((0, 14), (0, q_cols + kv_each - shard))).astype(LOW)
-        return jnp.concatenate([grads, gains], axis=0)
-
-    shares = swap(share)
-    own_tokens = seq_count * own
-    grads_all = jnp.concatenate([item[:own_tokens] for item in shares], axis=0)
-    gain_rows = sum(item[own_tokens : own_tokens + 2].astype(jnp.float32) for item in shares)
-    bias_row = jnp.sum(grads_all.astype(jnp.float32), axis=0, keepdims=True)
-    below = jnp.pad(jnp.concatenate([gain_rows, bias_row], axis=0), ((0, 13), (0, 0))).astype(LOW)
-    term = inner_rows(one_all, grads_all).astype(LOW)
-    in_blocks.append(links.hop_tp(after(in_blocks[-1], (term, out_blocks[1], gate_weight_grad))))
-    out_blocks.append(links.hop_tp(after(out_blocks[-1], in_blocks[1])))
-
-    def output_rows(hop):
-        return lax.dynamic_slice_in_dim(output_part, links.at(hop) * q_cols, q_cols, 0)
-
-    output_got = links.hop_tp(after(output_rows(1), in_blocks[1]))
-    in_blocks.append(
-        links.hop_tp(after(in_blocks[-1], (out_blocks[2], output_got, up_weight_grad)))
-    )
-    out_blocks.append(links.hop_tp(after(out_blocks[-1], in_blocks[2])))
-    output_got = links.hop_tp(add_low(output_rows(2), after(output_got, in_blocks[2])))
-    term = jnp.concatenate(
-        [item for j in range(fsdps) for item in (term[j * shard : (j + 1) * shard], below)], axis=0
-    )
-    total = links.sum_ctx(links.scatter_fsdp(term, 0))
-    query_weight_grad = total[:shard, :q_cols]
-    below = total[shard:]
+    )
+    kv_both = links.scatter_core(after(kv_pairs, in_blocks[3]))
+    output_weight_grad = links.sum_ctx(after(output_sum, in_blocks[3]))
+    kv_part = links.scatter_x(kv_both, 0)
+    in_blocks[0] = after(in_blocks[0], kv_both)
+    input_grad = last(meta, in_blocks, kv_blocks, qkv, inputs, attn_gamma)
+    out_blocks[0] = after(out_blocks[0], (kv_part, input_grad, up_weight_grad))
+    kv_total = links.sum_ctx(kv_part)
+    outputs = spread_out(meta, out_blocks, seq_count, LOW)
+    query_weight_grad = q_total[:shard]
     part = head_dim // fsdps
     query_bias_grad = lax.dynamic_slice_in_dim(
-        below[2, :q_cols].reshape(local_heads, head_dim), fsdp * part, part, 1
-    )
-    kv_low = jnp.concatenate(
-        [total[:shard, q_cols:], below[:, :q_cols].reshape(-1, kv_each), below[:, q_cols:]], axis=0
-    ).astype(LOW)
-    kv_low = lax.optimization_barrier(after(kv_low, in_blocks[2]))
-    kv_blocks = links.gather_tp(kv_low)
-    output_got = links.hop_tp(add_low(output_rows(3), output_got))
-    output_weight_grad = links.sum_ctx(add_low(output_rows(0), output_got))
-    out_blocks[0] = after(out_blocks[0], (kv_blocks[-1], output_weight_grad, up_weight_grad))
-    outputs = spread_out(meta, out_blocks, seq_count, LOW)
-    in_blocks[0] = after(in_blocks[0], outputs)
-    input_grad = spread_out(meta, in_blocks, seq_count, jnp.float32)
-    all_low = jnp.stack(kv_blocks)
-    by_device = [
-        lax.dynamic_index_in_dim(all_low, links.at(j), 0, keepdims=False) for j in range(tps)
-    ]
-    kv_weight = jnp.concatenate([item[:shard] for item in by_device], axis=1).astype(jnp.float32)
-    mine = lax.dynamic_index_in_dim(all_low, (tp - fsdp + tps) % tps, 0, keepdims=False)
-    gains = mine[shard : shard + 16 * (q_cols // kv_each)].reshape(16, q_cols).astype(jnp.float32)
-    kv_bias = jnp.stack([item[-14] for item in by_device]).reshape(2, kv_heads, head_dim)
-    kv_bias = lax.dynamic_slice_in_dim(kv_bias, fsdp * part, part, 2).astype(jnp.float32)
+        q_total[shard].reshape(local_heads, head_dim), fsdp * part, part, 1
+    )
+    kv_weight = kv_total[:shard]
+    gains = kv_total[shard : shard + 2, :shard]
+    kv_bias = kv_total[shard + 2].reshape(2, kv_heads, head_dim)
+    kv_bias = lax.dynamic_slice_in_dim(kv_bias, fsdp * part, part, 2)
     half = kv_cols // 2
 
     return (

time: 820 us -> 776 us (0.946)
  waiting for transfers between devices: 372 us -> 291 us
  starting transfers between devices: 51.1 us -> 66.5 us
  matrix products: 58.3 us -> 67.8 us
  other arithmetic: 46 us -> 55 us
    ppermute x2, waiting for transfers between devices: 25 us -> 0.01 us  [local(): kv_parts.append((grad_own, lax.ppermute(grad_before, 'ctx', [(1, 0)])))]
    ppermute x6 -> x7, waiting for transfers between devices: 62.7 us -> 40.1 us  [to_y(): return lax.ppermute(value, 'ctx', [(0, 1), (1, 0)])]
    pallas_call x1 -> x3, Pallas kernels: 10.1 us -> 24.4 us  [the longest x1 13.2 us: last(): call(functools.partial(last_kernel, tps), (seq_count,), [pl.BlockSpec((ow...]
    ppermute x30 -> x36, waiting for transfers between devices: 222 us -> 209 us  [hop_tp(): lax.ppermute(value, 'tp', [(i, (i + hop) % self.tps) for i in range(self....]
    ppermute x1, waiting for transfers between devices: 11.3 us -> 0.01 us  [local(): kv_before = lax.ppermute(kv_own, 'ctx', [(0, 1)])]
    ppermute x6 -> x7, starting transfers between devices: 6.88 us -> 16.9 us  [to_y(): return lax.ppermute(value, 'ctx', [(0, 1), (1, 0)])]
    pallas_call x4, Pallas kernels: 114 us -> 104 us  [feed(): pl.pallas_call(functools.partial(feed_kernel, first, hidden), grid_spec=p...]
    dot_general x5 -> x6, matrix products: 58.3 us -> 67.8 us  [inner_rows(): lax.dot_general(left, right, (((0,), (0,)), ((), ())), preferred_element_...]
  transfers between devices with their start and end apart: 60 -> 68, of which waited for: 30 -> 32; matrix products, arithmetic and copies ran while one was open for 16% -> 21% of each run, Pallas kernels for 24% -> 26%
where the time goes in v3:
time: 776 us; the launch traced here: 767 us
  waiting for transfers between devices  291 us (38%)
  Pallas kernels  203 us (26%)
  local copies, waits for them, and re-layouts  68.2 us (9%)
  matrix products  67.8 us (9%)
  starting transfers between devices  66.5 us (9%)
  other arithmetic  55 us (7%)
  between operations  15.8 us (2%)
    ppermute x36, waiting for transfers between devices, hop_tp(): lax.ppermute(value, 'tp', [(i, (i + hop) % self.tps) for i in range(self....  209 us
    pallas_call x4, Pallas kernels, feed(): pl.pallas_call(functools.partial(feed_kernel, first, hidden), grid_spec=p...  104 us
    dot_general x6, matrix products, inner_rows(): lax.dot_general(left, right, (((0,), (0,)), ((), ())), preferred_element_...  67.8 us
    ppermute x6, waiting for transfers between devices, to_x(): return lax.ppermute(value, 'fsdp', [(0, 2), (2, 0), (1, 3), (3, 1)])  40.3 us
    ppermute x7, waiting for transfers between devices, to_y(): return lax.ppermute(value, 'ctx', [(0, 1), (1, 0)])  40.1 us
    unnamed x203, local copies, waits for them, and re-layouts  36.7 us
    ppermute x36, starting transfers between devices, hop_tp(): lax.ppermute(value, 'tp', [(i, (i + hop) % self.tps) for i in range(self....  33 us
    convert_element_type x17, other arithmetic, add_low(): return (left.astype(jnp.float32) + right.astype(jnp.float32)).astype(LOW)  24.6 us
  transfers between devices with their start and end apart: 68, of which 32 were waited for; matrix products, arithmetic and copies ran while one was open for 21% of the time, Pallas kernels for 26%

profile of v3, /device:TPU:0, one launch (start us, length us, event | category | flops | bytes accessed | tf_op | source)
XLA Modules:
  0.0 767.0 jit_solution(4478856300512781920)
XLA Ops:
  15.3 16.2 %collective-permute-done.1.refs_2_.refs_10_ = bf16[400,896]{1,0:T(8,128)(2,1)} collective-permute-done((bf16[400,896]{1,0:T(8,128)(2,1)S(1)}, bf16[400,896]{1,0:T(8,128)(2,1)}, u32[]{:S(2)}, u32[]{:S(2)}) %collective-permute-start.1) | collective-permute-done | bytes 716832 | tf_op jit(solution)/shard_map/ppermute | solution.py:763
  58.3 13.9 %project.1 = (bf16[1536,1536]{1,0:T(8,128)(2,1)}, bf16[4,384,384]{2,1,0:T(8,128)(2,1)S(1)}, bf16[1536,512]{1,0:T(8,128)(2,1)}) custom-call(s32[6]{0:T(128)S(1)} %stack.100.meta.refs_0_, bf16[2,768,1536]{2,1,0:T(8,128)(2,1)} %refs_12_.1, f32[1,1536]{1,0:T(1,128)S(1)} %maximum_convert_fusion.gain_ref.refs_13_, f32[1,896]{1,0:T(1,128)S(1)} %bitcast.91, ...), custom_call_target="tpu_custom_call" | custom-call | flops 4227858432 | bytes 18874368 | tf_op jit(solution)/shard_map/project/pallas_call | solution.py:131
  87.9 15.8 %collective-permute-done.5 = bf16[384,384]{1,0:T(8,128)(2,1)S(1)} collective-permute-done((bf16[384,384]{1,0:T(8,128)(2,1)S(1)}, bf16[384,384]{1,0:T(8,128)(2,1)S(1)}, u32[]{:S(2)}, u32[]{:S(2)}) %collective-permute-start.5) | collective-permute-done | bytes 294944 | tf_op jit(solution)/shard_map/ppermute | solution.py:769
  121.7 23.4 %collective-permute-done.14.refs_2_ = bf16[1536,384]{1,0:T(8,128)(2,1)S(1)} collective-permute-done((bf16[1536,384]{1,0:T(8,128)(2,1)S(1)}, bf16[1536,384]{1,0:T(8,128)(2,1)S(1)}, u32[]{:S(2)}, u32[]{:S(2)}) %collective-permute-start.14) | collective-permute-done | bytes 1179680 | tf_op jit(solution)/shard_map/ppermute | solution.py:763
  155.4 11.4 %collective-permute-done.17.far_ref = bf16[1120,384]{1,0:T(8,128)(2,1)S(1)} collective-permute-done((bf16[1120,384]{1,0:T(8,128)(2,1)}, bf16[1120,384]{1,0:T(8,128)(2,1)S(1)}, u32[]{:S(2)}, u32[]{:S(2)}) %collective-permute-start.17) | collective-permute-done | bytes 860192 | tf_op jit(solution)/shard_map/ppermute | solution.py:766
  171.3 20.0 %collective-permute-done.31 = bf16[384,384]{1,0:T(8,128)(2,1)S(1)} collective-permute-done((bf16[384,384]{1,0:T(8,128)(2,1)}, bf16[384,384]{1,0:T(8,128)(2,1)S(1)}, u32[]{:S(2)}, u32[]{:S(2)}) %collective-permute-start.31) | collective-permute-done | bytes 294944 | tf_op jit(solution)/shard_map/ppermute | solution.py:769
  199.5 26.0 %feed.4 = (bf16[1536,2240]{1,0:T(8,128)(2,1)}, bf16[1536,2240]{1,0:T(8,128)(2,1)}, bf16[1536,2240]{1,0:T(8,128)(2,1)}, bf16[384,1536]{1,0:T(8,128)(2,1)}, bf16[384,1536]{1,0:T(8,128)(2,1)}) custom-call(s32[6]{0:T(128)} %copy-done.25, bf16[384,1536]{1,0:T(8,128)(2,1)} %copy-done.15, bf16[1536,1536]{1,0:T(8,128)(2,1)} %copy-done.73, ...), custom_call_target="tpu_custom_call" | custom-call | flops 15854469120 | bytes 20643840 | tf_op jit(solution)/shard_map/feed/pallas_call | solution.py:652
  228.6 25.8 %feed.5 = (bf16[1536,2240]{1,0:T(8,128)(2,1)}, bf16[1536,2240]{1,0:T(8,128)(2,1)}, bf16[1536,2240]{1,0:T(8,128)(2,1)}, bf16[384,1536]{1,0:T(8,128)(2,1)}, bf16[384,1536]{1,0:T(8,128)(2,1)}) custom-call(s32[6]{0:T(128)} %copy-done.25, bf16[384,1536]{1,0:T(8,128)(2,1)} %collective-permute-done.16.refs_1_, ...), custom_call_target="tpu_custom_call", output_to_operand_aliasing={{0}: (6, {}), {1}: (7, {}), {2}: (8, {})} | custom-call | flops 15854469120 | bytes 20643840 | tf_op jit(solution)/shard_map/feed/pallas_call | solution.py:652
  256.7 26.0 %feed.6 = (bf16[1536,2240]{1,0:T(8,128)(2,1)}, bf16[1536,2240]{1,0:T(8,128)(2,1)}, bf16[1536,2240]{1,0:T(8,128)(2,1)}, bf16[384,1536]{1,0:T(8,128)(2,1)}, bf16[384,1536]{1,0:T(8,128)(2,1)}) custom-call(s32[6]{0:T(128)} %copy-done.25, bf16[384,1536]{1,0:T(8,128)(2,1)} %copy-done.48, ...), custom_call_target="tpu_custom_call", output_to_operand_aliasing={{0}: (6, {}), {1}: (7, {}), {2}: (8, {})} | custom-call | flops 15854469120 | bytes 20643840 | tf_op jit(solution)/shard_map/feed/pallas_call | solution.py:652
  284.3 26.1 %feed.7 = (bf16[1536,2240]{1,0:T(8,128)(2,1)}, bf16[1536,2240]{1,0:T(8,128)(2,1)}, bf16[1536,2240]{1,0:T(8,128)(2,1)}, bf16[384,1536]{1,0:T(8,128)(2,1)}, bf16[384,1536]{1,0:T(8,128)(2,1)}) custom-call(s32[6]{0:T(128)} %copy-done.25, bf16[384,1536]{1,0:T(8,128)(2,1)} %copy-done.50, ...), custom_call_target="tpu_custom_call", output_to_operand_aliasing={{0}: (6, {}), {1}: (7, {}), {2}: (8, {})} | custom-call | flops 15854469120 | bytes 20643840 | tf_op jit(solution)/shard_map/feed/pallas_call | solution.py:652
  315.7 17.0 %convolution_convert_fusion.2 = bf16[1536,2240]{1,0:T(8,128)(2,1)} fusion(bf16[1536,1536]{1,0:T(8,128)(2,1)} %copy-done.73, bf16[1536,2240]{1,0:T(8,128)(2,1)} %get-tuple-element.156), kind=kOutput, calls=%fused_computation.2 | convolution fusion | flops 10573086720 | bytes 18481152 | tf_op jit(solution)/shard_map/dot_general | solution.py:35
  344.9 9.8 %turn.1 = (f32[384,1536]{1,0:T(8,128)}, bf16[384,1536]{1,0:T(8,128)(2,1)S(1)}, bf16[384,1536]{1,0:T(8,128)(2,1)S(1)}, f32[2,1,1536]{2,1,0:T(1,128)S(1)}) custom-call(s32[6]{0:T(128)S(1)} %copy-done.26, bf16[384,1536]{1,0:T(8,128)(2,1)S(1)} %copy-done.10, bf16[384,1536]{1,0:T(8,128)(2,1)S(1)} %copy-done.12, f32[384,1536]{1,0:T(8,128)} %get-tuple-element.126.h_ref, ...), custom_call_target="tpu_custom_call" | custom-call | flops 1811939328 | bytes 8388608 | tf_op jit(solution)/shard_map/turn/pallas_call | solution.py:447
  370.2 10.4 %attend_back.3 = (bf16[192,1536]{1,0:T(8,128)(2,1)S(1)}, bf16[2,2,768,128]{3,2,1,0:T(8,128)(2,1)}, bf16[2,2,768,128]{3,2,1,0:T(8,128)(2,1)S(1)}) custom-call(s32[6]{0:T(128)S(1)} %copy-done.26, bf16[4,384,384]{2,1,0:T(8,128)(2,1)S(1)} %copy-done.18, bf16[4,384,384]{2,1,0:T(8,128)(2,1)S(1)} %copy-done.18, bf16[1536,512]{1,0:T(8,128)(2,1)} %copy-done.34, ...), custom_call_target="tpu_custom_call" | custom-call | flops 7247757312 | bytes 4194304 | tf_op jit(solution)/shard_map/attend_back/pallas_call | solution.py:341
  433.0 16.8 %convolution_convert_fusion.1 = bf16[1536,2240]{1,0:T(8,128)(2,1)} fusion(bf16[1536,1536]{1,0:T(8,128)(2,1)S(1)} %constant_dynamic-update-slice_fusion.10, bf16[1536,2240]{1,0:T(8,128)(2,1)} %get-tuple-element.184), kind=kOutput, calls=%fused_computation.1 | convolution fusion | flops 10573086720 | bytes 18481152 | tf_op jit(solution)/shard_map/dot_general | solution.py:35
  472.3 10.3 %collective-permute-done.36 = bf16[2,2,2,192,128]{4,3,2,1,0:T(8,128)(2,1)S(1)} collective-permute-done((bf16[2,2,2,192,128]{4,3,2,1,0:T(8,128)(2,1)S(1)}, bf16[2,2,2,192,128]{4,3,2,1,0:T(8,128)(2,1)S(1)}, u32[]{:S(2)}, u32[]{:S(2)}) %collective-permute-start.36) | collective-permute-done | bytes 393248 | tf_op jit(solution)/shard_map/ppermute | solution.py:769
  500.2 17.5 %convolution_convert_fusion = bf16[1536,2240]{1,0:T(8,128)(2,1)} fusion(bf16[1536,1536]{1,0:T(8,128)(2,1)} %copy-done.65, bf16[1536,2240]{1,0:T(8,128)(2,1)} %get-tuple-element.187), kind=kOutput, calls=%fused_computation | convolution fusion | flops 10573086720 | bytes 18481152 | tf_op jit(solution)/shard_map/dot_general | solution.py:35
  522.7 21.1 %collective-permute-done.39.refs_6_ = bf16[400,512]{1,0:T(8,128)(2,1)S(1)} collective-permute-done((bf16[400,512]{1,0:T(8,128)(2,1)S(1)}, bf16[400,512]{1,0:T(8,128)(2,1)S(1)}, u32[]{:S(2)}, u32[]{:S(2)}) %collective-permute-start.39) | collective-permute-done | bytes 409632 | tf_op jit(solution)/shard_map/ppermute | solution.py:769
  577.9 11.2 %collective-permute-done.43.refs_1_ = bf16[384,1536]{1,0:T(8,128)(2,1)} collective-permute-done((bf16[384,1536]{1,0:T(8,128)(2,1)S(1)}, bf16[384,1536]{1,0:T(8,128)(2,1)}, u32[]{:S(2)}, u32[]{:S(2)}) %collective-permute-start.43) | collective-permute-done | bytes 1179680 | tf_op jit(solution)/shard_map/ppermute | solution.py:769
  592.6 10.8 %collective-permute-start.48 = (bf16[192,2240]{1,0:T(8,128)(2,1)}, bf16[192,2240]{1,0:T(8,128)(2,1)S(1)}, u32[]{:S(2)}, u32[]{:S(2)}) collective-permute-start(bf16[192,2240]{1,0:T(8,128)(2,1)} %reduce-scatter.4.cloned.1.call-done), channel_id=1, source_target_pairs={{0,4},{4,0},{1,5},{5,1},{2,6},{6,2},{3,7},{7,3},{8,12},{12,8},{9,1... | collective-permute-start | bytes 2580488 | tf_op jit(solution)/shard_map/ppermute | solution.py:766
  618.7 12.4 %collective-permute-done.48 = bf16[192,2240]{1,0:T(8,128)(2,1)S(1)} collective-permute-done((bf16[192,2240]{1,0:T(8,128)(2,1)}, bf16[192,2240]{1,0:T(8,128)(2,1)S(1)}, u32[]{:S(2)}, u32[]{:S(2)}) %collective-permute-start.48) | collective-permute-done | bytes 860192 | tf_op jit(solution)/shard_map/ppermute | solution.py:766
  640.2 28.0 %collective-permute-done.51 = bf16[384,384]{0,1:T(8,128)(2,1)S(1)} collective-permute-done((bf16[384,384]{0,1:T(8,128)(2,1)S(1)}, bf16[384,384]{0,1:T(8,128)(2,1)S(1)}, u32[]{:S(2)}, u32[]{:S(2)}) %collective-permute-start.51) | collective-permute-done | bytes 294944 | tf_op jit(solution)/shard_map/ppermute | solution.py:769
  681.8 18.4 %collective-permute-done.52.refs_3_ = bf16[384,1536]{1,0:T(8,128)(2,1)} collective-permute-done((bf16[384,1536]{1,0:T(8,128)(2,1)}, bf16[384,1536]{1,0:T(8,128)(2,1)}, u32[]{:S(2)}, u32[]{:S(2)}) %collective-permute-start.52) | collective-permute-done | bytes 1179680 | tf_op jit(solution)/shard_map/ppermute | solution.py:769
  713.9 13.8 %collective-permute-done.55 = bf16[192,2240]{1,0:T(8,128)(2,1)S(1)} collective-permute-done((bf16[192,2240]{1,0:T(8,128)(2,1)}, bf16[192,2240]{1,0:T(8,128)(2,1)S(1)}, u32[]{:S(2)}, u32[]{:S(2)}) %collective-permute-start.55) | collective-permute-done | bytes 860192 | tf_op jit(solution)/shard_map/ppermute | solution.py:766
  738.3 13.2 %last.1 = f32[2,768,1536]{2,1,0:T(8,128)} custom-call(s32[6]{0:T(128)S(1)} %copy-done.26, bf16[384,1536]{1,0:T(8,128)(2,1)S(1)} %copy-done.14, bf16[384,1536]{1,0:T(8,128)(2,1)} %collective-permute-done.41.refs_1_, bf16[384,1536]{1,0:T(8,128)(2,1)} %collective-permute-done.44.refs_2_, bf16[384,1536]{1,0:T(8,128)(2,1)} %collective-permute-done.52.refs_3_, ...), custom_call_target="tpu_custom_call" | custom-call | flops 2415919104 | bytes 16777216 | tf_op jit(solution)/shard_map/last/pallas_call | solution.py:587
  (472 shorter events, 335.7 us)
Async XLA Ops:
  7.2 192.1 %all-gather.4.cloned.1.call-start = ((), (), s32[]{:S(2)}) async-start(), calls=%async_computation.3 | async-start | bytes 8601600 | tf_op jit(solution)/shard_map/all_gather | solution.py:927
  31.5 167.9 %all-gather.6.cloned.1.call-start = ((), (), s32[]{:S(2)}) async-start(), calls=%async_computation.4 | async-start | bytes 8601600 | tf_op jit(solution)/shard_map/all_gather | solution.py:927
  54.1 51.2 %collective-permute-start.10 = (bf16[1120,384]{1,0:T(8,128)(2,1)}, bf16[1120,384]{1,0:T(8,128)(2,1)}, u32[]{:S(2)}, u32[]{:S(2)}) collective-permute-start(bf16[1120,384]{1,0:T(8,128)(2,1)} %dynamic-slice_bitcast_fusion), channel_id=1, source_target_pairs={{0,16},{16,0},{8,24},{24,8},{1,17},{17,1},{9,25},{25,9},{2,18},{18... | collective-permute-start | bytes 2580488 | tf_op jit(solution)/shard_map/ppermute | solution.py:763
  55.5 338.8 %all-gather.8.cloned.1.call-start = ((), (), s32[]{:S(2)}) async-start(), calls=%async_computation.5 | async-start | bytes 5898240 | tf_op jit(solution)/shard_map/all_gather | solution.py:959
  76.2 37.1 %collective-permute-start.7 = (bf16[1536,512]{1,0:T(8,128)(2,1)S(1)}, bf16[1536,512]{1,0:T(8,128)(2,1)S(1)}, u32[]{:S(2)}, u32[]{:S(2)}) collective-permute-start(bf16[1536,512]{1,0:T(8,128)(2,1)S(1)} %copy-done.33), channel_id=1, source_target_pairs={{0,4},{1,5},{2,6},{3,7},{8,12},{9,13},{10,14},{11,15},{16,20},{17,... | collective-permute-start | bytes 4718600 | tf_op jit(solution)/shard_map/ppermute | solution.py:908
  103.6 41.5 %collective-permute-start.14 = (bf16[1536,384]{1,0:T(8,128)(2,1)S(1)}, bf16[1536,384]{1,0:T(8,128)(2,1)S(1)}, u32[]{:S(2)}, u32[]{:S(2)}) collective-permute-start(bf16[1536,384]{1,0:T(8,128)(2,1)S(1)} %constant_dynamic-update-slice_fusion.refs_0_), channel_id=1, source_target_pairs={{0,16},{16,0},{8,24},{24,8},{1,17},{17,1},{9,25},{25,9},{2,18},{18... | collective-permute-start | bytes 3538952 | tf_op jit(solution)/shard_map/ppermute | solution.py:763
  105.3 41.5 %collective-permute-start.13 = (bf16[1536,384]{1,0:T(8,128)(2,1)S(1)}, bf16[1536,384]{1,0:T(8,128)(2,1)S(1)}, u32[]{:S(2)}, u32[]{:S(2)}) collective-permute-start(bf16[1536,384]{1,0:T(8,128)(2,1)S(1)} %constant_dynamic-update-slice_fusion.refs_0_), channel_id=1, source_target_pairs={{0,8},{8,0},{16,24},{24,16},{1,9},{9,1},{17,25},{25,17},{2,10},{10... | collective-permute-start | bytes 3538952 | tf_op jit(solution)/shard_map/ppermute | solution.py:760
  146.6 45.5 %collective-permute-start.18 = (bf16[2240,384]{1,0:T(8,128)(2,1)}, bf16[2240,384]{1,0:T(8,128)(2,1)}, u32[]{:S(2)}, u32[]{:S(2)}) collective-permute-start(bf16[2240,384]{1,0:T(8,128)(2,1)} %bitcast.29.own_ref), channel_id=1, source_target_pairs={{0,8},{8,0},{16,24},{24,16},{1,9},{9,1},{17,25},{25,17},{2,10},{10... | collective-permute-start | bytes 5160968 | tf_op jit(solution)/shard_map/ppermute | solution.py:760
  155.2 44.1 %collective-permute-start.16 = (bf16[384,1536]{1,0:T(8,128)(2,1)S(1)}, bf16[384,1536]{1,0:T(8,128)(2,1)}, u32[]{:S(2)}, u32[]{:S(2)}) collective-permute-start(bf16[384,1536]{1,0:T(8,128)(2,1)S(1)} %get-tuple-element.128.refs_1_), channel_id=1, source_target_pairs={{0,1},{1,2},{2,3},{3,0},{4,5},{5,6},{6,7},{7,4},{8,9},{9,10},{10,1... | collective-permute-start | bytes 3538952 | tf_op jit(solution)/shard_map/ppermute | solution.py:769
  155.2 36.9 %collective-permute-start.19 = (bf16[1120,384]{1,0:T(8,128)(2,1)}, bf16[1120,384]{1,0:T(8,128)(2,1)}, u32[]{:S(2)}, u32[]{:S(2)}) collective-permute-start(bf16[1120,384]{1,0:T(8,128)(2,1)} %collective-permute-done.10.near_ref), channel_id=1, source_target_pairs={{0,8},{8,0},{16,24},{24,16},{1,9},{9,1},{17,25},{25,17},{2,10},{10... | collective-permute-start | bytes 2580488 | tf_op jit(solution)/shard_map/ppermute | solution.py:760
  199.5 393.2 %reduce-scatter.4.cloned.1.call-start = ((), (), s32[]{:S(2)}) async-start(), calls=%async_computation.6 | async-start | bytes 7962624 | tf_op jit(solution)/shard_map/reduce_scatter | solution.py:822
  370.2 44.1 %collective-permute-start.27 = (bf16[384,1536]{1,0:T(8,128)(2,1)}, bf16[384,1536]{1,0:T(8,128)(2,1)}, u32[]{:S(2)}, u32[]{:S(2)}) collective-permute-start(bf16[384,1536]{1,0:T(8,128)(2,1)} %add_convert_fusion.4), channel_id=1, source_target_pairs={{0,1},{1,2},{2,3},{3,0},{4,5},{5,6},{6,7},{7,4},{8,9},{9,10},{10,1... | collective-permute-start | bytes 3538952 | tf_op jit(solution)/shard_map/ppermute | solution.py:769
  383.0 31.3 %collective-permute-start.29 = (bf16[384,384]{1,0:T(8,128)(2,1)}, bf16[384,384]{1,0:T(8,128)(2,1)}, u32[]{:S(2)}, u32[]{:S(2)}) collective-permute-start(bf16[384,384]{1,0:T(8,128)(2,1)} %get-tuple-element.251), channel_id=1, source_target_pairs={{0,2},{1,3},{2,0},{3,1},{4,6},{5,7},{6,4},{7,5},{8,10},{9,11},{10,... | collective-permute-start | bytes 884744 | tf_op jit(solution)/shard_map/ppermute | solution.py:769
  383.3 31.0 %collective-permute-start.33 = (bf16[2,2,768,128]{3,2,1,0:T(8,128)(2,1)}, bf16[2,2,768,128]{3,2,1,0:T(8,128)(2,1)}, u32[]{:S(2)}, u32[]{:S(2)}) collective-permute-start(bf16[2,2,768,128]{3,2,1,0:T(8,128)(2,1)} %get-tuple-element.173), channel_id=1, source_target_pairs={{4,0},{5,1},{6,2},{7,3},{12,8},{13,9},{14,10},{15,11},{20,16},{21,... | collective-permute-start | bytes 2359304 | tf_op jit(solution)/shard_map/ppermute | solution.py:997
  418.4 254.7 %reduce-scatter.8.cloned.1.call-start = ((), (), s32[]{:S(2)}) async-start(), calls=%async_computation.8 | async-start | bytes 7962624 | tf_op jit(solution)/shard_map/reduce_scatter | solution.py:822
  426.1 32.2 %collective-permute-start.34 = (bf16[384,1536]{1,0:T(8,128)(2,1)S(1)}, bf16[384,1536]{1,0:T(8,128)(2,1)}, u32[]{:S(2)}, u32[]{:S(2)}) collective-permute-start(bf16[384,1536]{1,0:T(8,128)(2,1)S(1)} %add_convert_fusion.3), channel_id=1, source_target_pairs={{0,1},{1,2},{2,3},{3,0},{4,5},{5,6},{6,7},{7,4},{8,9},{9,10},{10,1... | collective-permute-start | bytes 3538952 | tf_op jit(solution)/shard_map/ppermute | solution.py:769
  458.4 246.6 %reduce-scatter.6.cloned.1.call-start = ((), (), s32[]{:S(2)}) async-start(), calls=%async_computation.7 | async-start | bytes 7962624 | tf_op jit(solution)/shard_map/reduce_scatter | solution.py:822
  500.1 45.1 %collective-permute-start.41 = (bf16[384,1536]{1,0:T(8,128)(2,1)}, bf16[384,1536]{1,0:T(8,128)(2,1)}, u32[]{:S(2)}, u32[]{:S(2)}) collective-permute-start(bf16[384,1536]{1,0:T(8,128)(2,1)} %copy-done.13), channel_id=1, source_target_pairs={{0,1},{1,2},{2,3},{3,0},{4,5},{5,6},{6,7},{7,4},{8,9},{9,10},{10,1... | collective-permute-start | bytes 3538952 | tf_op jit(solution)/shard_map/ppermute | solution.py:769
  521.3 39.9 %collective-permute-start.42 = (bf16[1536,768]{0,1:T(8,128)(2,1)}, bf16[1536,768]{0,1:T(8,128)(2,1)}, u32[]{:S(2)}, u32[]{:S(2)}) collective-permute-start(bf16[1536,768]{0,1:T(8,128)(2,1)} %pad_maximum_fusion.1), channel_id=1, source_target_pairs={{0,8},{8,0},{16,24},{24,16},{1,9},{9,1},{17,25},{25,17},{2,10},{10... | collective-permute-start | bytes 7077896 | tf_op jit(solution)/shard_map/ppermute | solution.py:760
  592.6 38.4 %collective-permute-start.48 = (bf16[192,2240]{1,0:T(8,128)(2,1)}, bf16[192,2240]{1,0:T(8,128)(2,1)S(1)}, u32[]{:S(2)}, u32[]{:S(2)}) collective-permute-start(bf16[192,2240]{1,0:T(8,128)(2,1)} %reduce-scatter.4.cloned.1.call-done), channel_id=1, source_target_pairs={{0,4},{4,0},{1,5},{5,1},{2,6},{6,2},{3,7},{7,3},{8,12},{12,8},{9,1... | collective-permute-start | bytes 2580488 | tf_op jit(solution)/shard_map/ppermute | solution.py:766
  636.0 34.8 %collective-permute-start.49 = (bf16[384,1536]{1,0:T(8,128)(2,1)}, bf16[384,1536]{1,0:T(8,128)(2,1)}, u32[]{:S(2)}, u32[]{:S(2)}) collective-permute-start(bf16[384,1536]{1,0:T(8,128)(2,1)} %collective-permute-done.43.refs_1_), channel_id=1, source_target_pairs={{0,1},{1,2},{2,3},{3,0},{4,5},{5,6},{6,7},{7,4},{8,9},{9,10},{10,1... | collective-permute-start | bytes 3538952 | tf_op jit(solution)/shard_map/ppermute | solution.py:769
  637.3 30.9 %collective-permute-start.51 = (bf16[384,384]{0,1:T(8,128)(2,1)S(1)}, bf16[384,384]{0,1:T(8,128)(2,1)S(1)}, u32[]{:S(2)}, u32[]{:S(2)}) collective-permute-start(bf16[384,384]{0,1:T(8,128)(2,1)S(1)} %add_convert_fusion.17), channel_id=1, source_target_pairs={{0,1},{1,2},{2,3},{3,0},{4,5},{5,6},{6,7},{7,4},{8,9},{9,10},{10,1... | collective-permute-start | bytes 884744 | tf_op jit(solution)/shard_map/ppermute | solution.py:769
  637.9 32.1 %collective-permute-start.50 = (bf16[400,384]{1,0:T(8,128)(2,1)S(1)}, bf16[400,384]{1,0:T(8,128)(2,1)S(1)}, u32[]{:S(2)}, u32[]{:S(2)}) collective-permute-start(bf16[400,384]{1,0:T(8,128)(2,1)S(1)} %constant_dynamic-slice_fusion.4), channel_id=1, source_target_pairs={{0,16},{16,0},{8,24},{24,8},{1,17},{17,1},{9,25},{25,9},{2,18},{18... | collective-permute-start | bytes 921608 | tf_op jit(solution)/shard_map/ppermute | solution.py:763
  708.2 43.3 %collective-permute-start.59 = (bf16[384,1536]{1,0:T(8,128)(2,1)}, bf16[384,1536]{1,0:T(8,128)(2,1)}, u32[]{:S(2)}, u32[]{:S(2)}) collective-permute-start(bf16[384,1536]{1,0:T(8,128)(2,1)} %collective-permute-done.49.refs_2_), channel_id=1, source_target_pairs={{0,1},{1,2},{2,3},{3,0},{4,5},{5,6},{6,7},{7,4},{8,9},{9,10},{10,1... | collective-permute-start | bytes 3538952 | tf_op jit(solution)/shard_map/ppermute | solution.py:769
  (127 other events, 2152.9 us)
Sparse Core Ops, SparseCore 0:
  31.6 69.5 all-gather.3
  102.7 66.5 all-gather.5
  199.6 38.0 all-gather.7
  418.5 75.0 reduce-scatter.3
  498.0 65.4 reduce-scatter.7
  566.9 82.4 reduce-scatter.5

commit v4 on v3

--- a/solution.py
+++ b/solution.py
@@ -372,17 +372,28 @@
     )
 
 
+def output_pieces(meta, weights, tps):
+    own, other, near, far, other_near, other_far = weights
+    depth, half = own.shape[0], near.shape[0]
+    low = pl.multiple_of(meta[CTX] * (depth - half), 128)
+    high = pl.multiple_of((1 - meta[CTX]) * (depth - half), 128)
+    pieces = [(0, None, own), (1, None, other)]
+    if half == depth:
+        return pieces + [(2, None, near), (3, None, other_near)]
+    return pieces + [(2, low, near), (2, high, far), (3, low, other_near), (3, high, other_far)]
+
+
 def merge_kernel(tps, meta, o_ref, x_ref, *refs):
-    weights, (gain_ref, h_ref, n_ref, turned_ref) = refs[:4], refs[4:]
+    weights, (gain_ref, h_ref, n_ref, turned_ref) = refs[:6], refs[6:]
     rows, width = h_ref.shape
     size, depth = width // 4, o_ref.shape[1]
     part = depth // tps
     for hop in range(tps):
         turned_ref[:, hop * part : (hop + 1) * part] = o_ref[:, pl.ds(tp_at(meta, hop, tps, part), part)]
-    turned = turned_ref[...]
-    for flip, weight in enumerate(weights):
-        at = pl.ds(shard_at(meta, flip, size), size)
-        h_ref[:, at] = x_ref[0, :, at].astype(jnp.float32) + dot(turned, weight[...])
+    h_ref[...] = x_ref[...].reshape(rows, width).astype(jnp.float32)
+    for flip, first, weight in output_pieces(meta, weights, tps):
+        left = turned_ref[...] if first is None else turned_ref[:, pl.ds(first, weight.shape[0])]
+        h_ref[:, pl.ds(shard_at(meta, flip, size), size)] += dot(left, weight[...])
     hidden = h_ref[...]
     n_ref[...] = (hidden * root_of(hidden) * gain_ref[...]).astype(LOW)
 
@@ -414,7 +425,7 @@
 def turn_kernel(
     tps, meta, a_ref, b_ref, h_ref, c_ref, *refs,
 ):
-    weights, (gain_ref, hg_ref, bg_ref, ag_ref, term_ref, turned_ref) = refs[:4], refs[4:]
+    weights, (gain_ref, hg_ref, bg_ref, ag_ref, term_ref, turned_ref) = refs[:6], refs[6:]
     rows, width = h_ref.shape
     size, depth = width // 4, ag_ref.shape[1]
     two_grad = a_ref[...].astype(jnp.float32) + b_ref[...].astype(jnp.float32)
@@ -430,8 +441,9 @@
     hg_ref[...] = grad
     bg_ref[...] = grad.astype(LOW)
     turned_ref[...] = jnp.zeros_like(turned_ref)
-    for flip, weight in enumerate(weights):
-        turned_ref[...] += inner_cols(bg_ref[:, pl.ds(shard_at(meta, flip, size), size)], weight[...])
+    for flip, first, weight in output_pieces(meta, weights, tps):
+        at = slice(None) if first is None else pl.ds(first, weight.shape[0])
+        turned_ref[:, at] += inner_cols(bg_ref[:, pl.ds(shard_at(meta, flip, size), size)], weight[...])
     part = depth // tps
     for hop in range(tps):
         ag_ref[:, pl.ds(tp_at(meta, hop, tps, part), part)] = turned_ref[
@@ -639,12 +651,13 @@
         mix_ref[...] = (mix_acc[...] + mix).astype(LOW)
 
 
-def feed(meta, normed, cots, gate, up, down, hop, tps, kept):
+def feed(meta, normed, cots, gate_down, up, hop, tps, kept):
     rows, width = normed.shape
-    hidden = down.shape[0]
+    hidden = up.shape[1]
     tile = 768
     assert hidden > tile
-    weight = pl.BlockSpec((tile, width), lambda j, m: (j, 0))
+    gate_spec = pl.BlockSpec((None, tile, width), lambda j, m: (0, j, 0))
+    down_spec = pl.BlockSpec((None, tile, width), lambda j, m: (1, j, 0))
     column = pl.BlockSpec((rows, tile), lambda j, m: (hop, j))
     fixed = pl.BlockSpec((rows, width), lambda j, m: (0, 0))
     first = hop == 0
@@ -654,7 +667,7 @@
         grid_spec=pltpu.PrefetchScalarGridSpec(
             num_scalar_prefetch=1,
             grid=(-(-hidden // tile),),
-            in_specs=[fixed, pl.BlockSpec((rows, width), lambda j, m: (hop, 0)), weight, weight, weight]
+            in_specs=[fixed, pl.BlockSpec((rows, width), lambda j, m: (hop, 0)), gate_spec, gate_spec, down_spec]
             + ([] if first else [pl.BlockSpec(memory_space=pl.ANY)] * 3),
             out_specs=[column, column, column, fixed, fixed],
             scratch_shapes=[pltpu.VMEM((rows, width), jnp.float32)] * 2,
@@ -666,7 +679,7 @@
             flops=12 * rows * width * hidden, bytes_accessed=6 * width * hidden, transcendentals=rows * hidden
         ),
         name="feed",
-    )(meta, normed, cots, gate, up, down, *(() if first else kept))
+    )(meta, normed, cots, gate_down, up, gate_down, *(() if first else kept))
     return hiddens, two_part, mixed_part
 
 
@@ -821,9 +834,13 @@
     def reduce_weight(self, term):
         part = lax.psum_scatter(term, ("fsdp", "ctx"), scatter_dimension=0, tiled=True)
         if self.ctxs != 2:
-            return lax.all_gather(part, "ctx", axis=0, tiled=True).astype(jnp.float32).T
+            return lax.all_gather(part, "ctx", axis=0, tiled=True), None
         part = lax.optimization_barrier(part)
-        got = self.to_y(part)
+        return part, self.to_y(part)
+
+    def lay_weight(self, part, got):
+        if got is None:
+            return part.astype(jnp.float32).T
         return lay(jnp.where(self.ctx == 0, part, got), jnp.where(self.ctx == 0, got, part))
 
 
@@ -923,14 +940,18 @@
 
     queries = jnp.stack(swap(lambda d: lax.dynamic_index_in_dim(query_blocks, d, 0, keepdims=False)))
 
-    def gather_whole(item):
-        return lax.all_gather(after(item, pack_across), "fsdp", axis=1, tiled=True)
-
-    gate_full, down_full = gather_whole(gate_weight.T), gather_whole(down_weight)
+    def gather_whole(*items):
+        return lax.all_gather(after(jnp.stack(items), pack_across), "fsdp", axis=2, tiled=True)
+
+    gate_down = gather_whole(gate_weight.T, down_weight)
     o_blocks = o_blocks[:2] + [after(item, kv_own) for item in o_blocks[2:]]
     o_wide = jnp.concatenate(o_blocks, axis=0)
     q_blocks = links.gather_tp(after(query_weight, kv_own))
-    o_across = links.to_x(o_wide)
+    if ctxs == 2:
+        o_near = links.to_x(lax.dynamic_slice_in_dim(o_wide, ctx * (depth // 2), depth // 2, 0))
+        o_far = links.to_y(after(o_near, kv_before))
+    else:
+        o_near = o_far = links.to_x(o_wide)
     o_core = links.to_core(after(o_wide, queries))
 
     late_cot = after(cotangent, kv_own)
@@ -943,22 +964,20 @@
     order = after(order, (cot_all, one_all, q_blocks[2], *([up_near] if ctxs == 2 else [])))
     sizes = (seq_count, kv_heads, head_dim, tps)
     mixed, lse = attend(meta, queries, kv_before, kv_own, order, key_block, sizes)
-    o_core_across = links.to_core(after(o_across, mixed))
-    o_parts = (o_wide, o_core, o_across, o_core_across)
+    o_core_near, o_core_far = (
+        links.to_core(after(item, (mixed, q_blocks[-1]))) for item in (o_near, o_far)
+    )
+    o_parts = (o_wide, o_core, o_near, o_far, o_core_near, o_core_far)
     hidden, normed_two = merge(meta, mixed, inputs, o_parts, mlp_gamma, tps)
     two_blocks = [normed_two, links.hop_tp(normed_two)]
-    q_wide = jnp.zeros((query_weight.shape[0], depth), LOW)
-    for hop, item in enumerate(q_blocks):
-        q_wide = lax.dynamic_update_slice_in_dim(q_wide, item, links.at(hop) * q_cols, 1)
     if ctxs == 2:
         up_cores = [links.to_core(after(item, mixed)) for item in (up_mine, up_near)]
         up_cores.append(links.to_core(after(up_far, normed_two)))
-        up_full = assemble(meta, up_mine, up_near, up_far, *up_cores)
+        up_full = assemble(meta, up_mine, up_near, up_far, *up_cores)[None]
     else:
         up_full = gather_whole(up_mine)
-    q_full = lax.all_gather(after(q_wide, down_full), "fsdp", axis=0, tiled=True)
-
-    two_blocks.append(links.hop_tp(after(two_blocks[-1], (gate_full, up_full, down_full))))
+
+    two_blocks.append(links.hop_tp(after(two_blocks[-1], (gate_down, up_full))))
     two_blocks.append(links.hop_tp(two_blocks[-1]))
     kept, two_parts, mixed_parts, two_total = None, [], [], None
     for hop in range(tps):
@@ -968,10 +987,15 @@
         if two_total is not None:
             block = after(block, two_total)
         kept, two_part, mixed_part = feed(
-            meta, block, cot_all, gate_full, up_full, down_full, hop, tps, kept
+            meta, block, cot_all, gate_down, up_full, hop, tps, kept
         )
         two_parts.append(two_part)
         mixed_parts.append(mixed_part)
+        if hop == 0:
+            q_wide = jnp.zeros((query_weight.shape[0], depth), LOW)
+            for back, item in enumerate(q_blocks):
+                q_wide = lax.dynamic_update_slice_in_dim(q_wide, item, links.at(back) * q_cols, 1)
+            q_full = lax.all_gather(q_wide, "fsdp", axis=0, tiled=True)
         if hop >= 1:
             two_total = two_part if hop == 1 else add_low(two_part, two_got)
             two_got = links.hop_tp(two_total)
@@ -980,7 +1004,7 @@
     act_all, gate_all, up_all = kept
     two_all = jnp.concatenate(two_blocks, axis=0)
     down_term = inner_rows(cot_all, after(act_all, two_total)).astype(LOW)
-    two_got = after(two_got, down_term)
+    two_got = after(two_got, (down_term, two_all))
 
     hidden_grad, branch_grad, attended_grad, mlp_term = turn(
         meta, two_own, two_got, hidden, cotangent, o_parts, mlp_gamma, depth, tps
@@ -1028,26 +1052,26 @@
 
     kv_mine, kv_next = kv_rows(0), kv_rows(1)
     mixed_next = add_low(mixed_parts[3], mixed_got)
-    mixed_got = links.hop_tp(after(mixed_next, (shares, kv_next, input_low, output_pairs)))
-    kv_got = links.hop_tp(kv_next)
+    mixed_got = links.hop_tp(after(mixed_next, shares))
+    kv_got = links.hop_tp(after(kv_next, (input_low, output_pairs)))
+    down_weight_grad = links.lay_weight(*links.reduce_weight(after(down_term, kv_next)))
+    kv_next = add_low(kv_rows(2), kv_got)
     gate_term = inner_rows(two_all, after(gate_all, kv_next)).astype(LOW)
-    down_weight_grad = links.reduce_weight(after(down_term, kv_next))
-    kv_next = add_low(kv_rows(2), kv_got)
 
     in_blocks = [input_low, links.hop_tp(after(input_low, (mixed_got, kv_next, gate_term)))]
-    kv_got = links.hop_tp(kv_next)
-    gate_weight_grad = links.reduce_weight(after(gate_term, mixed_got)).T
-    up_term = inner_rows(two_all, after(up_all, (mixed_got, gate_term))).astype(LOW)
+    kv_got = links.hop_tp(after(kv_next, mixed_got))
+    gate_weight_grad = links.lay_weight(*links.reduce_weight(after(gate_term, mixed_got))).T
     output_both = links.scatter_core(after(output_pairs, mixed_got))
-    kv_next = add_low(kv_rows(3), kv_got)
+    up_term = inner_rows(two_all, after(up_all, mixed_got)).astype(LOW)
+    kv_next = add_low(kv_rows(3), after(kv_got, up_term))
     out_low = hidden + mixed_parts[0].astype(jnp.float32) + mixed_got.astype(jnp.float32)
     out_low = lax.optimization_barrier(out_low.astype(LOW))
 
-    out_blocks = [out_low, links.hop_tp(after(out_low, (in_blocks[1], kv_next, up_term, output_both)))]
-    kv_got = links.hop_tp(kv_next)
-    up_weight_grad = links.reduce_weight(after(up_term, in_blocks[1])).T
+    out_blocks = [out_low, links.hop_tp(after(out_low, (in_blocks[1], kv_next)))]
+    kv_got = links.hop_tp(after(kv_next, in_blocks[1]))
+    up_part, up_got = links.reduce_weight(after(up_term, in_blocks[1]))
     output_part = links.scatter_x(after(output_both, in_blocks[1]), 1)
-    grads_all = after(jnp.concatenate(shares, axis=0), in_blocks[1])
+    grads_all = after(jnp.concatenate(shares, axis=0), kv_got)
     q_bias_row = jnp.sum(grads_all.astype(jnp.float32), axis=0, keepdims=True)
     q_below = jnp.pad(q_bias_row, ((0, 15), (0, 0))).astype(LOW)
     q_pairs = links.pairs(fsdp_rows(inner_rows(one_all, grads_all).astype(LOW), lambda j: q_below), 0)
@@ -1059,27 +1083,27 @@
     kv_blocks = [jnp.concatenate([kv_grad, gain_terms], axis=0)]
 
     in_blocks.append(links.hop_tp(after(in_blocks[1], (out_blocks[1], kv_blocks[0], q_pairs))))
-    kv_blocks.append(links.hop_tp(kv_blocks[0]))
+    kv_blocks.append(links.hop_tp(after(kv_blocks[0], out_blocks[1])))
     q_both = links.scatter_core(after(q_pairs, out_blocks[1]))
-    output_got = links.hop_tp(after(output_rows(1), out_blocks[1]))
-    output_next = add_low(output_rows(2), output_got)
 
     out_blocks.append(
         links.hop_tp(
-            after(out_blocks[1], (in_blocks[2], kv_blocks[1], q_both, output_next, down_weight_grad))
+            after(out_blocks[1], (in_blocks[2], kv_blocks[1], q_both))
         )
     )
-    kv_blocks.append(links.hop_tp(kv_blocks[1]))
+    kv_blocks.append(links.hop_tp(after(kv_blocks[1], in_blocks[2])))
     q_part = links.scatter_x(after(q_both, in_blocks[2]), 0)
-    output_got = links.hop_tp(after(output_next, in_blocks[2]))
-    output_next = add_low(output_rows(3), output_got)
+    output_got = links.hop_tp(after(output_rows(1), in_blocks[2]))
+    output_next = add_low(output_rows(2), output_got)
 
     in_blocks.append(
         links.hop_tp(after(in_blocks[2], (out_blocks[2], kv_blocks[2], q_part, output_next)))
     )
-    kv_blocks.append(links.hop_tp(kv_blocks[2]))
+    kv_blocks.append(links.hop_tp(after(kv_blocks[2], (out_blocks[2], down_weight_grad))))
     q_total = links.sum_ctx(after(q_part, out_blocks[2]))
     output_got = links.hop_tp(after(output_next, out_blocks[2]))
+    output_next = add_low(output_rows(3), output_got)
+    output_got = links.hop_tp(after(output_next, in_blocks[3]))
     output_sum = add_low(output_rows(0), output_got)
     own_tokens = seq_count * own
     kv_all = jnp.concatenate([item[:own_tokens] for item in kv_blocks], axis=0)
@@ -1096,16 +1120,17 @@
 
     out_blocks.append(
         links.hop_tp(
-            after(out_blocks[2], (in_blocks[3], kv_pairs, q_total, output_sum, gate_weight_grad))
+            after(out_blocks[2], (in_blocks[3], kv_pairs))
         )
     )
-    kv_both = links.scatter_core(after(kv_pairs, in_blocks[3]))
-    output_weight_grad = links.sum_ctx(after(output_sum, in_blocks[3]))
-    kv_part = links.scatter_x(kv_both, 0)
-    in_blocks[0] = after(in_blocks[0], kv_both)
+    kv_both = links.scatter_core(kv_pairs)
+    output_weight_grad = links.sum_ctx(output_sum)
     input_grad = last(meta, in_blocks, kv_blocks, qkv, inputs, attn_gamma)
-    out_blocks[0] = after(out_blocks[0], (kv_part, input_grad, up_weight_grad))
-    kv_total = links.sum_ctx(kv_part)
+    kv_part = links.scatter_x(after(kv_both, (in_blocks[3], gate_weight_grad)), 0)
+    up_part = after(up_part, (input_grad, out_blocks[3]))
+    up_weight_grad = links.lay_weight(up_part, up_got).T
+    out_blocks[0] = after(out_blocks[0], (output_sum, q_total))
+    kv_total = links.sum_ctx(after(kv_part, input_grad))
     outputs = spread_out(meta, out_blocks, seq_count, LOW)
     query_weight_grad = q_total[:shard]
     part = head_dim // fsdps

time: 776 us -> 734 us (0.946)
  waiting for transfers between devices: 291 us -> 234 us
  starting transfers between devices: 66.5 us -> 88.4 us
  local copies, waits for them, and re-layouts: 68.2 us -> 57.1 us
    ppermute x36, waiting for transfers between devices: 209 us -> 169 us  [hop_tp(): lax.ppermute(value, 'tp', [(i, (i + hop) % self.tps) for i in range(self....]
    ppermute x7 -> x8, starting transfers between devices: 16.9 us -> 39.3 us  [to_y(): return lax.ppermute(value, 'ctx', [(0, 1), (1, 0)])]
    ppermute x7 -> x8, waiting for transfers between devices: 40.1 us -> 27.5 us  [to_y(): return lax.ppermute(value, 'ctx', [(0, 1), (1, 0)])]
    unnamed x203 -> x185, local copies, waits for them, and re-layouts: 36.7 us -> 25.2 us
  transfers between devices with their start and end apart: 68 -> 69, of which waited for: 32 -> 33; matrix products, arithmetic and copies ran while one was open for 21% -> 22% of each run, Pallas kernels for 26% -> 28%
where the time goes in v4:
time: 734 us; the launch traced here: 725 us
  waiting for transfers between devices  234 us (32%)
  Pallas kernels  204 us (28%)
  starting transfers between devices  88.4 us (12%)
  matrix products  65.5 us (9%)
  other arithmetic  60.3 us (8%)
  local copies, waits for them, and re-layouts  57.1 us (8%)
  between operations  15.6 us (2%)
    ppermute x36, waiting for transfers between devices, hop_tp(): lax.ppermute(value, 'tp', [(i, (i + hop) % self.tps) for i in range(self....  169 us
    pallas_call x4, Pallas kernels, feed(): pl.pallas_call(functools.partial(feed_kernel, first, hidden), grid_spec=p...  104 us
    dot_general x6, matrix products, inner_rows(): lax.dot_general(left, right, (((0,), (0,)), ((), ())), preferred_element_...  65.5 us
    ppermute x8, starting transfers between devices, to_y(): return lax.ppermute(value, 'ctx', [(0, 1), (1, 0)])  39.3 us
    ppermute x6, waiting for transfers between devices, to_x(): return lax.ppermute(value, 'fsdp', [(0, 2), (2, 0), (1, 3), (3, 1)])  34.9 us
    ppermute x36, starting transfers between devices, hop_tp(): lax.ppermute(value, 'tp', [(i, (i + hop) % self.tps) for i in range(self....  33.8 us
    ppermute x8, waiting for transfers between devices, to_y(): return lax.ppermute(value, 'ctx', [(0, 1), (1, 0)])  27.5 us
    convert_element_type x17, other arithmetic, add_low(): return (left.astype(jnp.float32) + right.astype(jnp.float32)).astype(LOW)  26.8 us
  transfers between devices with their start and end apart: 69, of which 33 were waited for; matrix products, arithmetic and copies ran while one was open for 22% of the time, Pallas kernels for 28%

profile of v4, /device:TPU:0, one launch (start us, length us, event | category | flops | bytes accessed | tf_op | source)
XLA Modules:
  0.0 724.9 jit_solution(17133866340679853325)
XLA Ops:
  19.3 12.0 %collective-permute-done.1.refs_2_.refs_10_ = bf16[400,896]{1,0:T(8,128)(2,1)} collective-permute-done((bf16[400,896]{1,0:T(8,128)(2,1)S(1)}, bf16[400,896]{1,0:T(8,128)(2,1)}, u32[]{:S(2)}, u32[]{:S(2)}) %collective-permute-start.1) | collective-permute-done | bytes 716832 | tf_op jit(solution)/shard_map/ppermute | solution.py:776
  45.6 8.4 %collective-permute-done.11 = bf16[384,384]{1,0:T(8,128)(2,1)} collective-permute-done((bf16[384,384]{1,0:T(8,128)(2,1)}, bf16[384,384]{1,0:T(8,128)(2,1)}, u32[]{:S(2)}, u32[]{:S(2)}) %collective-permute-start.11) | collective-permute-done | bytes 294944 | tf_op jit(solution)/shard_map/ppermute | solution.py:782
  58.1 13.6 %project.1 = (bf16[1536,1536]{1,0:T(8,128)(2,1)}, bf16[4,384,384]{2,1,0:T(8,128)(2,1)S(1)}, bf16[1536,512]{1,0:T(8,128)(2,1)}) custom-call(s32[6]{0:T(128)S(1)} %stack.109.meta.refs_0_, bf16[2,768,1536]{2,1,0:T(8,128)(2,1)} %refs_12_.1, f32[1,1536]{1,0:T(1,128)S(1)} %maximum_convert_fusion.gain_ref.refs_13_, f32[1,896]{1,0:T(1,128)S(1)} %bitcast.95, ...), custom_call_target="tpu_custom_call" | custom-call | flops 4227858432 | bytes 18874368 | tf_op jit(solution)/shard_map/project/pallas_call | solution.py:131
  89.1 14.1 %collective-permute-done.5 = bf16[384,384]{1,0:T(8,128)(2,1)S(1)} collective-permute-done((bf16[384,384]{1,0:T(8,128)(2,1)S(1)}, bf16[384,384]{1,0:T(8,128)(2,1)S(1)}, u32[]{:S(2)}, u32[]{:S(2)}) %collective-permute-start.5) | collective-permute-done | bytes 294944 | tf_op jit(solution)/shard_map/ppermute | solution.py:782
  112.9 18.3 %collective-permute-done.14.refs_2_ = bf16[768,384]{1,0:T(8,128)(2,1)S(1)} collective-permute-done((bf16[768,384]{1,0:T(8,128)(2,1)S(1)}, bf16[768,384]{1,0:T(8,128)(2,1)S(1)}, u32[]{:S(2)}, u32[]{:S(2)}) %collective-permute-start.14) | collective-permute-done | bytes 589856 | tf_op jit(solution)/shard_map/ppermute | solution.py:776
  158.6 11.5 %collective-permute-done.20.far_ref = bf16[1120,384]{1,0:T(8,128)(2,1)} collective-permute-done((bf16[1120,384]{1,0:T(8,128)(2,1)}, bf16[1120,384]{1,0:T(8,128)(2,1)}, u32[]{:S(2)}, u32[]{:S(2)}) %collective-permute-start.20) | collective-permute-done | bytes 860192 | tf_op jit(solution)/shard_map/ppermute | solution.py:779
  190.8 25.8 %feed.4 = (bf16[1536,2240]{1,0:T(8,128)(2,1)}, bf16[1536,2240]{1,0:T(8,128)(2,1)}, bf16[1536,2240]{1,0:T(8,128)(2,1)}, bf16[384,1536]{1,0:T(8,128)(2,1)}, bf16[384,1536]{1,0:T(8,128)(2,1)}) custom-call(s32[6]{0:T(128)} %copy-done.25, bf16[384,1536]{1,0:T(8,128)(2,1)} %get-tuple-element.136.refs_1_, bf16[1536,1536]{1,0:T(8,128)(2,1)} %copy-done.30, ...), custom_call_target="tpu_custom_call" | custom-call | flops 15854469120 | bytes 20643840 | tf_op jit(solution)/shard_map/feed/pallas_call | solution.py:665
  220.5 26.1 %feed.5 = (bf16[1536,2240]{1,0:T(8,128)(2,1)}, bf16[1536,2240]{1,0:T(8,128)(2,1)}, bf16[1536,2240]{1,0:T(8,128)(2,1)}, bf16[384,1536]{1,0:T(8,128)(2,1)}, bf16[384,1536]{1,0:T(8,128)(2,1)}) custom-call(s32[6]{0:T(128)} %copy-done.25, bf16[384,1536]{1,0:T(8,128)(2,1)} %collective-permute-done.19.refs_1_, ...), custom_call_target="tpu_custom_call", output_to_operand_aliasing={{0}: (6, {}), {1}: (7, {}), {2}: (8, {})} | custom-call | flops 15854469120 | bytes 20643840 | tf_op jit(solution)/shard_map/feed/pallas_call | solution.py:665
  249.0 25.7 %feed.6 = (bf16[1536,2240]{1,0:T(8,128)(2,1)}, bf16[1536,2240]{1,0:T(8,128)(2,1)}, bf16[1536,2240]{1,0:T(8,128)(2,1)}, bf16[384,1536]{1,0:T(8,128)(2,1)}, bf16[384,1536]{1,0:T(8,128)(2,1)}) custom-call(s32[6]{0:T(128)} %copy-done.25, bf16[384,1536]{1,0:T(8,128)(2,1)} %copy-done.41, ...), custom_call_target="tpu_custom_call", output_to_operand_aliasing={{0}: (6, {}), {1}: (7, {}), {2}: (8, {})} | custom-call | flops 15854469120 | bytes 20643840 | tf_op jit(solution)/shard_map/feed/pallas_call | solution.py:665
  279.5 26.2 %feed.7 = (bf16[1536,2240]{1,0:T(8,128)(2,1)}, bf16[1536,2240]{1,0:T(8,128)(2,1)}, bf16[1536,2240]{1,0:T(8,128)(2,1)}, bf16[384,1536]{1,0:T(8,128)(2,1)}, bf16[384,1536]{1,0:T(8,128)(2,1)}) custom-call(s32[6]{0:T(128)} %copy-done.25, bf16[384,1536]{1,0:T(8,128)(2,1)} %copy-done.39, ...), custom_call_target="tpu_custom_call", output_to_operand_aliasing={{0}: (6, {}), {1}: (7, {}), {2}: (8, {})} | custom-call | flops 15854469120 | bytes 20643840 | tf_op jit(solution)/shard_map/feed/pallas_call | solution.py:665
  313.0 16.2 %convolution_convert_fusion.2 = bf16[1536,2240]{1,0:T(8,128)(2,1)} fusion(bf16[1536,1536]{1,0:T(8,128)(2,1)S(1)} %bitcast.101, bf16[1536,2240]{1,0:T(8,128)(2,1)} %get-tuple-element.163), kind=kOutput, calls=%fused_computation.2 | convolution fusion | flops 10573086720 | bytes 18481152 | tf_op jit(solution)/shard_map/dot_general | solution.py:35
  329.2 8.7 %collective-permute-done.28.b_ref = bf16[384,1536]{1,0:T(8,128)(2,1)} collective-permute-done((bf16[384,1536]{1,0:T(8,128)(2,1)}, bf16[384,1536]{1,0:T(8,128)(2,1)}, u32[]{:S(2)}, u32[]{:S(2)}) %collective-permute-start.28) | collective-permute-done | bytes 1179680 | tf_op jit(solution)/shard_map/ppermute | solution.py:782
  342.6 10.1 %turn.1 = (f32[384,1536]{1,0:T(8,128)}, bf16[384,1536]{1,0:T(8,128)(2,1)S(1)}, bf16[384,1536]{1,0:T(8,128)(2,1)S(1)}, f32[2,1,1536]{2,1,0:T(1,128)S(1)}) custom-call(s32[6]{0:T(128)S(1)} %copy-done.26, bf16[384,1536]{1,0:T(8,128)(2,1)S(1)} %copy-done.13, bf16[384,1536]{1,0:T(8,128)(2,1)} %collective-permute-done.28.b_ref, ...), custom_call_target="tpu_custom_call" | custom-call | flops 1811939328 | bytes 8388608 | tf_op jit(solution)/shard_map/turn/pallas_call | solution.py:459
  367.5 10.2 %attend_back.3 = (bf16[192,1536]{1,0:T(8,128)(2,1)S(1)}, bf16[2,2,768,128]{3,2,1,0:T(8,128)(2,1)}, bf16[2,2,768,128]{3,2,1,0:T(8,128)(2,1)S(1)}) custom-call(s32[6]{0:T(128)S(1)} %copy-done.26, bf16[4,384,384]{2,1,0:T(8,128)(2,1)S(1)} %copy-done.18, bf16[4,384,384]{2,1,0:T(8,128)(2,1)S(1)} %copy-done.18, bf16[1536,512]{1,0:T(8,128)(2,1)} %copy-done.28, ...), custom_call_target="tpu_custom_call" | custom-call | flops 7247757312 | bytes 4194304 | tf_op jit(solution)/shard_map/attend_back/pallas_call | solution.py:341
  404.9 8.4 %collective-permute-done.32 = bf16[384,384]{1,0:T(8,128)(2,1)} collective-permute-done((bf16[384,384]{1,0:T(8,128)(2,1)}, bf16[384,384]{1,0:T(8,128)(2,1)}, u32[]{:S(2)}, u32[]{:S(2)}) %collective-permute-start.32) | collective-permute-done | bytes 294944 | tf_op jit(solution)/shard_map/ppermute | solution.py:782
  436.1 18.6 %convolution_convert_fusion.1 = bf16[1536,2240]{1,0:T(8,128)(2,1)} fusion(bf16[1536,1536]{1,0:T(8,128)(2,1)} %constant_dynamic-update-slice_fusion.4, bf16[1536,2240]{1,0:T(8,128)(2,1)} %get-tuple-element.189), kind=kOutput, calls=%fused_computation.1 | convolution fusion | flops 10573086720 | bytes 18481152 | tf_op jit(solution)/shard_map/dot_general | solution.py:35
  466.9 17.0 %convolution_convert_fusion = bf16[1536,2240]{1,0:T(8,128)(2,1)} fusion(bf16[1536,1536]{1,0:T(8,128)(2,1)} %constant_dynamic-update-slice_fusion.4, bf16[1536,2240]{1,0:T(8,128)(2,1)} %get-tuple-element.194), kind=kOutput, calls=%fused_computation | convolution fusion | flops 10573086720 | bytes 18481152 | tf_op jit(solution)/shard_map/dot_general | solution.py:35
  483.8 17.6 %collective-permute-done.41 = bf16[2,2,2,192,128]{4,3,2,1,0:T(8,128)(2,1)} collective-permute-done((bf16[2,2,2,192,128]{4,3,2,1,0:T(8,128)(2,1)}, bf16[2,2,2,192,128]{4,3,2,1,0:T(8,128)(2,1)}, u32[]{:S(2)}, u32[]{:S(2)}) %collective-permute-start.41) | collective-permute-done | bytes 393248 | tf_op jit(solution)/shard_map/ppermute | solution.py:782
  508.0 9.6 %collective-permute-done.43.b_ref = bf16[2,2,2,192,128]{4,3,2,1,0:T(8,128)(2,1)} collective-permute-done((bf16[2,2,2,192,128]{4,3,2,1,0:T(8,128)(2,1)}, bf16[2,2,2,192,128]{4,3,2,1,0:T(8,128)(2,1)}, u32[]{:S(2)}, u32[]{:S(2)}) %collective-permute-start.43) | collective-permute-done | bytes 393248 | tf_op jit(solution)/shard_map/ppermute | solution.py:782
  547.9 28.0 %collective-permute-done.46.refs_5_ = bf16[400,512]{1,0:T(8,128)(2,1)S(1)} collective-permute-done((bf16[400,512]{1,0:T(8,128)(2,1)S(1)}, bf16[400,512]{1,0:T(8,128)(2,1)S(1)}, u32[]{:S(2)}, u32[]{:S(2)}) %collective-permute-start.46) | collective-permute-done | bytes 409632 | tf_op jit(solution)/shard_map/ppermute | solution.py:782
  595.6 17.8 %collective-permute-done.45 = bf16[384,384]{0,1:T(8,128)(2,1)S(1)} collective-permute-done((bf16[384,384]{0,1:T(8,128)(2,1)S(1)}, bf16[384,384]{0,1:T(8,128)(2,1)S(1)}, u32[]{:S(2)}, u32[]{:S(2)}) %collective-permute-start.45) | collective-permute-done | bytes 294944 | tf_op jit(solution)/shard_map/ppermute | solution.py:782
  623.6 8.8 %collective-permute-start.54 = (bf16[400,384]{1,0:T(8,128)(2,1)}, bf16[400,384]{1,0:T(8,128)(2,1)}, u32[]{:S(2)}, u32[]{:S(2)}) collective-permute-start(bf16[400,384]{1,0:T(8,128)(2,1)} %add_convert_fusion.14), channel_id=1, source_target_pairs={{0,4},{4,0},{1,5},{5,1},{2,6},{6,2},{3,7},{7,3},{8,12},{12,8},{9,1... | collective-permute-start | bytes 921608 | tf_op jit(solution)/shard_map/ppermute | solution.py:779
  671.5 9.2 %collective-permute-start.62 = (bf16[384,384]{0,1:T(8,128)(2,1)}, bf16[384,384]{0,1:T(8,128)(2,1)}, u32[]{:S(2)}, u32[]{:S(2)}) collective-permute-start(bf16[384,384]{0,1:T(8,128)(2,1)} %add_convert_fusion.15), channel_id=1, source_target_pairs={{0,4},{4,0},{1,5},{5,1},{2,6},{6,2},{3,7},{7,3},{8,12},{12,8},{9,1... | collective-permute-start | bytes 884744 | tf_op jit(solution)/shard_map/ppermute | solution.py:779
  680.8 13.3 %last.1 = f32[2,768,1536]{2,1,0:T(8,128)} custom-call(s32[6]{0:T(128)S(1)} %copy-done.26, bf16[384,1536]{1,0:T(8,128)(2,1)S(1)} %copy-done.16, bf16[384,1536]{1,0:T(8,128)(2,1)} %collective-permute-done.39.refs_1_, bf16[384,1536]{1,0:T(8,128)(2,1)} %collective-permute-done.44.refs_2_, bf16[384,1536]{1,0:T(8,128)(2,1)} %collective-permute-done.52.refs_3_, ...), custom_call_target="tpu_custom_call" | custom-call | flops 2415919104 | bytes 16777216 | tf_op jit(solution)/shard_map/last/pallas_call | solution.py:599
  (456 shorter events, 334.3 us)
Async XLA Ops:
  7.2 183.6 %all-gather.3.cloned.1.call-start = ((), (), s32[]{:S(2)}) async-start(), calls=%async_computation.3 | async-start | bytes 17203200 | tf_op jit(solution)/shard_map/all_gather | solution.py:944
  31.4 356.9 %all-gather.5.cloned.1.call-start = ((), (), s32[]{:S(2)}) async-start(), calls=%async_computation.4 | async-start | bytes 5898240 | tf_op jit(solution)/shard_map/all_gather | solution.py:998
  54.0 52.0 %collective-permute-start.10 = (bf16[1120,384]{1,0:T(8,128)(2,1)}, bf16[1120,384]{1,0:T(8,128)(2,1)}, u32[]{:S(2)}, u32[]{:S(2)}) collective-permute-start(bf16[1120,384]{1,0:T(8,128)(2,1)} %dynamic-slice_bitcast_fusion), channel_id=1, source_target_pairs={{0,16},{16,0},{8,24},{24,8},{1,17},{17,1},{9,25},{25,9},{2,18},{18... | collective-permute-start | bytes 2580488 | tf_op jit(solution)/shard_map/ppermute | solution.py:776
  75.7 55.4 %collective-permute-start.7 = (bf16[1536,512]{1,0:T(8,128)(2,1)S(1)}, bf16[1536,512]{1,0:T(8,128)(2,1)S(1)}, u32[]{:S(2)}, u32[]{:S(2)}) collective-permute-start(bf16[1536,512]{1,0:T(8,128)(2,1)S(1)} %copy-done.27), channel_id=1, source_target_pairs={{0,4},{1,5},{2,6},{3,7},{8,12},{9,13},{10,14},{11,15},{16,20},{17,... | collective-permute-start | bytes 4718600 | tf_op jit(solution)/shard_map/ppermute | solution.py:925
  106.0 44.3 %collective-permute-start.13 = (bf16[1536,384]{1,0:T(8,128)(2,1)S(1)}, bf16[1536,384]{1,0:T(8,128)(2,1)S(1)}, u32[]{:S(2)}, u32[]{:S(2)}) collective-permute-start(bf16[1536,384]{1,0:T(8,128)(2,1)S(1)} %constant_dynamic-update-slice_fusion.refs_0_), channel_id=1, source_target_pairs={{0,8},{8,0},{16,24},{24,16},{1,9},{9,1},{17,25},{25,17},{2,10},{10... | collective-permute-start | bytes 3538952 | tf_op jit(solution)/shard_map/ppermute | solution.py:773
  157.9 30.6 %collective-permute-start.19 = (bf16[384,1536]{1,0:T(8,128)(2,1)}, bf16[384,1536]{1,0:T(8,128)(2,1)}, u32[]{:S(2)}, u32[]{:S(2)}) collective-permute-start(bf16[384,1536]{1,0:T(8,128)(2,1)} %get-tuple-element.136.refs_1_), channel_id=1, source_target_pairs={{0,1},{1,2},{2,3},{3,0},{4,5},{5,6},{6,7},{7,4},{8,9},{9,10},{10,1... | collective-permute-start | bytes 3538952 | tf_op jit(solution)/shard_map/ppermute | solution.py:782
  175.2 408.5 %reduce-scatter.4.cloned.1.call-start = ((), (), s32[]{:S(2)}) async-start(), calls=%async_computation.5 | async-start | bytes 7962624 | tf_op jit(solution)/shard_map/reduce_scatter | solution.py:835
  361.0 37.9 %collective-permute-start.36 = (bf16[2,2,768,128]{3,2,1,0:T(8,128)(2,1)}, bf16[2,2,768,128]{3,2,1,0:T(8,128)(2,1)}, u32[]{:S(2)}, u32[]{:S(2)}) collective-permute-start(bf16[2,2,768,128]{3,2,1,0:T(8,128)(2,1)} %get-tuple-element.182), channel_id=1, source_target_pairs={{4,0},{5,1},{6,2},{7,3},{12,8},{13,9},{14,10},{15,11},{20,16},{21,... | collective-permute-start | bytes 2359304 | tf_op jit(solution)/shard_map/ppermute | solution.py:1021
  367.5 46.1 %collective-permute-start.30 = (bf16[384,1536]{1,0:T(8,128)(2,1)}, bf16[384,1536]{1,0:T(8,128)(2,1)}, u32[]{:S(2)}, u32[]{:S(2)}) collective-permute-start(bf16[384,1536]{1,0:T(8,128)(2,1)} %add_convert_fusion.4), channel_id=1, source_target_pairs={{0,1},{1,2},{2,3},{3,0},{4,5},{5,6},{6,7},{7,4},{8,9},{9,10},{10,1... | collective-permute-start | bytes 3538952 | tf_op jit(solution)/shard_map/ppermute | solution.py:782
  381.8 31.5 %collective-permute-start.32 = (bf16[384,384]{1,0:T(8,128)(2,1)}, bf16[384,384]{1,0:T(8,128)(2,1)}, u32[]{:S(2)}, u32[]{:S(2)}) collective-permute-start(bf16[384,384]{1,0:T(8,128)(2,1)} %get-tuple-element.263), channel_id=1, source_target_pairs={{0,2},{1,3},{2,0},{3,1},{4,6},{5,7},{6,4},{7,5},{8,10},{9,11},{10,... | collective-permute-start | bytes 884744 | tf_op jit(solution)/shard_map/ppermute | solution.py:782
  418.8 214.4 %reduce-scatter.6.cloned.1.call-start = ((), (), s32[]{:S(2)}) async-start(), calls=%async_computation.6 | async-start | bytes 7962624 | tf_op jit(solution)/shard_map/reduce_scatter | solution.py:835
  428.0 31.5 %collective-permute-start.34 = (bf16[384,1536]{1,0:T(8,128)(2,1)}, bf16[384,1536]{1,0:T(8,128)(2,1)S(1)}, u32[]{:S(2)}, u32[]{:S(2)}) collective-permute-start(bf16[384,1536]{1,0:T(8,128)(2,1)} %add_convert_fusion.3), channel_id=1, source_target_pairs={{0,1},{1,2},{2,3},{3,0},{4,5},{5,6},{6,7},{7,4},{8,9},{9,10},{10,1... | collective-permute-start | bytes 3538952 | tf_op jit(solution)/shard_map/ppermute | solution.py:782
  460.6 235.1 %reduce-scatter.8.cloned.1.call-start = ((), (), s32[]{:S(2)}) async-start(), calls=%async_computation.7 | async-start | bytes 7962624 | tf_op jit(solution)/shard_map/reduce_scatter | solution.py:835
  464.1 39.3 %collective-permute-start.39 = (bf16[384,1536]{1,0:T(8,128)(2,1)S(1)}, bf16[384,1536]{1,0:T(8,128)(2,1)}, u32[]{:S(2)}, u32[]{:S(2)}) collective-permute-start(bf16[384,1536]{1,0:T(8,128)(2,1)S(1)} %copy-done.15), channel_id=1, source_target_pairs={{0,1},{1,2},{2,3},{3,0},{4,5},{5,6},{6,7},{7,4},{8,9},{9,10},{10,1... | collective-permute-start | bytes 3538952 | tf_op jit(solution)/shard_map/ppermute | solution.py:782
  466.5 35.0 %collective-permute-start.41 = (bf16[2,2,2,192,128]{4,3,2,1,0:T(8,128)(2,1)}, bf16[2,2,2,192,128]{4,3,2,1,0:T(8,128)(2,1)}, u32[]{:S(2)}, u32[]{:S(2)}) collective-permute-start(bf16[2,2,2,192,128]{4,3,2,1,0:T(8,128)(2,1)} %add_convert_fusion.13), channel_id=1, source_target_pairs={{0,1},{1,2},{2,3},{3,0},{4,5},{5,6},{6,7},{7,4},{8,9},{9,10},{10,1... | collective-permute-start | bytes 1179656 | tf_op jit(solution)/shard_map/ppermute | solution.py:782
  506.8 33.2 %collective-permute-start.35 = (bf16[1536,768]{0,1:T(8,128)(2,1)}, bf16[1536,768]{0,1:T(8,128)(2,1)}, u32[]{:S(2)}, u32[]{:S(2)}) collective-permute-start(bf16[1536,768]{0,1:T(8,128)(2,1)} %pad_maximum_fusion.2), channel_id=1, source_target_pairs={{0,8},{8,0},{16,24},{24,16},{1,9},{9,1},{17,25},{25,17},{2,10},{10... | collective-permute-start | bytes 7077896 | tf_op jit(solution)/shard_map/ppermute | solution.py:773
  506.9 33.1 %collective-permute-start.42 = (bf16[384,1536]{1,0:T(8,128)(2,1)S(1)}, bf16[384,1536]{1,0:T(8,128)(2,1)}, u32[]{:S(2)}, u32[]{:S(2)}) collective-permute-start(bf16[384,1536]{1,0:T(8,128)(2,1)S(1)} %add_convert_fusion.2.refs_0_), channel_id=1, source_target_pairs={{0,1},{1,2},{2,3},{3,0},{4,5},{5,6},{6,7},{7,4},{8,9},{9,10},{10,1... | collective-permute-start | bytes 3538952 | tf_op jit(solution)/shard_map/ppermute | solution.py:782
  540.0 35.9 %collective-permute-start.44 = (bf16[384,1536]{1,0:T(8,128)(2,1)}, bf16[384,1536]{1,0:T(8,128)(2,1)}, u32[]{:S(2)}, u32[]{:S(2)}) collective-permute-start(bf16[384,1536]{1,0:T(8,128)(2,1)} %collective-permute-done.39.refs_1_), channel_id=1, source_target_pairs={{0,1},{1,2},{2,3},{3,0},{4,5},{5,6},{6,7},{7,4},{8,9},{9,10},{10,1... | collective-permute-start | bytes 3538952 | tf_op jit(solution)/shard_map/ppermute | solution.py:782
  543.5 37.3 %collective-permute-start.40 = (bf16[1536,384]{0,1:T(8,128)(2,1)}, bf16[1536,384]{0,1:T(8,128)(2,1)}, u32[]{:S(2)}, u32[]{:S(2)}) collective-permute-start(bf16[1536,384]{0,1:T(8,128)(2,1)} %constant_dynamic-slice_fusion.14), channel_id=1, source_target_pairs={{0,16},{16,0},{8,24},{24,8},{1,17},{17,1},{9,25},{25,9},{2,18},{18... | collective-permute-start | bytes 3538952 | tf_op jit(solution)/shard_map/ppermute | solution.py:776
  544.1 31.8 %collective-permute-start.46 = (bf16[400,512]{1,0:T(8,128)(2,1)S(1)}, bf16[400,512]{1,0:T(8,128)(2,1)S(1)}, u32[]{:S(2)}, u32[]{:S(2)}) collective-permute-start(bf16[400,512]{1,0:T(8,128)(2,1)S(1)} %fusion.10.refs_4_), channel_id=1, source_target_pairs={{0,1},{1,2},{2,3},{3,0},{4,5},{5,6},{6,7},{7,4},{8,9},{9,10},{10,1... | collective-permute-start | bytes 1228808 | tf_op jit(solution)/shard_map/ppermute | solution.py:782
  576.0 38.4 %collective-permute-start.48 = (bf16[384,1536]{1,0:T(8,128)(2,1)}, bf16[384,1536]{1,0:T(8,128)(2,1)}, u32[]{:S(2)}, u32[]{:S(2)}) collective-permute-start(bf16[384,1536]{1,0:T(8,128)(2,1)} %collective-permute-done.42.refs_1_), channel_id=1, source_target_pairs={{0,1},{1,2},{2,3},{3,0},{4,5},{5,6},{6,7},{7,4},{8,9},{9,10},{10,1... | collective-permute-start | bytes 3538952 | tf_op jit(solution)/shard_map/ppermute | solution.py:782
  583.8 30.6 %collective-permute-start.55 = (bf16[192,2240]{1,0:T(8,128)(2,1)}, bf16[192,2240]{1,0:T(8,128)(2,1)S(1)}, u32[]{:S(2)}, u32[]{:S(2)}) collective-permute-start(bf16[192,2240]{1,0:T(8,128)(2,1)} %reduce-scatter.4.cloned.1.call-done), channel_id=1, source_target_pairs={{0,4},{4,0},{1,5},{5,1},{2,6},{6,2},{3,7},{7,3},{8,12},{12,8},{9,1... | collective-permute-start | bytes 2580488 | tf_op jit(solution)/shard_map/ppermute | solution.py:779
  623.6 34.4 %collective-permute-start.52 = (bf16[384,1536]{1,0:T(8,128)(2,1)}, bf16[384,1536]{1,0:T(8,128)(2,1)}, u32[]{:S(2)}, u32[]{:S(2)}) collective-permute-start(bf16[384,1536]{1,0:T(8,128)(2,1)} %collective-permute-done.44.refs_2_), channel_id=1, source_target_pairs={{0,1},{1,2},{2,3},{3,0},{4,5},{5,6},{6,7},{7,4},{8,9},{9,10},{10,1... | collective-permute-start | bytes 3538952 | tf_op jit(solution)/shard_map/ppermute | solution.py:782
  658.0 41.9 %collective-permute-start.57 = (bf16[384,1536]{1,0:T(8,128)(2,1)}, bf16[384,1536]{1,0:T(8,128)(2,1)}, u32[]{:S(2)}, u32[]{:S(2)}) collective-permute-start(bf16[384,1536]{1,0:T(8,128)(2,1)} %collective-permute-done.48.refs_2_), channel_id=1, source_target_pairs={{0,1},{1,2},{2,3},{3,0},{4,5},{5,6},{6,7},{7,4},{8,9},{9,10},{10,1... | collective-permute-start | bytes 3538952 | tf_op jit(solution)/shard_map/ppermute | solution.py:782
  (119 other events, 1937.9 us)
Sparse Core Ops, SparseCore 0:
  31.5 122.9 all-gather.2
  175.4 35.1 all-gather.4
  419.0 75.4 reduce-scatter.3
  498.8 77.6 reduce-scatter.5
  579.8 76.4 reduce-scatter.7

commit v5 on v4

--- a/solution.py
+++ b/solution.py
@@ -212,10 +212,10 @@
 def bwd_kernel(heads, block, parts, seq, meta, *refs):
     q_refs, (
         kb_ref, vb_ref, k_ref, v_ref, order_ref, o_ref, g_ref, lse_ref, cos_ref, sin_ref,
-        dq_ref, db_ref, dd_ref, qg_ref, gg_ref, acc_ref,
+        dq_ref, db_ref, dd_ref, qg_ref, gg_ref, both_ref, acc_ref,
     ) = refs[:parts], refs[parts:]
     own, cols = q_refs[0].shape[1:]
-    head_dim = acc_ref.shape[1]
+    head_dim = acc_ref.shape[0]
     scale = 1.0 / math.sqrt(head_dim)
     each = cols // head_dim
     for head in range(heads):
@@ -225,8 +225,8 @@
             0, :, (head % each) * head_dim : (head % each + 1) * head_dim
         ]
         gg_ref[rows, :] = g_ref[:, at]
-        acc_ref[rows, :] = g_ref[:, at].astype(jnp.float32) * o_ref[:, at].astype(jnp.float32)
-    center = jnp.sum(jnp.transpose(acc_ref[...]), axis=0, keepdims=True)
+        both_ref[rows, :] = g_ref[:, at].astype(jnp.float32) * o_ref[:, at].astype(jnp.float32)
+    center = jnp.sum(jnp.transpose(both_ref[...]), axis=0, keepdims=True)
     acc_ref[...] = jnp.zeros_like(acc_ref)
     lse = lse_ref[...].reshape(order_ref.shape)
     first = meta[PLACE + seq] * own
@@ -245,7 +245,7 @@
         prob_grad = inner_cols(values, gg_ref[...])
         logit_grad = (probs * (prob_grad - center)).astype(LOW)
         out_ref[0, 0, pl.ds(start, block), :] = (dot(logit_grad, qg_ref[...]) * scale).astype(LOW)
-        acc_ref[...] += inner_rows(logit_grad, keys)
+        acc_ref[...] += inner_rows(keys, logit_grad)
 
     def early(index, carry):
         step(kb_ref, vb_ref, db_ref, index, False)
@@ -268,8 +268,9 @@
     lax.fori_loop(0, last, late, 0)
     step(k_ref, v_ref, dd_ref, last, True)
     lax.fori_loop(last + 1, k_ref.shape[0] // block, clear(dd_ref), 0)
+    both_ref[...] = jnp.transpose(acc_ref[...])
     for head in range(heads):
-        grad = acc_ref[head * own : (head + 1) * own, :] * scale
+        grad = both_ref[head * own : (head + 1) * own, :] * scale
         grad = grad * cos_ref[...] - pltpu.roll(grad, head_dim // 2, 1) * sin_ref[...]
         dq_ref[:, head * head_dim : (head + 1) * head_dim] = grad.astype(LOW)
 
@@ -363,6 +364,7 @@
             pltpu.VMEM((wide, head_dim), LOW),
             pltpu.VMEM((wide, head_dim), LOW),
             pltpu.VMEM((wide, head_dim), jnp.float32),
+            pltpu.VMEM((head_dim, wide), jnp.float32),
         ],
         cost=pl.CostEstimate(flops=16 * work, bytes_accessed=1 << 22, transcendentals=0),
         name="attend_back",
@@ -489,9 +491,12 @@
     return root * scaled - values * root**3 * jnp.mean(scaled * values, axis=-1, keepdims=True), term
 
 
-def finish_kernel(meta, g_ref, q_ref, x_ref, hg_ref, gain_ref, out_ref, term_ref):
+def finish_kernel(tps, meta, g_ref, q_ref, x_ref, hg_ref, gain_ref, out_ref, term_ref, turned_ref):
+    part = g_ref.shape[1] // tps
+    for hop in range(tps):
+        turned_ref[:, hop * part : (hop + 1) * part] = g_ref[:, pl.ds(tp_at(meta, hop, tps, part), part)]
     values = x_ref[...].reshape(hg_ref.shape).astype(jnp.float32)
-    part, term = back_through_norm(inner_cols(g_ref[...], q_ref[...]), values, gain_ref[...])
+    part, term = back_through_norm(inner_cols(turned_ref[...], q_ref[...]), values, gain_ref[...])
     term_ref[...] = term.reshape(term_ref.shape)
     out_ref[...] = (hg_ref[...] + part).astype(LOW)
 
@@ -502,7 +507,7 @@
     tokens = seq_count * own
     row = pl.BlockSpec((own, width), lambda s, m: (s, 0))
     return call(
-        finish_kernel,
+        functools.partial(finish_kernel, tps),
         (seq_count,),
         [
             pl.BlockSpec((own, q_grad.shape[1]), lambda s, m: (s, 0)),
@@ -513,6 +518,7 @@
         ],
         [row, pl.BlockSpec((1, 1, width), lambda s, m: (s, 0, 0))],
         [shape((tokens, width), LOW), shape((seq_count, 1, width), jnp.float32)],
+        [pltpu.VMEM((own, q_grad.shape[1]), LOW)],
         cost=pl.CostEstimate(
             flops=2 * tokens * q_grad.shape[1] * width, bytes_accessed=1 << 23, transcendentals=0
         ),
@@ -615,7 +621,7 @@
 
 def feed_kernel(first, hidden, *refs):
     n_ref, c_ref, wg_ref, wu_ref, wd_ref = refs[1:6]
-    act_ref, gg_ref, ug_ref, two_ref, mix_ref, two_acc, mix_acc = refs[6 if first else 9 :]
+    act_ref, gg_ref, ug_ref, all_ref, two_ref, mix_ref, two_acc, mix_acc = refs[6 if first else 10 :]
     step, tile = pl.program_id(0), wg_ref.shape[0]
     steps = -(-hidden // tile)
 
@@ -636,6 +642,7 @@
 
     @pl.when(step == 0)
     def _():
+        all_ref[...] = n_ref[...]
         two_acc[...], mix_acc[...] = body(tile)
 
     @pl.when(jnp.logical_and(step > 0, step < steps - 1))
@@ -668,12 +675,17 @@
             num_scalar_prefetch=1,
             grid=(-(-hidden // tile),),
             in_specs=[fixed, pl.BlockSpec((rows, width), lambda j, m: (hop, 0)), gate_spec, gate_spec, down_spec]
-            + ([] if first else [pl.BlockSpec(memory_space=pl.ANY)] * 3),
-            out_specs=[column, column, column, fixed, fixed],
+            + ([] if first else [pl.BlockSpec(memory_space=pl.ANY)] * 4),
+            out_specs=[
+                column, column, column, pl.BlockSpec((rows, width), lambda j, m: (hop, 0)), fixed, fixed
+            ],
             scratch_shapes=[pltpu.VMEM((rows, width), jnp.float32)] * 2,
         ),
-        out_shape=[wide, wide, wide, shape((rows, width), LOW), shape((rows, width), LOW)],
-        input_output_aliases={} if first else {6: 0, 7: 1, 8: 2},
+        out_shape=[
+            wide, wide, wide, shape((tps * rows, width), LOW),
+            shape((rows, width), LOW), shape((rows, width), LOW),
+        ],
+        input_output_aliases={} if first else {6: 0, 7: 1, 8: 2, 9: 3},
         compiler_params=pltpu.CompilerParams(vmem_limit_bytes=56 * MIB),
         cost_estimate=pl.CostEstimate(
             flops=12 * rows * width * hidden, bytes_accessed=6 * width * hidden, transcendentals=rows * hidden
@@ -946,7 +958,7 @@
     gate_down = gather_whole(gate_weight.T, down_weight)
     o_blocks = o_blocks[:2] + [after(item, kv_own) for item in o_blocks[2:]]
     o_wide = jnp.concatenate(o_blocks, axis=0)
-    q_blocks = links.gather_tp(after(query_weight, kv_own))
+    q_blocks = links.gather_tp(after(query_weight, queries))
     if ctxs == 2:
         o_near = links.to_x(lax.dynamic_slice_in_dim(o_wide, ctx * (depth // 2), depth // 2, 0))
         o_far = links.to_y(after(o_near, kv_before))
@@ -961,15 +973,15 @@
     )
 
     order = jnp.tile(jnp.arange(own, dtype=jnp.int32), depth // head_dim // kv_heads)[None]
-    order = after(order, (cot_all, one_all, q_blocks[2], *([up_near] if ctxs == 2 else [])))
+    order = after(order, (cot_all, one_all, q_blocks[1], *([up_near] if ctxs == 2 else [])))
     sizes = (seq_count, kv_heads, head_dim, tps)
     mixed, lse = attend(meta, queries, kv_before, kv_own, order, key_block, sizes)
     o_core_near, o_core_far = (
-        links.to_core(after(item, (mixed, q_blocks[-1]))) for item in (o_near, o_far)
+        links.to_core(after(item, (mixed, q_blocks[2]))) for item in (o_near, o_far)
     )
     o_parts = (o_wide, o_core, o_near, o_far, o_core_near, o_core_far)
     hidden, normed_two = merge(meta, mixed, inputs, o_parts, mlp_gamma, tps)
-    two_blocks = [normed_two, links.hop_tp(normed_two)]
+    two_blocks = [normed_two, links.hop_tp(after(normed_two, q_blocks[-1]))]
     if ctxs == 2:
         up_cores = [links.to_core(after(item, mixed)) for item in (up_mine, up_near)]
         up_cores.append(links.to_core(after(up_far, normed_two)))
@@ -992,19 +1004,16 @@
         two_parts.append(two_part)
         mixed_parts.append(mixed_part)
         if hop == 0:
-            q_wide = jnp.zeros((query_weight.shape[0], depth), LOW)
-            for back, item in enumerate(q_blocks):
-                q_wide = lax.dynamic_update_slice_in_dim(q_wide, item, links.at(back) * q_cols, 1)
+            q_wide = jnp.concatenate(q_blocks, axis=1)
             q_full = lax.all_gather(q_wide, "fsdp", axis=0, tiled=True)
         if hop >= 1:
             two_total = two_part if hop == 1 else add_low(two_part, two_got)
             two_got = links.hop_tp(two_total)
         two_total = two_total if hop >= 2 else None
     two_own = two_parts[0]
-    act_all, gate_all, up_all = kept
-    two_all = jnp.concatenate(two_blocks, axis=0)
+    act_all, gate_all, up_all, two_all = kept
     down_term = inner_rows(cot_all, after(act_all, two_total)).astype(LOW)
-    two_got = after(two_got, (down_term, two_all))
+    two_got = after(two_got, down_term)
 
     hidden_grad, branch_grad, attended_grad, mlp_term = turn(
         meta, two_own, two_got, hidden, cotangent, o_parts, mlp_gamma, depth, tps
@@ -1026,7 +1035,8 @@
     mixed_got = links.hop_tp(add_low(mixed_parts[2], after(mixed_got, q_grads[0])))
     q_grad = jnp.concatenate(q_grads, axis=0)
     shares = swap(lambda d: lax.dynamic_slice_in_dim(q_grad, d * q_cols, q_cols, 1))
-    input_low, attn_term = finish(meta, q_grad, q_full, inputs, hidden_grad, attn_gamma, tps)
+    mixed_next = add_low(mixed_parts[3], mixed_got)
+    input_low, attn_term = finish(meta, after(q_grad, mixed_next), q_full, inputs, hidden_grad, attn_gamma, tps)
     output_pairs = links.pairs(inner_rows(mixed, after(branch_grad, q_grads[-1])).astype(LOW), 1)
     token = (mixed_got, input_low, kv_parts, shares, output_pairs)
     kv_parts = [
@@ -1051,7 +1061,6 @@
         return lax.dynamic_slice_in_dim(output_part, links.at(hop) * q_cols, q_cols, 0)
 
     kv_mine, kv_next = kv_rows(0), kv_rows(1)
-    mixed_next = add_low(mixed_parts[3], mixed_got)
     mixed_got = links.hop_tp(after(mixed_next, shares))
     kv_got = links.hop_tp(after(kv_next, (input_low, output_pairs)))
     down_weight_grad = links.lay_weight(*links.reduce_weight(after(down_term, kv_next)))

time: 734 us -> 716 us (0.975)
  local copies, waits for them, and re-layouts: 57.1 us -> 39 us
    ppermute x36, waiting for transfers between devices: 169 us -> 187 us  [hop_tp(): lax.ppermute(value, 'tp', [(i, (i + hop) % self.tps) for i in range(self....]
    unnamed x185 -> x148, local copies, waits for them, and re-layouts: 25.2 us -> 15.1 us
    ppermute x6, waiting for transfers between devices: 34.9 us -> 25.2 us  [to_x(): return lax.ppermute(value, 'fsdp', [(0, 2), (2, 0), (1, 3), (3, 1)])]
    ppermute x8, starting transfers between devices: 39.3 us -> 31.8 us  [to_y(): return lax.ppermute(value, 'ctx', [(0, 1), (1, 0)])]
  transfers between devices with their start and end apart: 69 -> 69, of which waited for: 33 -> 34; matrix products, arithmetic and copies ran while one was open for 22% -> 21% of each run, Pallas kernels for 28% -> 29%
where the time goes in v5:
time: 716 us; the launch traced here: 707 us
  waiting for transfers between devices  238 us (33%)
  Pallas kernels  205 us (29%)
  starting transfers between devices  81.5 us (11%)
  matrix products  65.6 us (9%)
  other arithmetic  61.7 us (9%)
  local copies, waits for them, and re-layouts  39 us (5%)
  between operations  15.7 us (2%)
    ppermute x36, waiting for transfers between devices, hop_tp(): lax.ppermute(value, 'tp', [(i, (i + hop) % self.tps) for i in range(self....  187 us
    pallas_call x4, Pallas kernels, feed(): pl.pallas_call(functools.partial(feed_kernel, first, hidden), grid_spec=p...  106 us
    dot_general x6, matrix products, inner_rows(): lax.dot_general(left, right, (((0,), (0,)), ((), ())), preferred_element_...  65.6 us
    ppermute x36, starting transfers between devices, hop_tp(): lax.ppermute(value, 'tp', [(i, (i + hop) % self.tps) for i in range(self....  34 us
    ppermute x8, starting transfers between devices, to_y(): return lax.ppermute(value, 'ctx', [(0, 1), (1, 0)])  31.8 us
    ppermute x6, waiting for transfers between devices, to_x(): return lax.ppermute(value, 'fsdp', [(0, 2), (2, 0), (1, 3), (3, 1)])  25.2 us
    convert_element_type x17, other arithmetic, add_low(): return (left.astype(jnp.float32) + right.astype(jnp.float32)).astype(LOW)  25.2 us
    ppermute x8, waiting for transfers between devices, to_y(): return lax.ppermute(value, 'ctx', [(0, 1), (1, 0)])  22.4 us
  transfers between devices with their start and end apart: 69, of which 34 were waited for; matrix products, arithmetic and copies ran while one was open for 21% of the time, Pallas kernels for 29%

profile of v5, /device:TPU:0, one launch (start us, length us, event | category | flops | bytes accessed | tf_op | source)
XLA Modules:
  0.0 706.9 jit_solution(3682986978459861366)
XLA Ops:
  19.3 12.0 %collective-permute-done.1.refs_2_.refs_10_ = bf16[400,896]{1,0:T(8,128)(2,1)} collective-permute-done((bf16[400,896]{1,0:T(8,128)(2,1)S(1)}, bf16[400,896]{1,0:T(8,128)(2,1)}, u32[]{:S(2)}, u32[]{:S(2)}) %collective-permute-start.1) | collective-permute-done | bytes 716832 | tf_op jit(solution)/shard_map/ppermute | solution.py:788
  45.6 8.4 %collective-permute-done.10 = bf16[384,384]{1,0:T(8,128)(2,1)} collective-permute-done((bf16[384,384]{1,0:T(8,128)(2,1)}, bf16[384,384]{1,0:T(8,128)(2,1)}, u32[]{:S(2)}, u32[]{:S(2)}) %collective-permute-start.10) | collective-permute-done | bytes 294944 | tf_op jit(solution)/shard_map/ppermute | solution.py:794
  58.1 13.6 %project.1 = (bf16[1536,1536]{1,0:T(8,128)(2,1)}, bf16[4,384,384]{2,1,0:T(8,128)(2,1)S(1)}, bf16[1536,512]{1,0:T(8,128)(2,1)}) custom-call(s32[6]{0:T(128)S(1)} %stack.109.meta.refs_0_, bf16[2,768,1536]{2,1,0:T(8,128)(2,1)} %refs_12_.1, f32[1,1536]{1,0:T(1,128)S(1)} %maximum_convert_fusion.gain_ref.refs_13_, f32[1,896]{1,0:T(1,128)S(1)} %bitcast.95, ...), custom_call_target="tpu_custom_call" | custom-call | flops 4227858432 | bytes 18874368 | tf_op jit(solution)/shard_map/project/pallas_call | solution.py:131
  86.9 10.0 %collective-permute-done.5 = bf16[384,384]{1,0:T(8,128)(2,1)S(1)} collective-permute-done((bf16[384,384]{1,0:T(8,128)(2,1)S(1)}, bf16[384,384]{1,0:T(8,128)(2,1)S(1)}, u32[]{:S(2)}, u32[]{:S(2)}) %collective-permute-start.5) | collective-permute-done | bytes 294944 | tf_op jit(solution)/shard_map/ppermute | solution.py:794
  108.7 10.6 %collective-permute-done.13.refs_2_ = bf16[768,384]{1,0:T(8,128)(2,1)S(1)} collective-permute-done((bf16[768,384]{1,0:T(8,128)(2,1)S(1)}, bf16[768,384]{1,0:T(8,128)(2,1)S(1)}, u32[]{:S(2)}, u32[]{:S(2)}) %collective-permute-start.13) | collective-permute-done | bytes 589856 | tf_op jit(solution)/shard_map/ppermute | solution.py:788
  168.0 11.6 %collective-permute-done.19.refs_1_ = bf16[384,1536]{1,0:T(8,128)(2,1)} collective-permute-done((bf16[384,1536]{1,0:T(8,128)(2,1)}, bf16[384,1536]{1,0:T(8,128)(2,1)}, u32[]{:S(2)}, u32[]{:S(2)}) %collective-permute-start.19) | collective-permute-done | bytes 1179680 | tf_op jit(solution)/shard_map/ppermute | solution.py:794
  179.6 26.4 %feed.4 = (bf16[1536,2240]{1,0:T(8,128)(2,1)}, bf16[1536,2240]{1,0:T(8,128)(2,1)}, bf16[1536,2240]{1,0:T(8,128)(2,1)}, bf16[1536,1536]{1,0:T(8,128)(2,1)}, bf16[...) custom-call(s32[6]{0:T(128)} %copy-done.25, bf16[384,1536]{1,0:T(8,128)(2,1)} %get-tuple-element.143.refs_1_, ...), custom_call_target="tpu_custom_call" | custom-call | flops 15854469120 | bytes 20643840 | tf_op jit(solution)/shard_map/feed/pallas_call | solution.py:672
  208.4 26.2 %feed.5 = (bf16[1536,2240]{1,0:T(8,128)(2,1)}, bf16[1536,2240]{1,0:T(8,128)(2,1)}, bf16[1536,2240]{1,0:T(8,128)(2,1)}, bf16[1536,1536]{1,0:T(8,128)(2,1)}, bf16[...) custom-call(s32[6]{0:T(128)} %copy-done.25, ...), custom_call_target="tpu_custom_call", output_to_operand_aliasing={{0}: (6, {}), {1}: (7, {}), {2}: (8, {}), {3}: (9, {})} | custom-call | flops 15854469120 | bytes 20643840 | tf_op jit(solution)/shard_map/feed/pallas_call | solution.py:672
  236.0 26.4 %feed.6 = (bf16[1536,2240]{1,0:T(8,128)(2,1)}, bf16[1536,2240]{1,0:T(8,128)(2,1)}, bf16[1536,2240]{1,0:T(8,128)(2,1)}, bf16[1536,1536]{1,0:T(8,128)(2,1)}, bf16[...) custom-call(s32[6]{0:T(128)} %copy-done.25, ...), custom_call_target="tpu_custom_call", output_to_operand_aliasing={{0}: (6, {}), {1}: (7, {}), {2}: (8, {}), {3}: (9, {})} | custom-call | flops 15854469120 | bytes 20643840 | tf_op jit(solution)/shard_map/feed/pallas_call | solution.py:672
  266.5 26.5 %feed.7 = (bf16[1536,2240]{1,0:T(8,128)(2,1)}, bf16[1536,2240]{1,0:T(8,128)(2,1)}, bf16[1536,2240]{1,0:T(8,128)(2,1)}, bf16[1536,1536]{1,0:T(8,128)(2,1)}, bf16[...) custom-call(s32[6]{0:T(128)} %copy-done.25, ...), custom_call_target="tpu_custom_call", output_to_operand_aliasing={{0}: (6, {}), {1}: (7, {}), {2}: (8, {}), {3}: (9, {})} | custom-call | flops 15854469120 | bytes 20643840 | tf_op jit(solution)/shard_map/feed/pallas_call | solution.py:672
  297.9 16.3 %convolution_convert_fusion.2 = bf16[1536,2240]{1,0:T(8,128)(2,1)} fusion(bf16[1536,1536]{1,0:T(8,128)(2,1)S(1)} %bitcast.101, bf16[1536,2240]{1,0:T(8,128)(2,1)} %get-tuple-element.173), kind=kOutput, calls=%fused_computation.2 | convolution fusion | flops 10573086720 | bytes 18481152 | tf_op jit(solution)/shard_map/dot_general | solution.py:35
  314.1 9.2 %collective-permute-done.28.b_ref = bf16[384,1536]{1,0:T(8,128)(2,1)} collective-permute-done((bf16[384,1536]{1,0:T(8,128)(2,1)}, bf16[384,1536]{1,0:T(8,128)(2,1)}, u32[]{:S(2)}, u32[]{:S(2)}) %collective-permute-start.28) | collective-permute-done | bytes 1179680 | tf_op jit(solution)/shard_map/ppermute | solution.py:794
  326.8 10.1 %turn.1 = (f32[384,1536]{1,0:T(8,128)}, bf16[384,1536]{1,0:T(8,128)(2,1)S(1)}, bf16[384,1536]{1,0:T(8,128)(2,1)S(1)}, f32[2,1,1536]{2,1,0:T(1,128)S(1)}) custom-call(s32[6]{0:T(128)S(1)} %copy-done.26, bf16[384,1536]{1,0:T(8,128)(2,1)S(1)} %copy-done.13, bf16[384,1536]{1,0:T(8,128)(2,1)} %collective-permute-done.28.b_ref, ...), custom_call_target="tpu_custom_call" | custom-call | flops 1811939328 | bytes 8388608 | tf_op jit(solution)/shard_map/turn/pallas_call | solution.py:461
  351.8 10.2 %attend_back.3 = (bf16[192,1536]{1,0:T(8,128)(2,1)S(1)}, bf16[2,2,768,128]{3,2,1,0:T(8,128)(2,1)}, bf16[2,2,768,128]{3,2,1,0:T(8,128)(2,1)S(1)}) custom-call(s32[6]{0:T(128)S(1)} %copy-done.26, bf16[4,384,384]{2,1,0:T(8,128)(2,1)S(1)} %copy-done.18, bf16[4,384,384]{2,1,0:T(8,128)(2,1)S(1)} %copy-done.18, bf16[1536,512]{1,0:T(8,128)(2,1)} %copy-done.30, ...), custom_call_target="tpu_custom_call" | custom-call | flops 7247757312 | bytes 4194304 | tf_op jit(solution)/shard_map/attend_back/pallas_call | solution.py:342
  372.7 9.9 %collective-permute-done.30 = bf16[384,1536]{1,0:T(8,128)(2,1)S(1)} collective-permute-done((bf16[384,1536]{1,0:T(8,128)(2,1)S(1)}, bf16[384,1536]{1,0:T(8,128)(2,1)S(1)}, u32[]{:S(2)}, u32[]{:S(2)}) %collective-permute-start.30) | collective-permute-done | bytes 1179680 | tf_op jit(solution)/shard_map/ppermute | solution.py:794
  409.9 8.7 %collective-permute-done.38 = bf16[2,2,2,192,128]{4,3,2,1,0:T(8,128)(2,1)S(1)} collective-permute-done((bf16[2,2,2,192,128]{4,3,2,1,0:T(8,128)(2,1)}, bf16[2,2,2,192,128]{4,3,2,1,0:T(8,128)(2,1)S(1)}, u32[]{:S(2)}, u32[]{:S(2)}) %collective-permute-start.38) | collective-permute-done | bytes 393248 | tf_op jit(solution)/shard_map/ppermute | solution.py:794
  420.5 18.6 %convolution_convert_fusion.1 = bf16[1536,2240]{1,0:T(8,128)(2,1)} fusion(bf16[1536,1536]{1,0:T(8,128)(2,1)} %get-tuple-element.199, bf16[1536,2240]{1,0:T(8,128)(2,1)} %get-tuple-element.201), kind=kOutput, calls=%fused_computation.1 | convolution fusion | flops 10573086720 | bytes 18481152 | tf_op jit(solution)/shard_map/dot_general | solution.py:35
  450.2 17.1 %convolution_convert_fusion = bf16[1536,2240]{1,0:T(8,128)(2,1)} fusion(bf16[1536,1536]{1,0:T(8,128)(2,1)} %get-tuple-element.199, bf16[1536,2240]{1,0:T(8,128)(2,1)} %get-tuple-element.206), kind=kOutput, calls=%fused_computation | convolution fusion | flops 10573086720 | bytes 18481152 | tf_op jit(solution)/shard_map/dot_general | solution.py:35
  467.3 17.3 %collective-permute-done.41 = bf16[2,2,2,192,128]{4,3,2,1,0:T(8,128)(2,1)} collective-permute-done((bf16[2,2,2,192,128]{4,3,2,1,0:T(8,128)(2,1)}, bf16[2,2,2,192,128]{4,3,2,1,0:T(8,128)(2,1)}, u32[]{:S(2)}, u32[]{:S(2)}) %collective-permute-start.41) | collective-permute-done | bytes 393248 | tf_op jit(solution)/shard_map/ppermute | solution.py:794
  491.2 9.0 %collective-permute-done.43.b_ref = bf16[2,2,2,192,128]{4,3,2,1,0:T(8,128)(2,1)} collective-permute-done((bf16[2,2,2,192,128]{4,3,2,1,0:T(8,128)(2,1)}, bf16[2,2,2,192,128]{4,3,2,1,0:T(8,128)(2,1)}, u32[]{:S(2)}, u32[]{:S(2)}) %collective-permute-start.43) | collective-permute-done | bytes 393248 | tf_op jit(solution)/shard_map/ppermute | solution.py:794
  532.2 27.9 %collective-permute-done.46.refs_5_ = bf16[400,512]{1,0:T(8,128)(2,1)S(1)} collective-permute-done((bf16[400,512]{1,0:T(8,128)(2,1)S(1)}, bf16[400,512]{1,0:T(8,128)(2,1)S(1)}, u32[]{:S(2)}, u32[]{:S(2)}) %collective-permute-start.46) | collective-permute-done | bytes 409632 | tf_op jit(solution)/shard_map/ppermute | solution.py:794
  577.8 19.5 %collective-permute-done.45 = bf16[384,384]{0,1:T(8,128)(2,1)S(1)} collective-permute-done((bf16[384,384]{0,1:T(8,128)(2,1)S(1)}, bf16[384,384]{0,1:T(8,128)(2,1)S(1)}, u32[]{:S(2)}, u32[]{:S(2)}) %collective-permute-start.45) | collective-permute-done | bytes 294944 | tf_op jit(solution)/shard_map/ppermute | solution.py:794
  633.1 9.5 %collective-permute-done.52.refs_3_ = bf16[384,1536]{1,0:T(8,128)(2,1)} collective-permute-done((bf16[384,1536]{1,0:T(8,128)(2,1)}, bf16[384,1536]{1,0:T(8,128)(2,1)}, u32[]{:S(2)}, u32[]{:S(2)}) %collective-permute-start.52) | collective-permute-done | bytes 1179680 | tf_op jit(solution)/shard_map/ppermute | solution.py:794
  662.1 13.3 %last.1 = f32[2,768,1536]{2,1,0:T(8,128)} custom-call(s32[6]{0:T(128)S(1)} %copy-done.26, bf16[384,1536]{1,0:T(8,128)(2,1)S(1)} %copy-done.16, bf16[384,1536]{1,0:T(8,128)(2,1)} %collective-permute-done.39.refs_1_, bf16[384,1536]{1,0:T(8,128)(2,1)} %collective-permute-done.44.refs_2_, bf16[384,1536]{1,0:T(8,128)(2,1)} %collective-permute-done.52.refs_3_, ...), custom_call_target="tpu_custom_call" | custom-call | flops 2415919104 | bytes 16777216 | tf_op jit(solution)/shard_map/last/pallas_call | solution.py:605
  (414 shorter events, 322.9 us)
Async XLA Ops:
  7.2 172.4 %all-gather.3.cloned.1.call-start = ((), (), s32[]{:S(2)}) async-start(), calls=%async_computation.3 | async-start | bytes 17203200 | tf_op jit(solution)/shard_map/all_gather | solution.py:956
  31.4 354.3 %all-gather.5.cloned.1.call-start = ((), (), s32[]{:S(2)}) async-start(), calls=%async_computation.4 | async-start | bytes 5898240 | tf_op jit(solution)/shard_map/all_gather | solution.py:1008
  54.0 46.5 %collective-permute-start.9 = (bf16[1120,384]{1,0:T(8,128)(2,1)}, bf16[1120,384]{1,0:T(8,128)(2,1)}, u32[]{:S(2)}, u32[]{:S(2)}) collective-permute-start(bf16[1120,384]{1,0:T(8,128)(2,1)} %dynamic-slice_bitcast_fusion), channel_id=1, source_target_pairs={{0,16},{16,0},{8,24},{24,8},{1,17},{17,1},{9,25},{25,9},{2,18},{18... | collective-permute-start | bytes 2580488 | tf_op jit(solution)/shard_map/ppermute | solution.py:788
  75.8 43.5 %collective-permute-start.7 = (bf16[1536,512]{1,0:T(8,128)(2,1)S(1)}, bf16[1536,512]{1,0:T(8,128)(2,1)S(1)}, u32[]{:S(2)}, u32[]{:S(2)}) collective-permute-start(bf16[1536,512]{1,0:T(8,128)(2,1)S(1)} %copy-done.29), channel_id=1, source_target_pairs={{0,4},{1,5},{2,6},{3,7},{8,12},{9,13},{10,14},{11,15},{16,20},{17,... | collective-permute-start | bytes 4718600 | tf_op jit(solution)/shard_map/ppermute | solution.py:937
  86.3 32.9 %collective-permute-start.13 = (bf16[768,384]{1,0:T(8,128)(2,1)S(1)}, bf16[768,384]{1,0:T(8,128)(2,1)S(1)}, u32[]{:S(2)}, u32[]{:S(2)}) collective-permute-start(bf16[768,384]{1,0:T(8,128)(2,1)S(1)} %constant_dynamic-slice_fusion.23), channel_id=1, source_target_pairs={{0,16},{16,0},{8,24},{24,8},{1,17},{17,1},{9,25},{25,9},{2,18},{18... | collective-permute-start | bytes 1769480 | tf_op jit(solution)/shard_map/ppermute | solution.py:788
  100.4 38.1 %collective-permute-start.12 = (bf16[1536,384]{1,0:T(8,128)(2,1)S(1)}, bf16[1536,384]{1,0:T(8,128)(2,1)S(1)}, u32[]{:S(2)}, u32[]{:S(2)}) collective-permute-start(bf16[1536,384]{1,0:T(8,128)(2,1)S(1)} %constant_dynamic-update-slice_fusion.refs_0_), channel_id=1, source_target_pairs={{0,8},{8,0},{16,24},{24,16},{1,9},{9,1},{17,25},{25,17},{2,10},{10... | collective-permute-start | bytes 3538952 | tf_op jit(solution)/shard_map/ppermute | solution.py:785
  159.3 406.2 %reduce-scatter.4.cloned.1.call-start = ((), (), s32[]{:S(2)}) async-start(), calls=%async_computation.5 | async-start | bytes 7962624 | tf_op jit(solution)/shard_map/reduce_scatter | solution.py:847
  345.1 49.3 %collective-permute-start.36 = (bf16[2,2,768,128]{3,2,1,0:T(8,128)(2,1)}, bf16[2,2,768,128]{3,2,1,0:T(8,128)(2,1)}, u32[]{:S(2)}, u32[]{:S(2)}) collective-permute-start(bf16[2,2,768,128]{3,2,1,0:T(8,128)(2,1)} %get-tuple-element.193), channel_id=1, source_target_pairs={{4,0},{5,1},{6,2},{7,3},{12,8},{13,9},{14,10},{15,11},{20,16},{21,... | collective-permute-start | bytes 2359304 | tf_op jit(solution)/shard_map/ppermute | solution.py:1030
  363.3 31.1 %collective-permute-start.31 = (bf16[384,384]{1,0:T(8,128)(2,1)}, bf16[384,384]{1,0:T(8,128)(2,1)}, u32[]{:S(2)}, u32[]{:S(2)}) collective-permute-start(bf16[384,384]{1,0:T(8,128)(2,1)} %get-tuple-element.276), channel_id=1, source_target_pairs={{0,1},{1,2},{2,3},{3,0},{4,5},{5,6},{6,7},{7,4},{8,9},{9,10},{10,1... | collective-permute-start | bytes 884744 | tf_op jit(solution)/shard_map/ppermute | solution.py:794
  363.6 33.0 %collective-permute-start.32 = (bf16[384,384]{1,0:T(8,128)(2,1)}, bf16[384,384]{1,0:T(8,128)(2,1)}, u32[]{:S(2)}, u32[]{:S(2)}) collective-permute-start(bf16[384,384]{1,0:T(8,128)(2,1)} %get-tuple-element.275), channel_id=1, source_target_pairs={{0,2},{1,3},{2,0},{3,1},{4,6},{5,7},{6,4},{7,5},{8,10},{9,11},{10,... | collective-permute-start | bytes 884744 | tf_op jit(solution)/shard_map/ppermute | solution.py:794
  401.8 212.3 %reduce-scatter.6.cloned.1.call-start = ((), (), s32[]{:S(2)}) async-start(), calls=%async_computation.6 | async-start | bytes 7962624 | tf_op jit(solution)/shard_map/reduce_scatter | solution.py:847
  408.7 34.0 %collective-permute-start.34 = (bf16[384,1536]{1,0:T(8,128)(2,1)S(1)}, bf16[384,1536]{1,0:T(8,128)(2,1)}, u32[]{:S(2)}, u32[]{:S(2)}) collective-permute-start(bf16[384,1536]{1,0:T(8,128)(2,1)S(1)} %copy-done.41), channel_id=1, source_target_pairs={{0,1},{1,2},{2,3},{3,0},{4,5},{5,6},{6,7},{7,4},{8,9},{9,10},{10,1... | collective-permute-start | bytes 3538952 | tf_op jit(solution)/shard_map/ppermute | solution.py:794
  442.8 234.3 %reduce-scatter.8.cloned.1.call-start = ((), (), s32[]{:S(2)}) async-start(), calls=%async_computation.7 | async-start | bytes 7962624 | tf_op jit(solution)/shard_map/reduce_scatter | solution.py:847
  447.3 39.3 %collective-permute-start.39 = (bf16[384,1536]{1,0:T(8,128)(2,1)S(1)}, bf16[384,1536]{1,0:T(8,128)(2,1)}, u32[]{:S(2)}, u32[]{:S(2)}) collective-permute-start(bf16[384,1536]{1,0:T(8,128)(2,1)S(1)} %copy-done.15), channel_id=1, source_target_pairs={{0,1},{1,2},{2,3},{3,0},{4,5},{5,6},{6,7},{7,4},{8,9},{9,10},{10,1... | collective-permute-start | bytes 3538952 | tf_op jit(solution)/shard_map/ppermute | solution.py:794
  449.8 34.8 %collective-permute-start.41 = (bf16[2,2,2,192,128]{4,3,2,1,0:T(8,128)(2,1)}, bf16[2,2,2,192,128]{4,3,2,1,0:T(8,128)(2,1)}, u32[]{:S(2)}, u32[]{:S(2)}) collective-permute-start(bf16[2,2,2,192,128]{4,3,2,1,0:T(8,128)(2,1)} %add_convert_fusion.13), channel_id=1, source_target_pairs={{0,1},{1,2},{2,3},{3,0},{4,5},{5,6},{6,7},{7,4},{8,9},{9,10},{10,1... | collective-permute-start | bytes 1179656 | tf_op jit(solution)/shard_map/ppermute | solution.py:794
  490.9 32.5 %collective-permute-start.35 = (bf16[1536,768]{0,1:T(8,128)(2,1)}, bf16[1536,768]{0,1:T(8,128)(2,1)}, u32[]{:S(2)}, u32[]{:S(2)}) collective-permute-start(bf16[1536,768]{0,1:T(8,128)(2,1)} %pad_maximum_fusion.2), channel_id=1, source_target_pairs={{0,8},{8,0},{16,24},{24,16},{1,9},{9,1},{17,25},{25,17},{2,10},{10... | collective-permute-start | bytes 7077896 | tf_op jit(solution)/shard_map/ppermute | solution.py:785
  491.0 32.4 %collective-permute-start.42 = (bf16[384,1536]{1,0:T(8,128)(2,1)S(1)}, bf16[384,1536]{1,0:T(8,128)(2,1)}, u32[]{:S(2)}, u32[]{:S(2)}) collective-permute-start(bf16[384,1536]{1,0:T(8,128)(2,1)S(1)} %add_convert_fusion.2.refs_0_), channel_id=1, source_target_pairs={{0,1},{1,2},{2,3},{3,0},{4,5},{5,6},{6,7},{7,4},{8,9},{9,10},{10,1... | collective-permute-start | bytes 3538952 | tf_op jit(solution)/shard_map/ppermute | solution.py:794
  523.4 36.7 %collective-permute-start.44 = (bf16[384,1536]{1,0:T(8,128)(2,1)}, bf16[384,1536]{1,0:T(8,128)(2,1)}, u32[]{:S(2)}, u32[]{:S(2)}) collective-permute-start(bf16[384,1536]{1,0:T(8,128)(2,1)} %collective-permute-done.39.refs_1_), channel_id=1, source_target_pairs={{0,1},{1,2},{2,3},{3,0},{4,5},{5,6},{6,7},{7,4},{8,9},{9,10},{10,1... | collective-permute-start | bytes 3538952 | tf_op jit(solution)/shard_map/ppermute | solution.py:794
  526.9 35.7 %collective-permute-start.40 = (bf16[1536,384]{0,1:T(8,128)(2,1)}, bf16[1536,384]{0,1:T(8,128)(2,1)}, u32[]{:S(2)}, u32[]{:S(2)}) collective-permute-start(bf16[1536,384]{0,1:T(8,128)(2,1)} %constant_dynamic-slice_fusion.14), channel_id=1, source_target_pairs={{0,16},{16,0},{8,24},{24,8},{1,17},{17,1},{9,25},{25,9},{2,18},{18... | collective-permute-start | bytes 3538952 | tf_op jit(solution)/shard_map/ppermute | solution.py:788
  528.4 31.7 %collective-permute-start.46 = (bf16[400,512]{1,0:T(8,128)(2,1)S(1)}, bf16[400,512]{1,0:T(8,128)(2,1)S(1)}, u32[]{:S(2)}, u32[]{:S(2)}) collective-permute-start(bf16[400,512]{1,0:T(8,128)(2,1)S(1)} %fusion.10.refs_4_), channel_id=1, source_target_pairs={{0,1},{1,2},{2,3},{3,0},{4,5},{5,6},{6,7},{7,4},{8,9},{9,10},{10,1... | collective-permute-start | bytes 1228808 | tf_op jit(solution)/shard_map/ppermute | solution.py:794
  560.1 38.2 %collective-permute-start.48 = (bf16[384,1536]{1,0:T(8,128)(2,1)}, bf16[384,1536]{1,0:T(8,128)(2,1)}, u32[]{:S(2)}, u32[]{:S(2)}) collective-permute-start(bf16[384,1536]{1,0:T(8,128)(2,1)} %collective-permute-done.42.refs_1_), channel_id=1, source_target_pairs={{0,1},{1,2},{2,3},{3,0},{4,5},{5,6},{6,7},{7,4},{8,9},{9,10},{10,1... | collective-permute-start | bytes 3538952 | tf_op jit(solution)/shard_map/ppermute | solution.py:794
  565.6 32.7 %collective-permute-start.55 = (bf16[192,2240]{1,0:T(8,128)(2,1)}, bf16[192,2240]{1,0:T(8,128)(2,1)S(1)}, u32[]{:S(2)}, u32[]{:S(2)}) collective-permute-start(bf16[192,2240]{1,0:T(8,128)(2,1)} %reduce-scatter.4.cloned.1.call-done), channel_id=1, source_target_pairs={{0,4},{4,0},{1,5},{5,1},{2,6},{6,2},{3,7},{7,3},{8,12},{12,8},{9,1... | collective-permute-start | bytes 2580488 | tf_op jit(solution)/shard_map/ppermute | solution.py:791
  607.5 35.2 %collective-permute-start.52 = (bf16[384,1536]{1,0:T(8,128)(2,1)}, bf16[384,1536]{1,0:T(8,128)(2,1)}, u32[]{:S(2)}, u32[]{:S(2)}) collective-permute-start(bf16[384,1536]{1,0:T(8,128)(2,1)} %collective-permute-done.44.refs_2_), channel_id=1, source_target_pairs={{0,1},{1,2},{2,3},{3,0},{4,5},{5,6},{6,7},{7,4},{8,9},{9,10},{10,1... | collective-permute-start | bytes 3538952 | tf_op jit(solution)/shard_map/ppermute | solution.py:794
  642.7 38.6 %collective-permute-start.57 = (bf16[384,1536]{1,0:T(8,128)(2,1)}, bf16[384,1536]{1,0:T(8,128)(2,1)}, u32[]{:S(2)}, u32[]{:S(2)}) collective-permute-start(bf16[384,1536]{1,0:T(8,128)(2,1)} %collective-permute-done.48.refs_2_), channel_id=1, source_target_pairs={{0,1},{1,2},{2,3},{3,0},{4,5},{5,6},{6,7},{7,4},{8,9},{9,10},{10,1... | collective-permute-start | bytes 3538952 | tf_op jit(solution)/shard_map/ppermute | solution.py:794
  (102 other events, 1727.9 us)
Sparse Core Ops, SparseCore 0:
  31.5 121.2 all-gather.2
  159.5 39.0 all-gather.4
  401.9 74.1 reduce-scatter.3
  480.5 77.0 reduce-scatter.5
  561.0 77.3 reduce-scatter.7

commit v6 on v5

--- a/solution.py
+++ b/solution.py
@@ -153,6 +153,10 @@
     )(meta, inputs, gain, bias, *weights, cosine, sine)
 
 
+def half_block(block, own):
+    return block // 2 if block // 2 % own == 0 else block
+
+
 def fwd_kernel(
     heads, block, parts, meta, *refs
 ):
@@ -171,12 +175,10 @@
     m_ref[...] = jnp.full_like(m_ref, MASKED)
     l_ref[...] = jnp.zeros_like(l_ref)
     first = meta[PLACE + pl.program_id(0)] * own
-    last = first // block
-
-    def step(key_ref, value_ref, index, masked):
-        start = pl.multiple_of(index * block, block)
-        keys = key_ref[pl.ds(start, block), :]
-        values = value_ref[pl.ds(start, block), :]
+
+    def step(key_ref, value_ref, start, size, masked):
+        keys = key_ref[pl.ds(start, size), :]
+        values = value_ref[pl.ds(start, size), :]
         logits = inner_cols(keys, qg_ref[...]) * scale
         if masked:
             key_order = (start - first) + lax.broadcasted_iota(jnp.int32, logits.shape, 0)
@@ -190,16 +192,20 @@
         acc_ref[...] = acc_ref[...] * fade + inner_rows(values, weights.astype(LOW))
 
     def early(index, carry):
-        step(kb_ref, vb_ref, index, False)
+        step(kb_ref, vb_ref, pl.multiple_of(index * block, block), block, False)
         return carry
 
-    def late(index, carry):
-        step(k_ref, v_ref, index, False)
-        return carry
-
     lax.fori_loop(0, meta[BEFORE], early, 0)
-    lax.fori_loop(0, last, late, 0)
-    step(k_ref, v_ref, last, True)
+    short = half_block(block, own)
+
+    @pl.when(first < short)
+    def _():
+        step(k_ref, v_ref, 0, short, True)
+
+    @pl.when(first >= short)
+    def _():
+        step(k_ref, v_ref, 0, block, True)
+
     total = l_ref[...]
     lse_ref[...] = (m_ref[...] + jnp.log2(total)).reshape(lse_ref.shape)
     mixed = jnp.transpose(acc_ref[...] / total)
@@ -230,29 +236,23 @@
     acc_ref[...] = jnp.zeros_like(acc_ref)
     lse = lse_ref[...].reshape(order_ref.shape)
     first = meta[PLACE + seq] * own
-    last = first // block
-
-    def step(key_ref, value_ref, out_ref, index, masked):
-        start = pl.multiple_of(index * block, block)
-        keys = key_ref[pl.ds(start, block), :]
-        values = value_ref[pl.ds(start, block), :]
+
+    def step(key_ref, value_ref, out_ref, start, size, masked):
+        keys = key_ref[pl.ds(start, size), :]
+        values = value_ref[pl.ds(start, size), :]
         logits = inner_cols(keys, qg_ref[...]) * (scale * LOG2E)
         if masked:
             key_order = (start - first) + lax.broadcasted_iota(jnp.int32, logits.shape, 0)
             logits = jnp.where(key_order <= order_ref[...], logits, MASKED)
         probs = jnp.exp2(logits - lse)
-        out_ref[1, 0, pl.ds(start, block), :] = dot(probs.astype(LOW), gg_ref[...]).astype(LOW)
+        out_ref[1, 0, pl.ds(start, size), :] = dot(probs.astype(LOW), gg_ref[...]).astype(LOW)
         prob_grad = inner_cols(values, gg_ref[...])
         logit_grad = (probs * (prob_grad - center)).astype(LOW)
-        out_ref[0, 0, pl.ds(start, block), :] = (dot(logit_grad, qg_ref[...]) * scale).astype(LOW)
+        out_ref[0, 0, pl.ds(start, size), :] = (dot(logit_grad, qg_ref[...]) * scale).astype(LOW)
         acc_ref[...] += inner_rows(keys, logit_grad)
 
     def early(index, carry):
-        step(kb_ref, vb_ref, db_ref, index, False)
-        return carry
-
-    def late(index, carry):
-        step(k_ref, v_ref, dd_ref, index, False)
+        step(kb_ref, vb_ref, db_ref, pl.multiple_of(index * block, block), block, False)
         return carry
 
     def clear(ref):
@@ -265,9 +265,18 @@
 
     lax.fori_loop(0, meta[BEFORE], early, 0)
     lax.fori_loop(meta[BEFORE], kb_ref.shape[0] // block, clear(db_ref), 0)
-    lax.fori_loop(0, last, late, 0)
-    step(k_ref, v_ref, dd_ref, last, True)
-    lax.fori_loop(last + 1, k_ref.shape[0] // block, clear(dd_ref), 0)
+    short = half_block(block, own)
+
+    @pl.when(first < short)
+    def _():
+        step(k_ref, v_ref, dd_ref, 0, short, True)
+        if short < block:
+            dd_ref[:, :, short:, :] = jnp.zeros((2, 1, block - short, head_dim), LOW)
+
+    @pl.when(first >= short)
+    def _():
+        step(k_ref, v_ref, dd_ref, 0, block, True)
+
     both_ref[...] = jnp.transpose(acc_ref[...])
     for head in range(heads):
         grad = both_ref[head * own : (head + 1) * own, :] * scale
@@ -885,7 +894,7 @@
     depth = q_cols * tps
     shard = width // fsdps
     tokens = seq_count * block_len
-    key_block = block_len // 2 if block_len % (2 * own) == 0 else block_len
+    key_block = block_len
     seqs = range(seq_count)
 
     def place(seq, device):
@@ -1058,7 +1067,8 @@
         )
 
     def output_rows(hop):
-        return lax.dynamic_slice_in_dim(output_part, links.at(hop) * q_cols, q_cols, 0)
+        size = output_part.shape[0] // tps
+        return lax.dynamic_slice_in_dim(output_part, links.at(hop) * size, size, 0)
 
     kv_mine, kv_next = kv_rows(0), kv_rows(1)
     mixed_got = links.hop_tp(after(mixed_next, shares))
@@ -1072,9 +1082,9 @@
     gate_weight_grad = links.lay_weight(*links.reduce_weight(after(gate_term, mixed_got))).T
     output_both = links.scatter_core(after(output_pairs, mixed_got))
     up_term = inner_rows(two_all, after(up_all, mixed_got)).astype(LOW)
-    kv_next = add_low(kv_rows(3), after(kv_got, up_term))
     out_low = hidden + mixed_parts[0].astype(jnp.float32) + mixed_got.astype(jnp.float32)
     out_low = lax.optimization_barrier(out_low.astype(LOW))
+    kv_next = add_low(kv_rows(3), after(kv_got, (up_term, out_low)))
 
     out_blocks = [out_low, links.hop_tp(after(out_low, (in_blocks[1], kv_next)))]
     kv_got = links.hop_tp(after(kv_next, in_blocks[1]))

time: 716 us -> 711 us (level)
  starting transfers between devices: 81.5 us -> 73.5 us
    ppermute x8, starting transfers between devices: 31.8 us -> 23.4 us  [to_y(): return lax.ppermute(value, 'ctx', [(0, 1), (1, 0)])]
    unnamed x148 -> x144, local copies, waits for them, and re-layouts: 15.1 us -> 15.1 us
  transfers between devices with their start and end apart: 69 -> 69, of which waited for: 34 -> 35; matrix products, arithmetic and copies ran while one was open for 21% -> 21% of each run, Pallas kernels for 29% -> 29%
where the time goes in v6:
time: 711 us; the launch traced here: 703 us
  waiting for transfers between devices  244 us (34%)
  Pallas kernels  205 us (29%)
  starting transfers between devices  73.5 us (10%)
  matrix products  65.3 us (9%)
  other arithmetic  60.8 us (9%)
  local copies, waits for them, and re-layouts  39 us (5%)
  between operations  15.4 us (2%)
    ppermute x36, waiting for transfers between devices, hop_tp(): lax.ppermute(value, 'tp', [(i, (i + hop) % self.tps) for i in range(self....  188 us
    pallas_call x4, Pallas kernels, feed(): pl.pallas_call(functools.partial(feed_kernel, first, hidden), grid_spec=p...  106 us
    dot_general x6, matrix products, inner_rows(): lax.dot_general(left, right, (((0,), (0,)), ((), ())), preferred_element_...  65.3 us
    ppermute x36, starting transfers between devices, hop_tp(): lax.ppermute(value, 'tp', [(i, (i + hop) % self.tps) for i in range(self....  34.8 us
    ppermute x6, waiting for transfers between devices, to_x(): return lax.ppermute(value, 'fsdp', [(0, 2), (2, 0), (1, 3), (3, 1)])  28 us
    convert_element_type x17, other arithmetic, add_low(): return (left.astype(jnp.float32) + right.astype(jnp.float32)).astype(LOW)  25.2 us
    ppermute x8, waiting for transfers between devices, to_y(): return lax.ppermute(value, 'ctx', [(0, 1), (1, 0)])  25.1 us
    ppermute x8, starting transfers between devices, to_y(): return lax.ppermute(value, 'ctx', [(0, 1), (1, 0)])  23.4 us
  transfers between devices with their start and end apart: 69, of which 35 were waited for; matrix products, arithmetic and copies ran while one was open for 21% of the time, Pallas kernels for 29%

profile of v6, /device:TPU:0, one launch (start us, length us, event | category | flops | bytes accessed | tf_op | source)
XLA Modules:
  0.0 702.7 jit_solution(14352188951303120078)
XLA Ops:
  19.3 12.0 %collective-permute-done.1.refs_2_.refs_10_ = bf16[400,896]{1,0:T(8,128)(2,1)} collective-permute-done((bf16[400,896]{1,0:T(8,128)(2,1)S(1)}, bf16[400,896]{1,0:T(8,128)(2,1)}, u32[]{:S(2)}, u32[]{:S(2)}) %collective-permute-start.1) | collective-permute-done | bytes 716832 | tf_op jit(solution)/shard_map/ppermute | solution.py:797
  45.6 8.4 %collective-permute-done.10 = bf16[384,384]{1,0:T(8,128)(2,1)} collective-permute-done((bf16[384,384]{1,0:T(8,128)(2,1)}, bf16[384,384]{1,0:T(8,128)(2,1)}, u32[]{:S(2)}, u32[]{:S(2)}) %collective-permute-start.10) | collective-permute-done | bytes 294944 | tf_op jit(solution)/shard_map/ppermute | solution.py:803
  58.1 13.6 %project.1 = (bf16[1536,1536]{1,0:T(8,128)(2,1)}, bf16[4,384,384]{2,1,0:T(8,128)(2,1)S(1)}, bf16[1536,512]{1,0:T(8,128)(2,1)}) custom-call(s32[6]{0:T(128)S(1)} %stack.106.meta.refs_0_, bf16[2,768,1536]{2,1,0:T(8,128)(2,1)} %refs_12_.1, f32[1,1536]{1,0:T(1,128)S(1)} %maximum_convert_fusion.gain_ref.refs_13_, f32[1,896]{1,0:T(1,128)S(1)} %bitcast.94, ...), custom_call_target="tpu_custom_call" | custom-call | flops 4227858432 | bytes 18874368 | tf_op jit(solution)/shard_map/project/pallas_call | solution.py:131
  86.9 10.0 %collective-permute-done.5 = bf16[384,384]{1,0:T(8,128)(2,1)S(1)} collective-permute-done((bf16[384,384]{1,0:T(8,128)(2,1)S(1)}, bf16[384,384]{1,0:T(8,128)(2,1)S(1)}, u32[]{:S(2)}, u32[]{:S(2)}) %collective-permute-start.5) | collective-permute-done | bytes 294944 | tf_op jit(solution)/shard_map/ppermute | solution.py:803
  108.7 10.6 %collective-permute-done.13.refs_2_ = bf16[768,384]{1,0:T(8,128)(2,1)S(1)} collective-permute-done((bf16[768,384]{1,0:T(8,128)(2,1)S(1)}, bf16[768,384]{1,0:T(8,128)(2,1)S(1)}, u32[]{:S(2)}, u32[]{:S(2)}) %collective-permute-start.13) | collective-permute-done | bytes 589856 | tf_op jit(solution)/shard_map/ppermute | solution.py:797
  165.8 11.7 %collective-permute-done.19.refs_1_ = bf16[384,1536]{1,0:T(8,128)(2,1)} collective-permute-done((bf16[384,1536]{1,0:T(8,128)(2,1)}, bf16[384,1536]{1,0:T(8,128)(2,1)}, u32[]{:S(2)}, u32[]{:S(2)}) %collective-permute-start.19) | collective-permute-done | bytes 1179680 | tf_op jit(solution)/shard_map/ppermute | solution.py:803
  177.5 26.4 %feed.4 = (bf16[1536,2240]{1,0:T(8,128)(2,1)}, bf16[1536,2240]{1,0:T(8,128)(2,1)}, bf16[1536,2240]{1,0:T(8,128)(2,1)}, bf16[1536,1536]{1,0:T(8,128)(2,1)}, bf16[...) custom-call(s32[6]{0:T(128)} %copy-done.22, bf16[384,1536]{1,0:T(8,128)(2,1)} %get-tuple-element.143.refs_1_, ...), custom_call_target="tpu_custom_call" | custom-call | flops 15854469120 | bytes 20643840 | tf_op jit(solution)/shard_map/feed/pallas_call | solution.py:681
  206.3 26.2 %feed.5 = (bf16[1536,2240]{1,0:T(8,128)(2,1)}, bf16[1536,2240]{1,0:T(8,128)(2,1)}, bf16[1536,2240]{1,0:T(8,128)(2,1)}, bf16[1536,1536]{1,0:T(8,128)(2,1)}, bf16[...) custom-call(s32[6]{0:T(128)} %copy-done.22, ...), custom_call_target="tpu_custom_call", output_to_operand_aliasing={{0}: (6, {}), {1}: (7, {}), {2}: (8, {}), {3}: (9, {})} | custom-call | flops 15854469120 | bytes 20643840 | tf_op jit(solution)/shard_map/feed/pallas_call | solution.py:681
  234.0 26.4 %feed.6 = (bf16[1536,2240]{1,0:T(8,128)(2,1)}, bf16[1536,2240]{1,0:T(8,128)(2,1)}, bf16[1536,2240]{1,0:T(8,128)(2,1)}, bf16[1536,1536]{1,0:T(8,128)(2,1)}, bf16[...) custom-call(s32[6]{0:T(128)} %copy-done.22, ...), custom_call_target="tpu_custom_call", output_to_operand_aliasing={{0}: (6, {}), {1}: (7, {}), {2}: (8, {}), {3}: (9, {})} | custom-call | flops 15854469120 | bytes 20643840 | tf_op jit(solution)/shard_map/feed/pallas_call | solution.py:681
  264.4 26.7 %feed.7 = (bf16[1536,2240]{1,0:T(8,128)(2,1)}, bf16[1536,2240]{1,0:T(8,128)(2,1)}, bf16[1536,2240]{1,0:T(8,128)(2,1)}, bf16[1536,1536]{1,0:T(8,128)(2,1)}, bf16[...) custom-call(s32[6]{0:T(128)} %copy-done.22, ...), custom_call_target="tpu_custom_call", output_to_operand_aliasing={{0}: (6, {}), {1}: (7, {}), {2}: (8, {}), {3}: (9, {})} | custom-call | flops 15854469120 | bytes 20643840 | tf_op jit(solution)/shard_map/feed/pallas_call | solution.py:681
  296.0 16.3 %convolution_convert_fusion.2 = bf16[1536,2240]{1,0:T(8,128)(2,1)} fusion(bf16[1536,1536]{1,0:T(8,128)(2,1)S(1)} %bitcast.100, bf16[1536,2240]{1,0:T(8,128)(2,1)} %get-tuple-element.173), kind=kOutput, calls=%fused_computation.2 | convolution fusion | flops 10573086720 | bytes 18481152 | tf_op jit(solution)/shard_map/dot_general | solution.py:35
  312.2 9.2 %collective-permute-done.28.b_ref = bf16[384,1536]{1,0:T(8,128)(2,1)} collective-permute-done((bf16[384,1536]{1,0:T(8,128)(2,1)}, bf16[384,1536]{1,0:T(8,128)(2,1)}, u32[]{:S(2)}, u32[]{:S(2)}) %collective-permute-start.28) | collective-permute-done | bytes 1179680 | tf_op jit(solution)/shard_map/ppermute | solution.py:803
  324.9 10.1 %turn.1 = (f32[384,1536]{1,0:T(8,128)}, bf16[384,1536]{1,0:T(8,128)(2,1)S(1)}, bf16[384,1536]{1,0:T(8,128)(2,1)S(1)}, f32[2,1,1536]{2,1,0:T(1,128)S(1)}) custom-call(s32[6]{0:T(128)S(1)} %copy-done.23, bf16[384,1536]{1,0:T(8,128)(2,1)S(1)} %copy-done.13, bf16[384,1536]{1,0:T(8,128)(2,1)} %collective-permute-done.28.b_ref, ...), custom_call_target="tpu_custom_call" | custom-call | flops 1811939328 | bytes 8388608 | tf_op jit(solution)/shard_map/turn/pallas_call | solution.py:470
  349.9 9.3 %attend_back.3 = (bf16[192,1536]{1,0:T(8,128)(2,1)S(1)}, bf16[2,2,768,128]{3,2,1,0:T(8,128)(2,1)}, bf16[2,2,768,128]{3,2,1,0:T(8,128)(2,1)S(1)}) custom-call(s32[6]{0:T(128)S(1)} %copy-done.23, bf16[4,384,384]{2,1,0:T(8,128)(2,1)S(1)} %copy-done.15, bf16[4,384,384]{2,1,0:T(8,128)(2,1)S(1)} %copy-done.15, bf16[1536,512]{1,0:T(8,128)(2,1)} %copy-done.27, ...), custom_call_target="tpu_custom_call" | custom-call | flops 7247757312 | bytes 4194304 | tf_op jit(solution)/shard_map/attend_back/pallas_call | solution.py:351
  370.5 10.2 %collective-permute-done.30 = bf16[384,1536]{1,0:T(8,128)(2,1)S(1)} collective-permute-done((bf16[384,1536]{1,0:T(8,128)(2,1)S(1)}, bf16[384,1536]{1,0:T(8,128)(2,1)S(1)}, u32[]{:S(2)}, u32[]{:S(2)}) %collective-permute-start.30) | collective-permute-done | bytes 1179680 | tf_op jit(solution)/shard_map/ppermute | solution.py:803
  408.1 8.7 %collective-permute-done.38 = bf16[2,2,2,192,128]{4,3,2,1,0:T(8,128)(2,1)S(1)} collective-permute-done((bf16[2,2,2,192,128]{4,3,2,1,0:T(8,128)(2,1)}, bf16[2,2,2,192,128]{4,3,2,1,0:T(8,128)(2,1)S(1)}, u32[]{:S(2)}, u32[]{:S(2)}) %collective-permute-start.38) | collective-permute-done | bytes 393248 | tf_op jit(solution)/shard_map/ppermute | solution.py:803
  418.8 18.3 %convolution_convert_fusion.1 = bf16[1536,2240]{1,0:T(8,128)(2,1)} fusion(bf16[1536,1536]{1,0:T(8,128)(2,1)} %get-tuple-element.199, bf16[1536,2240]{1,0:T(8,128)(2,1)} %get-tuple-element.201), kind=kOutput, calls=%fused_computation.1 | convolution fusion | flops 10573086720 | bytes 18481152 | tf_op jit(solution)/shard_map/dot_general | solution.py:35
  444.0 17.1 %convolution_convert_fusion = bf16[1536,2240]{1,0:T(8,128)(2,1)} fusion(bf16[1536,1536]{1,0:T(8,128)(2,1)} %get-tuple-element.199, bf16[1536,2240]{1,0:T(8,128)(2,1)} %get-tuple-element.206), kind=kOutput, calls=%fused_computation | convolution fusion | flops 10573086720 | bytes 18481152 | tf_op jit(solution)/shard_map/dot_general | solution.py:35
  463.9 14.8 %collective-permute-done.41 = bf16[2,2,2,192,128]{4,3,2,1,0:T(8,128)(2,1)} collective-permute-done((bf16[2,2,2,192,128]{4,3,2,1,0:T(8,128)(2,1)}, bf16[2,2,2,192,128]{4,3,2,1,0:T(8,128)(2,1)}, u32[]{:S(2)}, u32[]{:S(2)}) %collective-permute-start.41) | collective-permute-done | bytes 393248 | tf_op jit(solution)/shard_map/ppermute | solution.py:803
  526.0 28.8 %collective-permute-done.46.refs_5_ = bf16[400,512]{1,0:T(8,128)(2,1)S(1)} collective-permute-done((bf16[400,512]{1,0:T(8,128)(2,1)S(1)}, bf16[400,512]{1,0:T(8,128)(2,1)S(1)}, u32[]{:S(2)}, u32[]{:S(2)}) %collective-permute-start.46) | collective-permute-done | bytes 409632 | tf_op jit(solution)/shard_map/ppermute | solution.py:803
  570.6 21.4 %collective-permute-done.45 = bf16[384,384]{0,1:T(8,128)(2,1)S(1)} collective-permute-done((bf16[384,384]{0,1:T(8,128)(2,1)S(1)}, bf16[384,384]{0,1:T(8,128)(2,1)S(1)}, u32[]{:S(2)}, u32[]{:S(2)}) %collective-permute-start.45) | collective-permute-done | bytes 294944 | tf_op jit(solution)/shard_map/ppermute | solution.py:803
  627.9 10.3 %collective-permute-done.52.refs_3_ = bf16[384,1536]{1,0:T(8,128)(2,1)} collective-permute-done((bf16[384,1536]{1,0:T(8,128)(2,1)}, bf16[384,1536]{1,0:T(8,128)(2,1)}, u32[]{:S(2)}, u32[]{:S(2)}) %collective-permute-start.52) | collective-permute-done | bytes 1179680 | tf_op jit(solution)/shard_map/ppermute | solution.py:803
  656.8 13.6 %last.1 = f32[2,768,1536]{2,1,0:T(8,128)} custom-call(s32[6]{0:T(128)S(1)} %copy-done.23, bf16[384,1536]{1,0:T(8,128)(2,1)} %get-tuple-element.202.refs_0_, bf16[384,1536]{1,0:T(8,128)(2,1)} %collective-permute-done.39.refs_1_, bf16[384,1536]{1,0:T(8,128)(2,1)} %collective-permute-done.44.refs_2_, bf16[384,1536]{1,0:T(8,128)(2,1)} %collective-permute-done.52.refs_3_, ...), custom_call_target="tpu_custom_call" | custom-call | flops 2415919104 | bytes 16777216 | tf_op jit(solution)/shard_map/last/pallas_call | solution.py:614
  685.2 8.3 %collective-permute-done.63 = bf16[192,2240]{1,0:T(8,128)(2,1)S(1)} collective-permute-done((bf16[192,2240]{1,0:T(8,128)(2,1)}, bf16[192,2240]{1,0:T(8,128)(2,1)S(1)}, u32[]{:S(2)}, u32[]{:S(2)}) %collective-permute-start.63) | collective-permute-done | bytes 860192 | tf_op jit(solution)/shard_map/ppermute | solution.py:800
  (410 shorter events, 319.1 us)
Async XLA Ops:
  7.2 170.3 %all-gather.3.cloned.1.call-start = ((), (), s32[]{:S(2)}) async-start(), calls=%async_computation.3 | async-start | bytes 17203200 | tf_op jit(solution)/shard_map/all_gather | solution.py:965
  31.4 352.0 %all-gather.5.cloned.1.call-start = ((), (), s32[]{:S(2)}) async-start(), calls=%async_computation.4 | async-start | bytes 5898240 | tf_op jit(solution)/shard_map/all_gather | solution.py:1017
  54.0 46.5 %collective-permute-start.9 = (bf16[1120,384]{1,0:T(8,128)(2,1)}, bf16[1120,384]{1,0:T(8,128)(2,1)}, u32[]{:S(2)}, u32[]{:S(2)}) collective-permute-start(bf16[1120,384]{1,0:T(8,128)(2,1)} %dynamic-slice_bitcast_fusion), channel_id=1, source_target_pairs={{0,16},{16,0},{8,24},{24,8},{1,17},{17,1},{9,25},{25,9},{2,18},{18... | collective-permute-start | bytes 2580488 | tf_op jit(solution)/shard_map/ppermute | solution.py:797
  75.8 43.5 %collective-permute-start.7 = (bf16[1536,512]{1,0:T(8,128)(2,1)S(1)}, bf16[1536,512]{1,0:T(8,128)(2,1)S(1)}, u32[]{:S(2)}, u32[]{:S(2)}) collective-permute-start(bf16[1536,512]{1,0:T(8,128)(2,1)S(1)} %copy-done.26), channel_id=1, source_target_pairs={{0,4},{1,5},{2,6},{3,7},{8,12},{9,13},{10,14},{11,15},{16,20},{17,... | collective-permute-start | bytes 4718600 | tf_op jit(solution)/shard_map/ppermute | solution.py:946
  86.3 32.9 %collective-permute-start.13 = (bf16[768,384]{1,0:T(8,128)(2,1)S(1)}, bf16[768,384]{1,0:T(8,128)(2,1)S(1)}, u32[]{:S(2)}, u32[]{:S(2)}) collective-permute-start(bf16[768,384]{1,0:T(8,128)(2,1)S(1)} %constant_dynamic-slice_fusion.23), channel_id=1, source_target_pairs={{0,16},{16,0},{8,24},{24,8},{1,17},{17,1},{9,25},{25,9},{2,18},{18... | collective-permute-start | bytes 1769480 | tf_op jit(solution)/shard_map/ppermute | solution.py:797
  100.4 35.9 %collective-permute-start.12 = (bf16[1536,384]{1,0:T(8,128)(2,1)S(1)}, bf16[1536,384]{1,0:T(8,128)(2,1)S(1)}, u32[]{:S(2)}, u32[]{:S(2)}) collective-permute-start(bf16[1536,384]{1,0:T(8,128)(2,1)S(1)} %constant_dynamic-update-slice_fusion.refs_0_), channel_id=1, source_target_pairs={{0,8},{8,0},{16,24},{24,16},{1,9},{9,1},{17,25},{25,17},{2,10},{10... | collective-permute-start | bytes 3538952 | tf_op jit(solution)/shard_map/ppermute | solution.py:794
  157.2 405.9 %reduce-scatter.4.cloned.1.call-start = ((), (), s32[]{:S(2)}) async-start(), calls=%async_computation.5 | async-start | bytes 7962624 | tf_op jit(solution)/shard_map/reduce_scatter | solution.py:856
  343.1 49.8 %collective-permute-start.36 = (bf16[2,2,768,128]{3,2,1,0:T(8,128)(2,1)}, bf16[2,2,768,128]{3,2,1,0:T(8,128)(2,1)}, u32[]{:S(2)}, u32[]{:S(2)}) collective-permute-start(bf16[2,2,768,128]{3,2,1,0:T(8,128)(2,1)} %get-tuple-element.193), channel_id=1, source_target_pairs={{4,0},{5,1},{6,2},{7,3},{12,8},{13,9},{14,10},{15,11},{20,16},{21,... | collective-permute-start | bytes 2359304 | tf_op jit(solution)/shard_map/ppermute | solution.py:1039
  360.5 32.4 %collective-permute-start.31 = (bf16[384,384]{1,0:T(8,128)(2,1)}, bf16[384,384]{1,0:T(8,128)(2,1)}, u32[]{:S(2)}, u32[]{:S(2)}) collective-permute-start(bf16[384,384]{1,0:T(8,128)(2,1)} %get-tuple-element.276), channel_id=1, source_target_pairs={{0,1},{1,2},{2,3},{3,0},{4,5},{5,6},{6,7},{7,4},{8,9},{9,10},{10,1... | collective-permute-start | bytes 884744 | tf_op jit(solution)/shard_map/ppermute | solution.py:803
  360.5 34.2 %collective-permute-start.32 = (bf16[384,384]{1,0:T(8,128)(2,1)}, bf16[384,384]{1,0:T(8,128)(2,1)}, u32[]{:S(2)}, u32[]{:S(2)}) collective-permute-start(bf16[384,384]{1,0:T(8,128)(2,1)} %get-tuple-element.275), channel_id=1, source_target_pairs={{0,2},{1,3},{2,0},{3,1},{4,6},{5,7},{6,4},{7,5},{8,10},{9,11},{10,... | collective-permute-start | bytes 884744 | tf_op jit(solution)/shard_map/ppermute | solution.py:803
  400.0 207.8 %reduce-scatter.6.cloned.1.call-start = ((), (), s32[]{:S(2)}) async-start(), calls=%async_computation.6 | async-start | bytes 7962624 | tf_op jit(solution)/shard_map/reduce_scatter | solution.py:856
  406.9 34.0 %collective-permute-start.34 = (bf16[384,1536]{1,0:T(8,128)(2,1)S(1)}, bf16[384,1536]{1,0:T(8,128)(2,1)}, u32[]{:S(2)}, u32[]{:S(2)}) collective-permute-start(bf16[384,1536]{1,0:T(8,128)(2,1)S(1)} %copy-done.38), channel_id=1, source_target_pairs={{0,1},{1,2},{2,3},{3,0},{4,5},{5,6},{6,7},{7,4},{8,9},{9,10},{10,1... | collective-permute-start | bytes 3538952 | tf_op jit(solution)/shard_map/ppermute | solution.py:803
  441.0 231.0 %reduce-scatter.8.cloned.1.call-start = ((), (), s32[]{:S(2)}) async-start(), calls=%async_computation.7 | async-start | bytes 7962624 | tf_op jit(solution)/shard_map/reduce_scatter | solution.py:856
  441.0 39.5 %collective-permute-start.39 = (bf16[384,1536]{1,0:T(8,128)(2,1)}, bf16[384,1536]{1,0:T(8,128)(2,1)}, u32[]{:S(2)}, u32[]{:S(2)}) collective-permute-start(bf16[384,1536]{1,0:T(8,128)(2,1)} %get-tuple-element.202.refs_0_), channel_id=1, source_target_pairs={{0,1},{1,2},{2,3},{3,0},{4,5},{5,6},{6,7},{7,4},{8,9},{9,10},{10,1... | collective-permute-start | bytes 3538952 | tf_op jit(solution)/shard_map/ppermute | solution.py:803
  443.7 35.0 %collective-permute-start.41 = (bf16[2,2,2,192,128]{4,3,2,1,0:T(8,128)(2,1)}, bf16[2,2,2,192,128]{4,3,2,1,0:T(8,128)(2,1)}, u32[]{:S(2)}, u32[]{:S(2)}) collective-permute-start(bf16[2,2,2,192,128]{4,3,2,1,0:T(8,128)(2,1)} %add_convert_fusion.13), channel_id=1, source_target_pairs={{0,1},{1,2},{2,3},{3,0},{4,5},{5,6},{6,7},{7,4},{8,9},{9,10},{10,1... | collective-permute-start | bytes 1179656 | tf_op jit(solution)/shard_map/ppermute | solution.py:803
  485.6 31.6 %collective-permute-start.35 = (bf16[1536,768]{0,1:T(8,128)(2,1)}, bf16[1536,768]{0,1:T(8,128)(2,1)}, u32[]{:S(2)}, u32[]{:S(2)}) collective-permute-start(bf16[1536,768]{0,1:T(8,128)(2,1)} %pad_maximum_fusion.2), channel_id=1, source_target_pairs={{0,8},{8,0},{16,24},{24,16},{1,9},{9,1},{17,25},{25,17},{2,10},{10... | collective-permute-start | bytes 7077896 | tf_op jit(solution)/shard_map/ppermute | solution.py:794
  517.2 37.5 %collective-permute-start.44 = (bf16[384,1536]{1,0:T(8,128)(2,1)}, bf16[384,1536]{1,0:T(8,128)(2,1)}, u32[]{:S(2)}, u32[]{:S(2)}) collective-permute-start(bf16[384,1536]{1,0:T(8,128)(2,1)} %collective-permute-done.39.refs_1_), channel_id=1, source_target_pairs={{0,1},{1,2},{2,3},{3,0},{4,5},{5,6},{6,7},{7,4},{8,9},{9,10},{10,1... | collective-permute-start | bytes 3538952 | tf_op jit(solution)/shard_map/ppermute | solution.py:803
  520.8 39.3 %collective-permute-start.40 = (bf16[1536,384]{0,1:T(8,128)(2,1)}, bf16[1536,384]{0,1:T(8,128)(2,1)}, u32[]{:S(2)}, u32[]{:S(2)}) collective-permute-start(bf16[1536,384]{0,1:T(8,128)(2,1)} %constant_dynamic-slice_fusion.14), channel_id=1, source_target_pairs={{0,16},{16,0},{8,24},{24,8},{1,17},{17,1},{9,25},{25,9},{2,18},{18... | collective-permute-start | bytes 3538952 | tf_op jit(solution)/shard_map/ppermute | solution.py:797
  522.2 32.6 %collective-permute-start.46 = (bf16[400,512]{1,0:T(8,128)(2,1)S(1)}, bf16[400,512]{1,0:T(8,128)(2,1)S(1)}, u32[]{:S(2)}, u32[]{:S(2)}) collective-permute-start(bf16[400,512]{1,0:T(8,128)(2,1)S(1)} %fusion.10.refs_4_), channel_id=1, source_target_pairs={{0,1},{1,2},{2,3},{3,0},{4,5},{5,6},{6,7},{7,4},{8,9},{9,10},{10,1... | collective-permute-start | bytes 1228808 | tf_op jit(solution)/shard_map/ppermute | solution.py:803
  554.8 38.2 %collective-permute-start.48 = (bf16[384,1536]{1,0:T(8,128)(2,1)}, bf16[384,1536]{1,0:T(8,128)(2,1)}, u32[]{:S(2)}, u32[]{:S(2)}) collective-permute-start(bf16[384,1536]{1,0:T(8,128)(2,1)} %collective-permute-done.42.refs_1_), channel_id=1, source_target_pairs={{0,1},{1,2},{2,3},{3,0},{4,5},{5,6},{6,7},{7,4},{8,9},{9,10},{10,1... | collective-permute-start | bytes 3538952 | tf_op jit(solution)/shard_map/ppermute | solution.py:803
  569.1 31.7 %collective-permute-start.50 = (bf16[400,512]{1,0:T(8,128)(2,1)S(1)}, bf16[400,512]{1,0:T(8,128)(2,1)S(1)}, u32[]{:S(2)}, u32[]{:S(2)}) collective-permute-start(bf16[400,512]{1,0:T(8,128)(2,1)S(1)} %collective-permute-done.46.refs_5_), channel_id=1, source_target_pairs={{0,1},{1,2},{2,3},{3,0},{4,5},{5,6},{6,7},{7,4},{8,9},{9,10},{10,1... | collective-permute-start | bytes 1228808 | tf_op jit(solution)/shard_map/ppermute | solution.py:803
  602.1 36.0 %collective-permute-start.52 = (bf16[384,1536]{1,0:T(8,128)(2,1)}, bf16[384,1536]{1,0:T(8,128)(2,1)}, u32[]{:S(2)}, u32[]{:S(2)}) collective-permute-start(bf16[384,1536]{1,0:T(8,128)(2,1)} %collective-permute-done.44.refs_2_), channel_id=1, source_target_pairs={{0,1},{1,2},{2,3},{3,0},{4,5},{5,6},{6,7},{7,4},{8,9},{9,10},{10,1... | collective-permute-start | bytes 3538952 | tf_op jit(solution)/shard_map/ppermute | solution.py:803
  607.9 33.0 %collective-permute-start.59 = (bf16[192,2240]{1,0:T(8,128)(2,1)}, bf16[192,2240]{1,0:T(8,128)(2,1)}, u32[]{:S(2)}, u32[]{:S(2)}) collective-permute-start(bf16[192,2240]{1,0:T(8,128)(2,1)} %reduce-scatter.6.cloned.1.call-done), channel_id=1, source_target_pairs={{0,4},{4,0},{1,5},{5,1},{2,6},{6,2},{3,7},{7,3},{8,12},{12,8},{9,1... | collective-permute-start | bytes 2580488 | tf_op jit(solution)/shard_map/ppermute | solution.py:800
  638.2 38.0 %collective-permute-start.57 = (bf16[384,1536]{1,0:T(8,128)(2,1)}, bf16[384,1536]{1,0:T(8,128)(2,1)}, u32[]{:S(2)}, u32[]{:S(2)}) collective-permute-start(bf16[384,1536]{1,0:T(8,128)(2,1)} %collective-permute-done.48.refs_2_), channel_id=1, source_target_pairs={{0,1},{1,2},{2,3},{3,0},{4,5},{5,6},{6,7},{7,4},{8,9},{9,10},{10,1... | collective-permute-start | bytes 3538952 | tf_op jit(solution)/shard_map/ppermute | solution.py:803
  (100 other events, 1707.9 us)
Sparse Core Ops, SparseCore 0:
  31.5 121.1 all-gather.2
  157.3 39.0 all-gather.4
  400.2 72.7 reduce-scatter.3
  477.3 79.7 reduce-scatter.5
  560.5 76.4 reduce-scatter.7

commit v7 on v6

--- a/solution.py
+++ b/solution.py
@@ -1048,18 +1048,18 @@
     input_low, attn_term = finish(meta, after(q_grad, mixed_next), q_full, inputs, hidden_grad, attn_gamma, tps)
     output_pairs = links.pairs(inner_rows(mixed, after(branch_grad, q_grads[-1])).astype(LOW), 1)
     token = (mixed_got, input_low, kv_parts, shares, output_pairs)
-    kv_parts = [
-        mine if got is None else add_low(after(mine, token), got) for mine, got in kv_parts
-    ]
+    kv_parts = [(after(mine, token), got) for mine, got in kv_parts]
+
+    def kv_block(seq, hop):
+        mine, got = (
+            None if item is None
+            else lax.dynamic_slice_in_dim(item, place(seq, links.at(hop)) * own, own, 2)
+            for item in kv_parts[seq]
+        )
+        return mine if got is None else add_low(mine, got)
 
     def kv_rows(hop):
-        return jnp.stack(
-            [
-                lax.dynamic_slice_in_dim(kv_parts[s], place(s, links.at(hop)) * own, own, 2)
-                for s in seqs
-            ],
-            axis=2,
-        )
+        return jnp.stack([kv_block(s, hop) for s in seqs], axis=2)
 
     def fsdp_rows(value, below):
         return jnp.concatenate(
@@ -1073,7 +1073,7 @@
     kv_mine, kv_next = kv_rows(0), kv_rows(1)
     mixed_got = links.hop_tp(after(mixed_next, shares))
     kv_got = links.hop_tp(after(kv_next, (input_low, output_pairs)))
-    down_weight_grad = links.lay_weight(*links.reduce_weight(after(down_term, kv_next)))
+    down_weight_grad = links.lay_weight(*links.reduce_weight(after(down_term, kv_parts[-1])))
     kv_next = add_low(kv_rows(2), kv_got)
     gate_term = inner_rows(two_all, after(gate_all, kv_next)).astype(LOW)
 

time: 711 us -> 711 us (level)
    convert_element_type x17 -> x15, other arithmetic: 25.2 us -> 21.3 us  [add_low(): return (left.astype(jnp.float32) + right.astype(jnp.float32)).astype(LOW)]
    unnamed x144 -> x142, local copies, waits for them, and re-layouts: 15.1 us -> 16 us
where the time goes in v7:
time: 711 us; the launch traced here: 702 us
  waiting for transfers between devices  244 us (34%)
  Pallas kernels  205 us (29%)
  starting transfers between devices  74 us (10%)
  matrix products  64.4 us (9%)
  other arithmetic  60.3 us (8%)
  local copies, waits for them, and re-layouts  39.1 us (5%)
  between operations  15.4 us (2%)
    ppermute x36, waiting for transfers between devices, hop_tp(): lax.ppermute(value, 'tp', [(i, (i + hop) % self.tps) for i in range(self....  193 us
    pallas_call x4, Pallas kernels, feed(): pl.pallas_call(functools.partial(feed_kernel, first, hidden), grid_spec=p...  106 us
    dot_general x6, matrix products, inner_rows(): lax.dot_general(left, right, (((0,), (0,)), ((), ())), preferred_element_...  64.4 us
    ppermute x36, starting transfers between devices, hop_tp(): lax.ppermute(value, 'tp', [(i, (i + hop) % self.tps) for i in range(self....  32.7 us
    ppermute x8, starting transfers between devices, to_y(): return lax.ppermute(value, 'ctx', [(0, 1), (1, 0)])  25.2 us
    ppermute x6, waiting for transfers between devices, to_x(): return lax.ppermute(value, 'fsdp', [(0, 2), (2, 0), (1, 3), (3, 1)])  25.1 us
    ppermute x8, waiting for transfers between devices, to_y(): return lax.ppermute(value, 'ctx', [(0, 1), (1, 0)])  23.1 us
    convert_element_type x15, other arithmetic, add_low(): return (left.astype(jnp.float32) + right.astype(jnp.float32)).astype(LOW)  21.3 us
  transfers between devices with their start and end apart: 69, of which 35 were waited for; matrix products, arithmetic and copies ran while one was open for 21% of the time, Pallas kernels for 29%

profile of v7, /device:TPU:0, one launch (start us, length us, event | category | flops | bytes accessed | tf_op | source)
XLA Modules:
  0.0 702.1 jit_solution(4799385149694979923)
XLA Ops:
  19.3 12.0 %collective-permute-done.1.refs_2_.refs_10_ = bf16[400,896]{1,0:T(8,128)(2,1)} collective-permute-done((bf16[400,896]{1,0:T(8,128)(2,1)S(1)}, bf16[400,896]{1,0:T(8,128)(2,1)}, u32[]{:S(2)}, u32[]{:S(2)}) %collective-permute-start.1) | collective-permute-done | bytes 716832 | tf_op jit(solution)/shard_map/ppermute | solution.py:797
  45.6 8.4 %collective-permute-done.10 = bf16[384,384]{1,0:T(8,128)(2,1)} collective-permute-done((bf16[384,384]{1,0:T(8,128)(2,1)}, bf16[384,384]{1,0:T(8,128)(2,1)}, u32[]{:S(2)}, u32[]{:S(2)}) %collective-permute-start.10) | collective-permute-done | bytes 294944 | tf_op jit(solution)/shard_map/ppermute | solution.py:803
  58.1 13.6 %project.1 = (bf16[1536,1536]{1,0:T(8,128)(2,1)}, bf16[4,384,384]{2,1,0:T(8,128)(2,1)S(1)}, bf16[1536,512]{1,0:T(8,128)(2,1)}) custom-call(s32[6]{0:T(128)S(1)} %stack.106.meta.refs_0_, bf16[2,768,1536]{2,1,0:T(8,128)(2,1)} %refs_12_.1, f32[1,1536]{1,0:T(1,128)S(1)} %maximum_convert_fusion.2.gain_ref.refs_13_, f32[1,896]{1,0:T(1,128)S(1)} %bitcast.96, ...), custom_call_target="tpu_custom_call" | custom-call | flops 4227858432 | bytes 18874368 | tf_op jit(solution)/shard_map/project/pallas_call | solution.py:131
  86.9 10.0 %collective-permute-done.5 = bf16[384,384]{1,0:T(8,128)(2,1)S(1)} collective-permute-done((bf16[384,384]{1,0:T(8,128)(2,1)S(1)}, bf16[384,384]{1,0:T(8,128)(2,1)S(1)}, u32[]{:S(2)}, u32[]{:S(2)}) %collective-permute-start.5) | collective-permute-done | bytes 294944 | tf_op jit(solution)/shard_map/ppermute | solution.py:803
  108.7 10.6 %collective-permute-done.13.refs_2_ = bf16[768,384]{1,0:T(8,128)(2,1)S(1)} collective-permute-done((bf16[768,384]{1,0:T(8,128)(2,1)S(1)}, bf16[768,384]{1,0:T(8,128)(2,1)S(1)}, u32[]{:S(2)}, u32[]{:S(2)}) %collective-permute-start.13) | collective-permute-done | bytes 589856 | tf_op jit(solution)/shard_map/ppermute | solution.py:797
  147.7 8.3 %collective-permute-done.20.far_ref = bf16[1120,384]{1,0:T(8,128)(2,1)} collective-permute-done((bf16[1120,384]{1,0:T(8,128)(2,1)}, bf16[1120,384]{1,0:T(8,128)(2,1)}, u32[]{:S(2)}, u32[]{:S(2)}) %collective-permute-start.20) | collective-permute-done | bytes 860192 | tf_op jit(solution)/shard_map/ppermute | solution.py:800
  165.8 11.7 %collective-permute-done.19.refs_1_ = bf16[384,1536]{1,0:T(8,128)(2,1)} collective-permute-done((bf16[384,1536]{1,0:T(8,128)(2,1)}, bf16[384,1536]{1,0:T(8,128)(2,1)}, u32[]{:S(2)}, u32[]{:S(2)}) %collective-permute-start.19) | collective-permute-done | bytes 1179680 | tf_op jit(solution)/shard_map/ppermute | solution.py:803
  177.5 26.4 %feed.4 = (bf16[1536,2240]{1,0:T(8,128)(2,1)}, bf16[1536,2240]{1,0:T(8,128)(2,1)}, bf16[1536,2240]{1,0:T(8,128)(2,1)}, bf16[1536,1536]{1,0:T(8,128)(2,1)}, bf16[...) custom-call(s32[6]{0:T(128)} %copy-done.21, bf16[384,1536]{1,0:T(8,128)(2,1)} %get-tuple-element.143.refs_1_, ...), custom_call_target="tpu_custom_call" | custom-call | flops 15854469120 | bytes 20643840 | tf_op jit(solution)/shard_map/feed/pallas_call | solution.py:681
  206.3 26.2 %feed.5 = (bf16[1536,2240]{1,0:T(8,128)(2,1)}, bf16[1536,2240]{1,0:T(8,128)(2,1)}, bf16[1536,2240]{1,0:T(8,128)(2,1)}, bf16[1536,1536]{1,0:T(8,128)(2,1)}, bf16[...) custom-call(s32[6]{0:T(128)} %copy-done.21, ...), custom_call_target="tpu_custom_call", output_to_operand_aliasing={{0}: (6, {}), {1}: (7, {}), {2}: (8, {}), {3}: (9, {})} | custom-call | flops 15854469120 | bytes 20643840 | tf_op jit(solution)/shard_map/feed/pallas_call | solution.py:681
  234.0 26.4 %feed.6 = (bf16[1536,2240]{1,0:T(8,128)(2,1)}, bf16[1536,2240]{1,0:T(8,128)(2,1)}, bf16[1536,2240]{1,0:T(8,128)(2,1)}, bf16[1536,1536]{1,0:T(8,128)(2,1)}, bf16[...) custom-call(s32[6]{0:T(128)} %copy-done.21, ...), custom_call_target="tpu_custom_call", output_to_operand_aliasing={{0}: (6, {}), {1}: (7, {}), {2}: (8, {}), {3}: (9, {})} | custom-call | flops 15854469120 | bytes 20643840 | tf_op jit(solution)/shard_map/feed/pallas_call | solution.py:681
  264.4 26.7 %feed.7 = (bf16[1536,2240]{1,0:T(8,128)(2,1)}, bf16[1536,2240]{1,0:T(8,128)(2,1)}, bf16[1536,2240]{1,0:T(8,128)(2,1)}, bf16[1536,1536]{1,0:T(8,128)(2,1)}, bf16[...) custom-call(s32[6]{0:T(128)} %copy-done.21, ...), custom_call_target="tpu_custom_call", output_to_operand_aliasing={{0}: (6, {}), {1}: (7, {}), {2}: (8, {}), {3}: (9, {})} | custom-call | flops 15854469120 | bytes 20643840 | tf_op jit(solution)/shard_map/feed/pallas_call | solution.py:681
  296.0 16.3 %convolution_convert_fusion.2 = bf16[1536,2240]{1,0:T(8,128)(2,1)} fusion(bf16[1536,1536]{1,0:T(8,128)(2,1)S(1)} %bitcast.102, bf16[1536,2240]{1,0:T(8,128)(2,1)} %get-tuple-element.173), kind=kOutput, calls=%fused_computation.2 | convolution fusion | flops 10573086720 | bytes 18481152 | tf_op jit(solution)/shard_map/dot_general | solution.py:35
  312.2 9.2 %collective-permute-done.28.b_ref = bf16[384,1536]{1,0:T(8,128)(2,1)} collective-permute-done((bf16[384,1536]{1,0:T(8,128)(2,1)}, bf16[384,1536]{1,0:T(8,128)(2,1)}, u32[]{:S(2)}, u32[]{:S(2)}) %collective-permute-start.28) | collective-permute-done | bytes 1179680 | tf_op jit(solution)/shard_map/ppermute | solution.py:803
  324.9 10.1 %turn.1 = (f32[384,1536]{1,0:T(8,128)}, bf16[384,1536]{1,0:T(8,128)(2,1)S(1)}, bf16[384,1536]{1,0:T(8,128)(2,1)S(1)}, f32[2,1,1536]{2,1,0:T(1,128)S(1)}) custom-call(s32[6]{0:T(128)S(1)} %copy-done.22, bf16[384,1536]{1,0:T(8,128)(2,1)S(1)} %copy-done.13, bf16[384,1536]{1,0:T(8,128)(2,1)} %collective-permute-done.28.b_ref, ...), custom_call_target="tpu_custom_call" | custom-call | flops 1811939328 | bytes 8388608 | tf_op jit(solution)/shard_map/turn/pallas_call | solution.py:470
  349.9 9.3 %attend_back.3 = (bf16[192,1536]{1,0:T(8,128)(2,1)S(1)}, bf16[2,2,768,128]{3,2,1,0:T(8,128)(2,1)}, bf16[2,2,768,128]{3,2,1,0:T(8,128)(2,1)S(1)}) custom-call(s32[6]{0:T(128)S(1)} %copy-done.22, bf16[4,384,384]{2,1,0:T(8,128)(2,1)S(1)} %copy-done.15, bf16[4,384,384]{2,1,0:T(8,128)(2,1)S(1)} %copy-done.15, bf16[1536,512]{1,0:T(8,128)(2,1)} %copy-done.26, ...), custom_call_target="tpu_custom_call" | custom-call | flops 7247757312 | bytes 4194304 | tf_op jit(solution)/shard_map/attend_back/pallas_call | solution.py:351
  370.5 10.3 %collective-permute-done.30 = bf16[384,1536]{1,0:T(8,128)(2,1)S(1)} collective-permute-done((bf16[384,1536]{1,0:T(8,128)(2,1)S(1)}, bf16[384,1536]{1,0:T(8,128)(2,1)S(1)}, u32[]{:S(2)}, u32[]{:S(2)}) %collective-permute-start.30) | collective-permute-done | bytes 1179680 | tf_op jit(solution)/shard_map/ppermute | solution.py:803
  406.5 9.4 %collective-permute-done.38 = bf16[2,2,2,192,128]{4,3,2,1,0:T(8,128)(2,1)S(1)} collective-permute-done((bf16[2,2,2,192,128]{4,3,2,1,0:T(8,128)(2,1)S(1)}, bf16[2,2,2,192,128]{4,3,2,1,0:T(8,128)(2,1)S(1)}, u32[]{:S(2)}, u32[]{:S(2)}) %collective-permute-start.38) | collective-permute-done | bytes 393248 | tf_op jit(solution)/shard_map/ppermute | solution.py:803
  416.8 17.4 %convolution_convert_fusion.1 = bf16[1536,2240]{1,0:T(8,128)(2,1)} fusion(bf16[1536,1536]{1,0:T(8,128)(2,1)} %get-tuple-element.199, bf16[1536,2240]{1,0:T(8,128)(2,1)} %get-tuple-element.201), kind=kOutput, calls=%fused_computation.1 | convolution fusion | flops 10573086720 | bytes 18481152 | tf_op jit(solution)/shard_map/dot_general | solution.py:35
  444.0 17.1 %convolution_convert_fusion = bf16[1536,2240]{1,0:T(8,128)(2,1)} fusion(bf16[1536,1536]{1,0:T(8,128)(2,1)} %get-tuple-element.199, bf16[1536,2240]{1,0:T(8,128)(2,1)} %get-tuple-element.206), kind=kOutput, calls=%fused_computation | convolution fusion | flops 10573086720 | bytes 18481152 | tf_op jit(solution)/shard_map/dot_general | solution.py:35
  464.0 15.0 %collective-permute-done.41 = bf16[2,2,2,192,128]{4,3,2,1,0:T(8,128)(2,1)} collective-permute-done((bf16[2,2,2,192,128]{4,3,2,1,0:T(8,128)(2,1)}, bf16[2,2,2,192,128]{4,3,2,1,0:T(8,128)(2,1)}, u32[]{:S(2)}, u32[]{:S(2)}) %collective-permute-start.41) | collective-permute-done | bytes 393248 | tf_op jit(solution)/shard_map/ppermute | solution.py:803
  526.3 28.8 %collective-permute-done.46.refs_5_ = bf16[400,512]{1,0:T(8,128)(2,1)S(1)} collective-permute-done((bf16[400,512]{1,0:T(8,128)(2,1)S(1)}, bf16[400,512]{1,0:T(8,128)(2,1)S(1)}, u32[]{:S(2)}, u32[]{:S(2)}) %collective-permute-start.46) | collective-permute-done | bytes 409632 | tf_op jit(solution)/shard_map/ppermute | solution.py:803
  571.2 21.2 %collective-permute-done.45 = bf16[384,384]{0,1:T(8,128)(2,1)S(1)} collective-permute-done((bf16[384,384]{0,1:T(8,128)(2,1)S(1)}, bf16[384,384]{0,1:T(8,128)(2,1)S(1)}, u32[]{:S(2)}, u32[]{:S(2)}) %collective-permute-start.45) | collective-permute-done | bytes 294944 | tf_op jit(solution)/shard_map/ppermute | solution.py:803
  628.2 10.4 %collective-permute-done.52.refs_3_ = bf16[384,1536]{1,0:T(8,128)(2,1)} collective-permute-done((bf16[384,1536]{1,0:T(8,128)(2,1)}, bf16[384,1536]{1,0:T(8,128)(2,1)}, u32[]{:S(2)}, u32[]{:S(2)}) %collective-permute-start.52) | collective-permute-done | bytes 1179680 | tf_op jit(solution)/shard_map/ppermute | solution.py:803
  656.5 13.6 %last.1 = f32[2,768,1536]{2,1,0:T(8,128)} custom-call(s32[6]{0:T(128)S(1)} %copy-done.22, bf16[384,1536]{1,0:T(8,128)(2,1)} %get-tuple-element.202.refs_0_, bf16[384,1536]{1,0:T(8,128)(2,1)} %collective-permute-done.39.refs_1_, bf16[384,1536]{1,0:T(8,128)(2,1)} %collective-permute-done.44.refs_2_, bf16[384,1536]{1,0:T(8,128)(2,1)} %collective-permute-done.52.refs_3_, ...), custom_call_target="tpu_custom_call" | custom-call | flops 2415919104 | bytes 16777216 | tf_op jit(solution)/shard_map/last/pallas_call | solution.py:614
  (407 shorter events, 318.4 us)
Async XLA Ops:
  7.2 170.3 %all-gather.3.cloned.1.call-start = ((), (), s32[]{:S(2)}) async-start(), calls=%async_computation.3 | async-start | bytes 17203200 | tf_op jit(solution)/shard_map/all_gather | solution.py:965
  31.4 352.0 %all-gather.5.cloned.1.call-start = ((), (), s32[]{:S(2)}) async-start(), calls=%async_computation.4 | async-start | bytes 5898240 | tf_op jit(solution)/shard_map/all_gather | solution.py:1017
  54.0 46.5 %collective-permute-start.9 = (bf16[1120,384]{1,0:T(8,128)(2,1)}, bf16[1120,384]{1,0:T(8,128)(2,1)}, u32[]{:S(2)}, u32[]{:S(2)}) collective-permute-start(bf16[1120,384]{1,0:T(8,128)(2,1)} %dynamic-slice_bitcast_fusion), channel_id=1, source_target_pairs={{0,16},{16,0},{8,24},{24,8},{1,17},{17,1},{9,25},{25,9},{2,18},{18... | collective-permute-start | bytes 2580488 | tf_op jit(solution)/shard_map/ppermute | solution.py:797
  75.8 43.5 %collective-permute-start.7 = (bf16[1536,512]{1,0:T(8,128)(2,1)S(1)}, bf16[1536,512]{1,0:T(8,128)(2,1)S(1)}, u32[]{:S(2)}, u32[]{:S(2)}) collective-permute-start(bf16[1536,512]{1,0:T(8,128)(2,1)S(1)} %copy-done.25), channel_id=1, source_target_pairs={{0,4},{1,5},{2,6},{3,7},{8,12},{9,13},{10,14},{11,15},{16,20},{17,... | collective-permute-start | bytes 4718600 | tf_op jit(solution)/shard_map/ppermute | solution.py:946
  86.3 32.9 %collective-permute-start.13 = (bf16[768,384]{1,0:T(8,128)(2,1)S(1)}, bf16[768,384]{1,0:T(8,128)(2,1)S(1)}, u32[]{:S(2)}, u32[]{:S(2)}) collective-permute-start(bf16[768,384]{1,0:T(8,128)(2,1)S(1)} %constant_dynamic-slice_fusion.23), channel_id=1, source_target_pairs={{0,16},{16,0},{8,24},{24,8},{1,17},{17,1},{9,25},{25,9},{2,18},{18... | collective-permute-start | bytes 1769480 | tf_op jit(solution)/shard_map/ppermute | solution.py:797
  100.4 35.9 %collective-permute-start.12 = (bf16[1536,384]{1,0:T(8,128)(2,1)S(1)}, bf16[1536,384]{1,0:T(8,128)(2,1)S(1)}, u32[]{:S(2)}, u32[]{:S(2)}) collective-permute-start(bf16[1536,384]{1,0:T(8,128)(2,1)S(1)} %constant_dynamic-update-slice_fusion.refs_0_), channel_id=1, source_target_pairs={{0,8},{8,0},{16,24},{24,16},{1,9},{9,1},{17,25},{25,17},{2,10},{10... | collective-permute-start | bytes 3538952 | tf_op jit(solution)/shard_map/ppermute | solution.py:794
  157.2 403.4 %reduce-scatter.4.cloned.1.call-start = ((), (), s32[]{:S(2)}) async-start(), calls=%async_computation.5 | async-start | bytes 7962624 | tf_op jit(solution)/shard_map/reduce_scatter | solution.py:856
  343.1 49.8 %collective-permute-start.36 = (bf16[2,2,768,128]{3,2,1,0:T(8,128)(2,1)}, bf16[2,2,768,128]{3,2,1,0:T(8,128)(2,1)}, u32[]{:S(2)}, u32[]{:S(2)}) collective-permute-start(bf16[2,2,768,128]{3,2,1,0:T(8,128)(2,1)} %get-tuple-element.193), channel_id=1, source_target_pairs={{4,0},{5,1},{6,2},{7,3},{12,8},{13,9},{14,10},{15,11},{20,16},{21,... | collective-permute-start | bytes 2359304 | tf_op jit(solution)/shard_map/ppermute | solution.py:1039
  360.5 32.5 %collective-permute-start.31 = (bf16[384,384]{1,0:T(8,128)(2,1)}, bf16[384,384]{1,0:T(8,128)(2,1)}, u32[]{:S(2)}, u32[]{:S(2)}) collective-permute-start(bf16[384,384]{1,0:T(8,128)(2,1)} %get-tuple-element.284), channel_id=1, source_target_pairs={{0,1},{1,2},{2,3},{3,0},{4,5},{5,6},{6,7},{7,4},{8,9},{9,10},{10,1... | collective-permute-start | bytes 884744 | tf_op jit(solution)/shard_map/ppermute | solution.py:803
  360.5 34.2 %collective-permute-start.32 = (bf16[384,384]{1,0:T(8,128)(2,1)}, bf16[384,384]{1,0:T(8,128)(2,1)}, u32[]{:S(2)}, u32[]{:S(2)}) collective-permute-start(bf16[384,384]{1,0:T(8,128)(2,1)} %get-tuple-element.283), channel_id=1, source_target_pairs={{0,2},{1,3},{2,0},{3,1},{4,6},{5,7},{6,4},{7,5},{8,10},{9,11},{10,... | collective-permute-start | bytes 884744 | tf_op jit(solution)/shard_map/ppermute | solution.py:803
  394.8 213.5 %reduce-scatter.6.cloned.1.call-start = ((), (), s32[]{:S(2)}) async-start(), calls=%async_computation.6 | async-start | bytes 7962624 | tf_op jit(solution)/shard_map/reduce_scatter | solution.py:856
  406.4 33.9 %collective-permute-start.34 = (bf16[384,1536]{1,0:T(8,128)(2,1)}, bf16[384,1536]{1,0:T(8,128)(2,1)S(1)}, u32[]{:S(2)}, u32[]{:S(2)}) collective-permute-start(bf16[384,1536]{1,0:T(8,128)(2,1)} %add_convert_fusion.3), channel_id=1, source_target_pairs={{0,1},{1,2},{2,3},{3,0},{4,5},{5,6},{6,7},{7,4},{8,9},{9,10},{10,1... | collective-permute-start | bytes 3538952 | tf_op jit(solution)/shard_map/ppermute | solution.py:803
  441.4 230.4 %reduce-scatter.8.cloned.1.call-start = ((), (), s32[]{:S(2)}) async-start(), calls=%async_computation.7 | async-start | bytes 7962624 | tf_op jit(solution)/shard_map/reduce_scatter | solution.py:856
  441.4 39.5 %collective-permute-start.39 = (bf16[384,1536]{1,0:T(8,128)(2,1)}, bf16[384,1536]{1,0:T(8,128)(2,1)}, u32[]{:S(2)}, u32[]{:S(2)}) collective-permute-start(bf16[384,1536]{1,0:T(8,128)(2,1)} %get-tuple-element.202.refs_0_), channel_id=1, source_target_pairs={{0,1},{1,2},{2,3},{3,0},{4,5},{5,6},{6,7},{7,4},{8,9},{9,10},{10,1... | collective-permute-start | bytes 3538952 | tf_op jit(solution)/shard_map/ppermute | solution.py:803
  443.7 35.2 %collective-permute-start.41 = (bf16[2,2,2,192,128]{4,3,2,1,0:T(8,128)(2,1)}, bf16[2,2,2,192,128]{4,3,2,1,0:T(8,128)(2,1)}, u32[]{:S(2)}, u32[]{:S(2)}) collective-permute-start(bf16[2,2,2,192,128]{4,3,2,1,0:T(8,128)(2,1)} %fusion.10), channel_id=1, source_target_pairs={{0,1},{1,2},{2,3},{3,0},{4,5},{5,6},{6,7},{7,4},{8,9},{9,10},{10,1... | collective-permute-start | bytes 1179656 | tf_op jit(solution)/shard_map/ppermute | solution.py:803
  486.0 31.6 %collective-permute-start.35 = (bf16[1536,768]{0,1:T(8,128)(2,1)}, bf16[1536,768]{0,1:T(8,128)(2,1)}, u32[]{:S(2)}, u32[]{:S(2)}) collective-permute-start(bf16[1536,768]{0,1:T(8,128)(2,1)} %pad_maximum_fusion.2), channel_id=1, source_target_pairs={{0,8},{8,0},{16,24},{24,16},{1,9},{9,1},{17,25},{25,17},{2,10},{10... | collective-permute-start | bytes 7077896 | tf_op jit(solution)/shard_map/ppermute | solution.py:794
  486.0 31.6 %collective-permute-start.42 = (bf16[384,1536]{1,0:T(8,128)(2,1)S(1)}, bf16[384,1536]{1,0:T(8,128)(2,1)}, u32[]{:S(2)}, u32[]{:S(2)}) collective-permute-start(bf16[384,1536]{1,0:T(8,128)(2,1)S(1)} %add_convert_fusion.2.refs_0_), channel_id=1, source_target_pairs={{0,1},{1,2},{2,3},{3,0},{4,5},{5,6},{6,7},{7,4},{8,9},{9,10},{10,1... | collective-permute-start | bytes 3538952 | tf_op jit(solution)/shard_map/ppermute | solution.py:803
  517.6 37.5 %collective-permute-start.44 = (bf16[384,1536]{1,0:T(8,128)(2,1)}, bf16[384,1536]{1,0:T(8,128)(2,1)}, u32[]{:S(2)}, u32[]{:S(2)}) collective-permute-start(bf16[384,1536]{1,0:T(8,128)(2,1)} %collective-permute-done.39.refs_1_), channel_id=1, source_target_pairs={{0,1},{1,2},{2,3},{3,0},{4,5},{5,6},{6,7},{7,4},{8,9},{9,10},{10,1... | collective-permute-start | bytes 3538952 | tf_op jit(solution)/shard_map/ppermute | solution.py:803
  521.1 36.5 %collective-permute-start.40 = (bf16[1536,384]{0,1:T(8,128)(2,1)}, bf16[1536,384]{0,1:T(8,128)(2,1)}, u32[]{:S(2)}, u32[]{:S(2)}) collective-permute-start(bf16[1536,384]{0,1:T(8,128)(2,1)} %constant_dynamic-slice_fusion.12), channel_id=1, source_target_pairs={{0,16},{16,0},{8,24},{24,8},{1,17},{17,1},{9,25},{25,9},{2,18},{18... | collective-permute-start | bytes 3538952 | tf_op jit(solution)/shard_map/ppermute | solution.py:797
  522.5 32.7 %collective-permute-start.46 = (bf16[400,512]{1,0:T(8,128)(2,1)S(1)}, bf16[400,512]{1,0:T(8,128)(2,1)S(1)}, u32[]{:S(2)}, u32[]{:S(2)}) collective-permute-start(bf16[400,512]{1,0:T(8,128)(2,1)S(1)} %fusion.12.refs_4_), channel_id=1, source_target_pairs={{0,1},{1,2},{2,3},{3,0},{4,5},{5,6},{6,7},{7,4},{8,9},{9,10},{10,1... | collective-permute-start | bytes 1228808 | tf_op jit(solution)/shard_map/ppermute | solution.py:803
  555.1 38.2 %collective-permute-start.48 = (bf16[384,1536]{1,0:T(8,128)(2,1)}, bf16[384,1536]{1,0:T(8,128)(2,1)}, u32[]{:S(2)}, u32[]{:S(2)}) collective-permute-start(bf16[384,1536]{1,0:T(8,128)(2,1)} %collective-permute-done.42.refs_1_), channel_id=1, source_target_pairs={{0,1},{1,2},{2,3},{3,0},{4,5},{5,6},{6,7},{7,4},{8,9},{9,10},{10,1... | collective-permute-start | bytes 3538952 | tf_op jit(solution)/shard_map/ppermute | solution.py:803
  560.6 32.7 %collective-permute-start.55 = (bf16[192,2240]{1,0:T(8,128)(2,1)}, bf16[192,2240]{1,0:T(8,128)(2,1)S(1)}, u32[]{:S(2)}, u32[]{:S(2)}) collective-permute-start(bf16[192,2240]{1,0:T(8,128)(2,1)} %reduce-scatter.4.cloned.1.call-done), channel_id=1, source_target_pairs={{0,4},{4,0},{1,5},{5,1},{2,6},{6,2},{3,7},{7,3},{8,12},{12,8},{9,1... | collective-permute-start | bytes 2580488 | tf_op jit(solution)/shard_map/ppermute | solution.py:800
  602.5 36.0 %collective-permute-start.52 = (bf16[384,1536]{1,0:T(8,128)(2,1)}, bf16[384,1536]{1,0:T(8,128)(2,1)}, u32[]{:S(2)}, u32[]{:S(2)}) collective-permute-start(bf16[384,1536]{1,0:T(8,128)(2,1)} %collective-permute-done.44.refs_2_), channel_id=1, source_target_pairs={{0,1},{1,2},{2,3},{3,0},{4,5},{5,6},{6,7},{7,4},{8,9},{9,10},{10,1... | collective-permute-start | bytes 3538952 | tf_op jit(solution)/shard_map/ppermute | solution.py:803
  638.5 37.4 %collective-permute-start.57 = (bf16[384,1536]{1,0:T(8,128)(2,1)}, bf16[384,1536]{1,0:T(8,128)(2,1)}, u32[]{:S(2)}, u32[]{:S(2)}) collective-permute-start(bf16[384,1536]{1,0:T(8,128)(2,1)} %collective-permute-done.48.refs_2_), channel_id=1, source_target_pairs={{0,1},{1,2},{2,3},{3,0},{4,5},{5,6},{6,7},{7,4},{8,9},{9,10},{10,1... | collective-permute-start | bytes 3538952 | tf_op jit(solution)/shard_map/ppermute | solution.py:803
  (99 other events, 1699.4 us)
Sparse Core Ops, SparseCore 0:
  31.5 121.1 all-gather.2
  157.3 39.0 all-gather.4
  394.9 72.8 reduce-scatter.3
  472.1 76.8 reduce-scatter.5
  552.3 81.6 reduce-scatter.7
